TPU v7x, 32 devices: a whole 2x2x4 slice. The times are simulated.
32 devices in a mesh: conf: 2 (over x), tgt: 8 (over z, y), src: 2 (over core).
Axes of the slice: x: 2, y: 2, z: 4, core: 2. Of those that a mesh axis runs over, the one named last changes fastest.
Arguments:
- right_side: float32 [128, 8192], P('conf', ('tgt', 'src')), parts along dimension 0, may hold values from -6 to 6
- atom_centers: float32 [6, 40000], P('conf'), parts along dimension 0, may hold values from -4 to 4
- tessera_owner: int32 [8192], replicated, may hold values from 0 to 39999
- tessera_angles: float32 [2, 8192], replicated, may hold values from -3.140625 to 3.140625
- self_term: float32 [8192], P(('tgt', 'src')), may hold values from 0.5 to 2
Outputs:
- surface_charge: float32 [128, 8192], P('conf', ('tgt', 'src')), parts along dimension 0
- residual: float32 [128, 8192], P('conf', ('tgt', 'src')), parts along dimension 0
There are 2 independent parts, one for each index of `conf`. A program takes and returns all parts, laid end to end along the dimension named above; an argument that names none is the same for every part. Nothing has to cross between parts.
All inputs are finite; a program needn't handle non-finite values.
Results may differ from a plain program's by a relative error of at most 0.006.
The roundings to bfloat16 on the way count: a program that leaves them out, or rounds other values in their place, can miss the bound.
Values may be sent and summed in bfloat16 or wider, within the bound.
No kernel may reach another device: no remote copies, remote signals or barrier semaphores. Data moves between devices by JAX's collectives and lax.ppermute only.
A program may use at most 128 MiB of HBM per device.

v0:
```python
import jax
import jax.numpy as jnp
from jax import lax
from jax.sharding import PartitionSpec as P

ITERS = 2


soft_square = 0.09
probe_radius = 0.15


def positions(atom_centers, tessera_owner, tessera_angles):
    base = jnp.take(atom_centers, tessera_owner, axis=1)
    azimuth = tessera_angles[0]
    polar = tessera_angles[1]
    sine = jnp.sin(polar)
    offsets = jnp.stack([jnp.cos(azimuth) * sine, jnp.sin(azimuth) * sine, jnp.cos(polar)])
    return base + probe_radius * offsets


def tile_apply(total, source_pos, charges, target_pos):
    diff = source_pos[0][:, None] - target_pos[0][None, :]
    dist_sq = diff * diff
    diff = source_pos[1][:, None] - target_pos[1][None, :]
    dist_sq = dist_sq + diff * diff
    diff = source_pos[2][:, None] - target_pos[2][None, :]
    dist_sq = dist_sq + diff * diff
    kern = lax.rsqrt(dist_sq + soft_square).astype(jnp.bfloat16)
    return total + jnp.dot(charges, kern, preferred_element_type=jnp.float32)


def products(left, right):
    return lax.dot_general(
        left,
        right,
        (((1,), (1,)), ((), ())),
        precision=lax.Precision.HIGHEST,
        preferred_element_type=jnp.float32,
    )


def chol_solve(matrix, rhs):
    lower = jnp.linalg.cholesky(matrix)
    middle = lax.linalg.triangular_solve(lower, rhs, left_side=True, lower=True)
    return lax.linalg.triangular_solve(lower, middle, left_side=True, lower=True, transpose_a=True)


def per_device(right_side, atom_centers, tessera_owner, tessera_angles, self_term):
    shard = right_side.shape[1]
    columns = right_side.shape[0]
    n_src = lax.axis_size("src")
    tgt_index = lax.axis_index("tgt")
    src_index = lax.axis_index("src")
    allpos = positions(atom_centers, tessera_owner, tessera_angles)

    def residual_norm(residual):
        return lax.psum(products(residual, residual), ("tgt", "src"))

    solution = jnp.zeros_like(right_side)
    residual = right_side
    direction = right_side
    norm_now = residual_norm(residual)
    for step in range(ITERS):
        charges = direction.astype(jnp.bfloat16)
        width = shard * n_src
        target_pos = lax.dynamic_slice_in_dim(allpos, tgt_index * width, width, 1)
        empty = jnp.zeros((columns, width), jnp.float32)
        piece = lax.all_gather(charges, "tgt", axis=1, tiled=True)
        sub = min(piece.shape[1], shard)
        count = piece.shape[1] // sub

        def one_block(j, acc):
            column = j * sub
            row_first = column // shard * width + src_index * shard + column % shard
            source_pos = lax.dynamic_slice_in_dim(allpos, row_first, sub, 1)
            part = lax.dynamic_slice_in_dim(piece, j * sub, sub, 1)
            return tile_apply(acc, source_pos, part, target_pos)

        partial_value = lax.fori_loop(0, count, one_block, empty)
        near = lax.psum_scatter(partial_value, "src", scatter_dimension=1, tiled=True)
        image = near + self_term[None, :] * direction
        gram = lax.psum(products(direction, image), ("tgt", "src"))
        alpha = chol_solve(gram, norm_now)
        solution = solution + jnp.dot(alpha.T, direction, precision=lax.Precision.HIGHEST)
        residual = residual - jnp.dot(alpha.T, image, precision=lax.Precision.HIGHEST)
        if step + 1 < ITERS:
            norm_next = residual_norm(residual)
            beta = chol_solve(norm_now, norm_next)
            direction = residual + jnp.dot(beta.T, direction, precision=lax.Precision.HIGHEST)
            norm_now = norm_next
    return (solution, residual)


def solution(mesh):
    return jax.shard_map(
        per_device,
        mesh=mesh,
        in_specs=(P("conf", ("tgt", "src")), P("conf", None), P(), P(), P(("tgt", "src"))),
        out_specs=(P("conf", ("tgt", "src")), P("conf", ("tgt", "src"))),
        check_vma=False,
    )
```

profile of v0, /device:TPU:0, one launch (start us, length us, event | category | flops | bytes accessed | tf_op | source)
XLA Modules:
  0.0 391.9 jit_solution(6626522547750146130)
XLA Ops:
  7.2 0.8 fusion.42
  8.0 0.8 compare_and_fusion
  8.8 2.7 cosine_multiply_fusion
  11.5 10.8 %copy.31 = f32[3,40000]{0,1:T(8,128)} copy(f32[3,40000]{1,0:T(4,128)} %param.15) | data formatting | bytes 960000 | tf_op args[1]
  22.3 34.5 %gather_fusion = f32[8192,3]{1,0:T(8,128)} fusion(f32[3,40000]{0,1:T(8,128)} %copy.31, s32[8192]{0:T(1024)S(1)} %fusion.42), kind=kCustom, calls=%fused_computation | custom fusion | bytes 229376 | tf_op jit(solution)/shard_map/jit(_take)/gather | solution.py:14
  56.9 2.9 copy.32
  59.8 33.0 %all_gather.6 = bf16[64,4096]{1,0:T(8,128)(2,1)S(1)} all-gather(bf16[64,512]{1,0:T(8,128)(2,1)S(1)} %convert_element_type.26), channel_id=1, replica_groups=mesh['conf'=2,'tgt'=8,'src'=2] {'tgt'}, dimensions={1}, use_global_device_ids=true | all-gather | bytes 589824 | tf_op jit(solution)/shard_map/all_gather | solution.py:69
  92.8 0.1 fusion.18
  93.0 9.5 %while.32 = (s32[]{:T(128)}, f32[64,1024]{1,0:T(8,128)S(1)}, bf16[64,4096]{1,0:T(8,128)(2,1)S(1)}, s32[]{:T(128)}, f32[3,8192]{1,0:T(4,128)S(1)}, /*index=5*/f32...) while((s32[]{:T(128)}, f32[64,1024]{1,0:T(8,128)S(1)}, ...), condition=%wide.region_1.2_spmd.clone, body=%wide.region_0.1_spmd.clone.sunk | while | flops 72482848 | bytes 645621 | solution.py:80
  93.1 1.0 convolution_add_fusion.6
  94.2 0.1 constant_dynamic-slice_fusion.5
  94.3 1.0 convolution_add_fusion.6
  95.5 1.0 convolution_add_fusion.6
  96.7 1.0 convolution_add_fusion.6
  97.8 0.1 constant_dynamic-slice_fusion.5
  97.9 1.0 convolution_add_fusion.6
  99.0 1.0 convolution_add_fusion.6
  100.1 0.1 constant_dynamic-slice_fusion.5
  100.2 1.0 convolution_add_fusion.6
  101.4 1.0 convolution_add_fusion.6
  102.5 0.7 copy-done.2
  103.2 0.3 fusion.46
  103.5 8.6 %reduce-scatter.3.cloned.1.call-done = f32[64,512]{1,0:T(8,128)} async-done(((f32[64,1024]{1,0:T(8,128)}), f32[64,512]{1,0:T(8,128)}) %reduce-scatter.3.cloned.1.call-update) | async-done | bytes 131088 | tf_op jit(solution)/shard_map/reduce_scatter | solution.py:81
  112.1 1.2 convolution_bitcast_fusion
  113.3 62.0 %all-reduce = (f32[64,64]{0,1:T(8,128)S(1)}, f32[64,64]{0,1:T(8,128)S(1)}) all-reduce(f32[64,64]{0,1:T(8,128)S(1)} %fusion.46, f32[64,64]{0,1:T(8,128)S(1)} %convolution_bitcast_fusion), channel_id=1, replica_groups=mesh['conf'=2,'tgt'=8,'src'=2] {'tgt','src'}, use_global_device_ids=true, to_apply=%region_6.8 | all-reduce | flops 8192 | bytes 65536 | tf_op jit(solution)/shard_map/psum | solution.py:58
  175.5 5.8 %cholesky.70 = f32[64,64]{1,0:T(8,128)S(1)} custom-call(f32[64,64]{1,0:T(8,128)S(1)} %get-tuple-element.434), custom_call_target="Cholesky" | custom-call | tf_op jit(solution)/shard_map/jit(cholesky)/cholesky | solution.py:44
  181.4 0.6 compare_reduce_fusion.1
  182.0 0.7 fusion.25
  182.7 4.9 %custom-call.17 = f32[1,64,64]{1,2,0:T(8,128)S(1)} custom-call(f32[1,64,64]{2,1,0:T(8,128)S(1)} %fusion.25), custom_call_target="InvertDiagBlocksLowerTriangular" | custom-call | tf_op jit(solution)/shard_map/triangular_solve/custom-call.2 | solution.py:46
  187.6 5.9 %cholesky.59 = f32[64,64]{1,0:T(8,128)S(1)} custom-call(f32[64,64]{1,0:T(8,128)S(1)} %get-tuple-element.435), custom_call_target="Cholesky" | custom-call | tf_op jit(solution)/shard_map/jit(cholesky)/cholesky | solution.py:44
  193.5 0.6 compare_reduce_fusion.2
  194.1 0.7 fusion.24
  194.8 4.9 %custom-call.15 = f32[1,64,64]{1,2,0:T(8,128)S(1)} custom-call(f32[1,64,64]{2,1,0:T(8,128)S(1)} %fusion.24), custom_call_target="InvertDiagBlocksLowerTriangular" | custom-call | tf_op jit(solution)/shard_map/triangular_solve/custom-call.2 | solution.py:46
  199.7 0.2 fusion.37
  199.9 0.2 fusion.39
  200.1 1.2 convolution_subtract_fusion.1
  201.3 0.3 fusion.48
  201.6 57.6 %psum.30 = f32[64,64]{1,0:T(8,128)S(1)} all-reduce(f32[64,64]{1,0:T(8,128)S(1)} %fusion.48), channel_id=1, replica_groups=mesh['conf'=2,'tgt'=8,'src'=2] {'tgt','src'}, use_global_device_ids=true, to_apply=%region_7.11 | all-reduce | flops 4096 | bytes 32768 | tf_op jit(solution)/shard_map/psum | solution.py:58
  259.2 0.2 fusion.32
  259.5 0.2 fusion.34
  259.6 0.3 fusion.45
  260.0 31.3 %all_gather.7 = bf16[64,4096]{1,0:T(8,128)(2,1)S(1)} all-gather(bf16[64,512]{1,0:T(8,128)(2,1)S(1)} %get-tuple-element.432), channel_id=1, replica_groups=mesh['conf'=2,'tgt'=8,'src'=2] {'tgt'}, dimensions={1}, use_global_device_ids=true | all-gather | bytes 589824 | tf_op jit(solution)/shard_map/all_gather | solution.py:69
  291.3 9.4 %while.33 = (s32[]{:T(128)}, f32[64,1024]{1,0:T(8,128)S(1)}, bf16[64,4096]{1,0:T(8,128)(2,1)S(1)}, s32[]{:T(128)}, f32[3,8192]{1,0:T(4,128)S(1)}, /*index=5*/f32...) while((s32[]{:T(128)}, f32[64,1024]{1,0:T(8,128)S(1)}, ...), condition=%wide.region_9.13_spmd.clone, body=%wide.region_8.12_spmd.clone.sunk | while | flops 72482848 | bytes 645621 | solution.py:80
  291.4 1.0 convolution_add_fusion.7
  292.6 1.0 convolution_add_fusion.7
  293.8 1.0 convolution_add_fusion.7
  294.9 1.0 convolution_add_fusion.7
  296.1 1.0 convolution_add_fusion.7
  297.3 1.0 convolution_add_fusion.7
  298.5 1.0 convolution_add_fusion.7
  299.7 1.0 convolution_add_fusion.7
  300.7 0.7 copy-done.1
  301.4 0.3 fusion.47
  301.8 4.7 %reduce-scatter.5.cloned.1.call-done = f32[64,512]{1,0:T(8,128)} async-done(((f32[64,1024]{1,0:T(8,128)}), f32[64,512]{1,0:T(8,128)}) %reduce-scatter.5.cloned.1.call-update) | async-done | bytes 131088 | tf_op jit(solution)/shard_map/reduce_scatter | solution.py:81
  306.5 1.2 fusion.19
  307.7 61.9 %psum.31 = f32[64,64]{0,1:T(8,128)S(1)} all-reduce(f32[64,64]{0,1:T(8,128)S(1)} %fusion.19), channel_id=1, replica_groups=mesh['conf'=2,'tgt'=8,'src'=2] {'tgt','src'}, use_global_device_ids=true, to_apply=%region_11.15 | all-reduce | flops 4096 | bytes 32768 | tf_op jit(solution)/shard_map/psum | solution.py:83
  369.7 5.8 %cholesky.81 = f32[64,64]{1,0:T(8,128)S(1)} custom-call(f32[64,64]{1,0:T(8,128)S(1)} %fusion.31), custom_call_target="Cholesky" | custom-call | tf_op jit(solution)/shard_map/jit(cholesky)/cholesky | solution.py:44
  375.5 0.6 compare_reduce_fusion
  376.2 0.7 fusion.26
  376.8 4.9 %custom-call.19 = f32[1,64,64]{1,2,0:T(8,128)S(1)} custom-call(f32[1,64,64]{2,1,0:T(8,128)S(1)} %fusion.26), custom_call_target="InvertDiagBlocksLowerTriangular" | custom-call | tf_op jit(solution)/shard_map/triangular_solve/custom-call.2 | solution.py:46
  381.7 0.3 fusion.27
  382.0 0.2 fusion.29
  382.2 1.0 convolution_add_fusion.2
  383.2 1.9 convolution_subtract_fusion
  (51 shorter events, 1.8 us)
Async XLA Ops:
  7.2 104.9 %reduce-scatter.3.cloned.1.call-start = ((), (), s32[]{:S(2)}) async-start(), calls=%async_computation.2 | async-start | bytes 393216 | tf_op jit(solution)/shard_map/reduce_scatter | solution.py:81
  56.9 2.9 copy-start
  92.9 19.2 %copy-start.3 = (f32[512]{0:T(512)S(1)}, f32[512]{0:T(512)}, u32[]{:S(2)}) copy-start(f32[512]{0:T(512)} %param.18) | copy-start | bytes 6148
  102.5 0.7 copy-start.2
  103.2 203.3 %reduce-scatter.5.cloned.1.call-start = ((), (), s32[]{:S(2)}) async-start(), calls=%async_computation.3 | async-start | bytes 393216 | tf_op jit(solution)/shard_map/reduce_scatter | solution.py:81
  300.7 0.7 copy-start.1
Sparse Core Ops, SparseCore 0:
  103.3 8.7 reduce-scatter.2
  301.6 4.8 reduce-scatter.4
where the time goes:
time: 393 us; the launch traced here: 392 us
  blocking collectives  246 us (63%)
  local copies, waits for them, and re-layouts  51.4 us (13%)
  other arithmetic  40.7 us (10%)
  matrix products  25 us (6%)
  between operations  14.3 us (4%)
  waiting for transfers between devices  13.4 us (3%)
    psum x2, blocking collectives, residual_norm(): return lax.psum(products(residual, residual), ('tgt', 'src'))  120 us
    all_gather x2, blocking collectives, per_device(): piece = lax.all_gather(charges, 'tgt', axis=1, tiled=True)  64.3 us
    psum x1, blocking collectives, per_device(): gram = lax.psum(products(direction, image), ('tgt', 'src'))  61.9 us
    gather x2, local copies, waits for them, and re-layouts, positions(): base = jnp.take(atom_centers, tessera_owner, axis=1)  37.4 us
    another operation x9, other arithmetic, chol_solve(): lower = jnp.linalg.cholesky(matrix)  19.6 us
    another operation x6, other arithmetic, chol_solve(): lax.linalg.triangular_solve(lower, middle, left_side=True, lower=True, tr...  16.6 us
    dot_general x16, matrix products, tile_apply(): return total + jnp.dot(charges, kern, preferred_element_type=jnp.float32)  16.2 us
    reduce_scatter x2, waiting for transfers between devices, per_device(): lax.psum_scatter(partial_value, 'src', scatter_dimension=1, tiled=True)  13.3 us
  transfers between devices with their start and end apart: 2, of which 2 were waited for; matrix products, arithmetic and copies ran while one was open for 0% of the time, Pallas kernels for 0%

commit v1 on v0

--- a/solution.py
+++ b/solution.py
@@ -1,22 +1,37 @@
+import functools
+
 import jax
 import jax.numpy as jnp
 from jax import lax
+from jax.experimental import pallas as pl
+from jax.experimental.pallas import tpu as pltpu
 from jax.sharding import PartitionSpec as P
 
 ITERS = 2
-
+GROUP = 4
+LOW = 256
+STORED_LIMIT = 32 * 2**20
 
 soft_square = 0.09
 probe_radius = 0.15
+HIGHEST = lax.Precision.HIGHEST
+MIB = 2**20
+
+
+def params(mib, **kw):
+    return pltpu.CompilerParams(vmem_limit_bytes=mib * MIB, **kw)
 
 
 def positions(atom_centers, tessera_owner, tessera_angles):
     base = jnp.take(atom_centers, tessera_owner, axis=1)
+    return base + probe_radius * unit_offsets(tessera_angles)
+
+
+def unit_offsets(tessera_angles):
     azimuth = tessera_angles[0]
     polar = tessera_angles[1]
     sine = jnp.sin(polar)
-    offsets = jnp.stack([jnp.cos(azimuth) * sine, jnp.sin(azimuth) * sine, jnp.cos(polar)])
-    return base + probe_radius * offsets
+    return jnp.stack([jnp.cos(azimuth) * sine, jnp.sin(azimuth) * sine, jnp.cos(polar)])
 
 
 def tile_apply(total, source_pos, charges, target_pos):
@@ -35,7 +50,7 @@
         left,
         right,
         (((1,), (1,)), ((), ())),
-        precision=lax.Precision.HIGHEST,
+        precision=HIGHEST,
         preferred_element_type=jnp.float32,
     )
 
@@ -46,7 +61,7 @@
     return lax.linalg.triangular_solve(lower, middle, left_side=True, lower=True, transpose_a=True)
 
 
-def per_device(right_side, atom_centers, tessera_owner, tessera_angles, self_term):
+def per_device_general(right_side, atom_centers, tessera_owner, tessera_angles, self_term):
     shard = right_side.shape[1]
     columns = right_side.shape[0]
     n_src = lax.axis_size("src")
@@ -82,21 +97,346 @@
         image = near + self_term[None, :] * direction
         gram = lax.psum(products(direction, image), ("tgt", "src"))
         alpha = chol_solve(gram, norm_now)
-        solution = solution + jnp.dot(alpha.T, direction, precision=lax.Precision.HIGHEST)
-        residual = residual - jnp.dot(alpha.T, image, precision=lax.Precision.HIGHEST)
+        solution = solution + jnp.dot(alpha.T, direction, precision=HIGHEST)
+        residual = residual - jnp.dot(alpha.T, image, precision=HIGHEST)
         if step + 1 < ITERS:
             norm_next = residual_norm(residual)
             beta = chol_solve(norm_now, norm_next)
-            direction = residual + jnp.dot(beta.T, direction, precision=lax.Precision.HIGHEST)
+            direction = residual + jnp.dot(beta.T, direction, precision=HIGHEST)
             norm_now = norm_next
     return (solution, residual)
 
 
+def three_parts(value):
+    first = value.astype(jnp.bfloat16)
+    rest = value - first.astype(jnp.float32)
+    second = rest.astype(jnp.bfloat16)
+    third = (rest - second.astype(jnp.float32)).astype(jnp.bfloat16)
+    return first, second, third
+
+
+def position_kernel(starts, table_ref, owner_ref, offset_ref, out_ref, parts_ref, *, chunk, count, rows):
+    for part, value in enumerate(three_parts(table_ref[...])):
+        parts_ref[part * 3 * rows : (part + 1) * 3 * rows, :] = value
+
+    def one(j, carry):
+        first = pl.multiple_of(starts[j], chunk)
+        at = pl.multiple_of(j * chunk, chunk)
+        owner = owner_ref[:, pl.ds(first, chunk)]
+        low = lax.broadcasted_iota(jnp.int32, (LOW, chunk), 0) == (owner & (LOW - 1))
+        rows_of = jnp.dot(parts_ref[...], low.astype(jnp.bfloat16), preferred_element_type=jnp.float32)
+        high = lax.broadcasted_iota(jnp.int32, (rows, chunk), 0) == (owner // LOW)
+        for axis in range(3):
+            value = rows_of[axis * rows : (axis + 1) * rows]
+            for part in range(1, 3):
+                place = (part * 3 + axis) * rows
+                value = value + rows_of[place : place + rows]
+            base = jnp.sum(jnp.where(high, value, 0.0), axis=0, keepdims=True)
+            out_ref[axis : axis + 1, pl.ds(at, chunk)] = base + probe_radius * offset_ref[axis : axis + 1, pl.ds(first, chunk)]
+        return carry
+
+    lax.fori_loop(0, count, one, 0)
+
+
+def chosen_positions(table, owner, offsets, starts, chunk):
+    count = starts.shape[0]
+    rows = table.shape[0] // 3
+    whole = pl.BlockSpec(memory_space=pltpu.VMEM)
+    return pl.pallas_call(
+        functools.partial(position_kernel, chunk=chunk, count=count, rows=rows),
+        out_shape=jax.ShapeDtypeStruct((3, count * chunk), jnp.float32),
+        in_specs=[pl.BlockSpec(memory_space=pltpu.SMEM), whole, whole, whole],
+        out_specs=whole,
+        scratch_shapes=[pltpu.VMEM((9 * rows, LOW), jnp.bfloat16)],
+        compiler_params=params(24),
+        cost_estimate=pl.CostEstimate(flops=2 * 9 * rows * LOW * count * chunk, bytes_accessed=4 * 40000 * 3, transcendentals=0),
+        name="positions",
+    )(starts, table, owner, offsets)
+
+
+def entry_kernel(source_ref, target_ref, out_ref):
+    dist_sq = None
+    for axis in range(3):
+        diff = source_ref[:, axis : axis + 1] - target_ref[axis : axis + 1, :]
+        dist_sq = diff * diff if dist_sq is None else dist_sq + diff * diff
+    out_ref[...] = lax.rsqrt(dist_sq + soft_square).astype(jnp.bfloat16)
+
+
+def entries(source_pos, target_pos):
+    n, m = source_pos.shape[0], target_pos.shape[1]
+    step = 256
+    return pl.pallas_call(
+        entry_kernel,
+        grid=(n // step,),
+        out_shape=jax.ShapeDtypeStruct((n, m), jnp.bfloat16),
+        in_specs=[pl.BlockSpec((step, 3), lambda i: (i, 0)), pl.BlockSpec((3, m), lambda i: (0, 0))],
+        out_specs=pl.BlockSpec((step, m), lambda i: (i, 0)),
+        compiler_params=params(16),
+        cost_estimate=pl.CostEstimate(flops=12 * n * m, bytes_accessed=2 * n * m, transcendentals=n * m),
+        name="entries",
+    )(source_pos, target_pos)
+
+
+def apply_kernel(*refs, pieces, per):
+    charge_refs, kern_ref, out_ref = refs[:pieces], refs[pieces], refs[pieces + 1]
+    j = pl.program_id(0)
+
+    @pl.when(j == 0)
+    def _():
+        out_ref[...] = jnp.zeros_like(out_ref)
+
+    for piece in range(pieces):
+        for part in range(per):
+
+            @pl.when(j == piece * per + part)
+            def _(piece=piece, part=part):
+                step = kern_ref.shape[0]
+                charges = charge_refs[piece][:, part * step : (part + 1) * step]
+                out_ref[...] += jnp.dot(charges, kern_ref[...], preferred_element_type=jnp.float32)
+
+
+def apply_entries(charges, kern):
+    pieces = len(charges)
+    k, n = charges[0].shape
+    m = kern.shape[1]
+    step = 512
+    per = n // step
+    return pl.pallas_call(
+        functools.partial(apply_kernel, pieces=pieces, per=per),
+        grid=(pieces * per,),
+        out_shape=jax.ShapeDtypeStruct((k, m), jnp.float32),
+        in_specs=[pl.BlockSpec((k, n), lambda j: (0, 0))] * pieces + [pl.BlockSpec((step, m), lambda j: (j, 0))],
+        out_specs=pl.BlockSpec((k, m), lambda j: (0, 0)),
+        compiler_params=params(24),
+        cost_estimate=pl.CostEstimate(flops=2 * k * n * pieces * m, bytes_accessed=2 * pieces * n * m, transcendentals=0),
+        name="apply",
+    )(*charges, kern)
+
+
+def dots(left, right):
+    return lax.dot_general(left, right, (((1,), (1,)), ((), ())), precision=HIGHEST, preferred_element_type=jnp.float32)
+
+
+def left_t(left, right):
+    return lax.dot_general(left, right, (((0,), (0,)), ((), ())), precision=HIGHEST, preferred_element_type=jnp.float32)
+
+
+def mul(left, right):
+    return jnp.dot(left, right, precision=HIGHEST, preferred_element_type=jnp.float32)
+
+
+def eliminate(systems):
+    k = systems[0].shape[0]
+    row_of = lax.broadcasted_iota(jnp.int32, systems[0].shape, 0)
+    systems = list(systems)
+    for i in range(k):
+        for s, system in enumerate(systems):
+            row = system[i : i + 1, :] / system[i : i + 1, i : i + 1]
+            systems[s] = jnp.where(row_of == i, row, system - system[:, i : i + 1] * row)
+    return [system[:, k:] for system in systems]
+
+
+def fold(square):
+    half = square.shape[0] // 2
+    return jnp.concatenate([square[:half], square[half:]], axis=1)
+
+
+def unfold(folded):
+    k = folded.shape[1] // 2
+    return jnp.concatenate([folded[:, :k], folded[:, k:]], axis=0)
+
+
+def first_gram_kernel(own_ref, other_ref, self_ref, direction_ref, image_ref, gram_ref):
+    direction = direction_ref[...]
+    image = own_ref[...] + other_ref[...] + self_ref[...] * direction
+    image_ref[...] = image
+    k = direction.shape[0]
+    both = dots(jnp.concatenate([direction, image], axis=0), image)
+    gram_ref[:k, :] = jnp.concatenate([both[:k], both[k:]], axis=1)
+    gram_ref[k:, :] = fold(dots(direction, direction))
+
+
+def first_gram(partial, other, self_row, direction):
+    k, n = direction.shape
+    mine = pl.BlockSpec((k, n), lambda i: (0, 0))
+    whole = pl.BlockSpec(memory_space=pltpu.VMEM)
+    return pl.pallas_call(
+        first_gram_kernel,
+        grid=(1,),
+        out_shape=[jax.ShapeDtypeStruct((k, n), jnp.float32), jax.ShapeDtypeStruct((k + k // 2, 2 * k), jnp.float32)],
+        in_specs=[mine, whole, whole, whole],
+        out_specs=[whole, whole],
+        compiler_params=params(16),
+        cost_estimate=pl.CostEstimate(flops=6 * 2 * 3 * k * k * n, bytes_accessed=4 * k * n * 4, transcendentals=0),
+        name="first_gram",
+    )(partial, other, self_row, direction)
+
+
+def first_update_kernel(*refs, count):
+    part_refs, (image_ref, direction_ref, alpha_ref, residual_ref, next_ref, charges_ref) = refs[:count], refs[count:]
+    total = sum_of([ref[...] for ref in part_refs])
+    k = total.shape[1] // 2
+    gram, image_sq, norm = total[:k, :k], total[:k, k:], unfold(total[k:, :])
+    norm = 0.5 * (norm + norm.T)
+    unit = (lax.broadcasted_iota(jnp.int32, (k, k), 0) == lax.broadcasted_iota(jnp.int32, (k, k), 1)).astype(jnp.float32)
+    alpha, inverse = eliminate([
+        jnp.concatenate([0.5 * (gram + gram.T), norm], axis=1),
+        jnp.concatenate([norm, unit], axis=1),
+    ])
+    cross = mul(gram, alpha)
+    norm_next = norm - cross - cross.T + left_t(alpha, mul(image_sq, alpha))
+    beta = mul(inverse, norm_next)
+    alpha_ref[:, :k] = alpha
+    alpha_ref[:, k:] = norm_next
+    direction = direction_ref[...]
+    residual = direction - left_t(alpha, image_ref[...])
+    residual_ref[...] = residual
+    later = residual + left_t(beta, direction)
+    next_ref[...] = later
+    charges_ref[...] = later.astype(jnp.bfloat16)
+
+
+def sum_of(values):
+    while len(values) > 1:
+        values = [values[i] + values[i + 1] for i in range(0, len(values), 2)]
+    return values[0]
+
+
+def first_update(parts, image, direction):
+    k, n = direction.shape
+    whole = pl.BlockSpec(memory_space=pltpu.VMEM)
+    return pl.pallas_call(
+        functools.partial(first_update_kernel, count=len(parts)),
+        out_shape=[
+            jax.ShapeDtypeStruct((k, 2 * k), jnp.float32),
+            jax.ShapeDtypeStruct((k, n), jnp.float32),
+            jax.ShapeDtypeStruct((k, n), jnp.float32),
+            jax.ShapeDtypeStruct((k, n), jnp.bfloat16),
+        ],
+        in_specs=[whole] * (len(parts) + 2),
+        out_specs=[whole] * 4,
+        compiler_params=params(16),
+        cost_estimate=pl.CostEstimate(flops=6 * 2 * 2 * k * k * n, bytes_accessed=4 * k * n * 5, transcendentals=0),
+        name="first_update",
+    )(*parts, image, direction)
+
+
+def second_gram_kernel(own_ref, other_ref, self_ref, direction_ref, image_ref, gram_ref):
+    direction = direction_ref[...]
+    image = own_ref[...] + other_ref[...] + self_ref[...] * direction
+    image_ref[...] = image
+    k = direction.shape[0]
+    gram_ref[:, :k] = dots(direction, image)
+    gram_ref[:, k:] = jnp.zeros((k, k), jnp.float32)
+
+
+def second_gram(partial, other, self_row, direction):
+    k, n = direction.shape
+    mine = pl.BlockSpec((k, n), lambda i: (0, 0))
+    whole = pl.BlockSpec(memory_space=pltpu.VMEM)
+    return pl.pallas_call(
+        second_gram_kernel,
+        grid=(1,),
+        out_shape=[jax.ShapeDtypeStruct((k, n), jnp.float32), jax.ShapeDtypeStruct((k, 2 * k), jnp.float32)],
+        in_specs=[mine, whole, whole, whole],
+        out_specs=[whole, whole],
+        compiler_params=params(16),
+        cost_estimate=pl.CostEstimate(flops=6 * 2 * k * k * n, bytes_accessed=4 * k * n * 4, transcendentals=0),
+        name="second_gram",
+    )(partial, other, self_row, direction)
+
+
+def last_update_kernel(*refs, count):
+    part_refs = refs[:count]
+    alpha_ref, first_ref, residual_ref, direction_ref, image_ref, charge_ref, out_ref = refs[count:]
+    total = sum_of([ref[...] for ref in part_refs])
+    k = total.shape[0]
+    gram = total[:, :k]
+    (alpha,) = eliminate([jnp.concatenate([0.5 * (gram + gram.T), alpha_ref[:, k:]], axis=1)])
+    charge_ref[...] = left_t(alpha_ref[:, :k], first_ref[...]) + left_t(alpha, direction_ref[...])
+    out_ref[...] = residual_ref[...] - left_t(alpha, image_ref[...])
+
+
+def last_update(parts, alpha, first, residual, direction, image):
+    k, n = first.shape
+    whole = pl.BlockSpec(memory_space=pltpu.VMEM)
+    return pl.pallas_call(
+        functools.partial(last_update_kernel, count=len(parts)),
+        out_shape=[jax.ShapeDtypeStruct((k, n), jnp.float32)] * 2,
+        in_specs=[whole] * (len(parts) + 5),
+        out_specs=[whole] * 2,
+        compiler_params=params(16),
+        cost_estimate=pl.CostEstimate(flops=6 * 3 * 2 * k * k * n, bytes_accessed=4 * k * n * 6, transcendentals=0),
+        name="last_update",
+    )(*parts, alpha, first, residual, direction, image)
+
+
+def per_device_grouped(right_side, atom_centers, tessera_owner, tessera_angles, self_term):
+    columns, shard = right_side.shape
+    n_tgt = lax.axis_size("tgt")
+    n_src = lax.axis_size("src")
+    t = lax.axis_index("tgt")
+    s = lax.axis_index("src")
+    copies = n_tgt // GROUP
+    member = t % GROUP
+    ours = t // GROUP
+    width = shard * n_src
+
+    def swap(value, bits):
+        return lax.ppermute(value, "tgt", [(i, i ^ bits) for i in range(n_tgt)])
+
+    def swap_core(value):
+        return lax.ppermute(value, "src", [(0, 1), (1, 0)])
+
+    near = jnp.concatenate([right_side, jnp.broadcast_to(self_term[None, :], (8, shard))], axis=0)
+    far = swap(near, GROUP)
+    both = jnp.where(ours == 0, jnp.concatenate([near, far], axis=1), jnp.concatenate([far, near], axis=1))
+    direction, self_row = both[:columns], both[columns : columns + 1]
+    charges = direction.astype(jnp.bfloat16)
+    gathered = [charges] + [swap(charges, bits) for bits in range(1, GROUP)]
+
+    table = jnp.pad(atom_centers, ((0, 0), (0, -atom_centers.shape[1] % (LOW * 8)))).reshape(-1, LOW)
+    offsets = unit_offsets(tessera_angles.reshape(2, -1, 128)).reshape(3, -1)
+    starts = [((member ^ bits) + GROUP * c) * width + s * shard for bits in range(GROUP) for c in range(copies)]
+    starts += [(member + GROUP * c) * width + (1 - s) * shard for c in range(copies)]
+    pos = chosen_positions(table, tessera_owner[None, :], offsets, jnp.stack(starts).astype(jnp.int32), shard)
+    n_near = copies * shard
+    n_all = GROUP * n_near
+    target_pos = jnp.concatenate([pos[:, :n_near], pos[:, n_all:]], axis=1)
+    kern = entries(pos[:, :n_all].T, target_pos)
+
+    def group_sum_parts(value):
+        value = value + swap_core(value)
+        return [value] + [swap(value, bits) for bits in range(1, GROUP)]
+
+    partial = apply_entries(gathered, kern)
+    image, gram = first_gram(partial, swap_core(partial[:, n_near:]), self_row, direction)
+    alpha, residual, later, charges = first_update(group_sum_parts(gram), image, direction)
+
+    gathered = [charges] + [swap(charges, bits) for bits in range(1, GROUP)]
+    partial = apply_entries(gathered, kern)
+    image, gram = second_gram(partial, swap_core(partial[:, n_near:]), self_row, later)
+    parts = group_sum_parts(gram)
+
+    def mine(value):
+        return lax.dynamic_slice_in_dim(value, ours * shard, shard, 1)
+
+    return tuple(last_update(parts, alpha, right_side, mine(residual), mine(later), mine(image)))
+
+
 def solution(mesh):
-    return jax.shard_map(
-        per_device,
-        mesh=mesh,
-        in_specs=(P("conf", ("tgt", "src")), P("conf", None), P(), P(), P(("tgt", "src"))),
-        out_specs=(P("conf", ("tgt", "src")), P("conf", ("tgt", "src"))),
-        check_vma=False,
-    )
+    n_tgt, n_src = mesh.shape["tgt"], mesh.shape["src"]
+
+    def run(right_side, atom_centers, tessera_owner, tessera_angles, self_term):
+        total = right_side.shape[1]
+        stored = 2 * (total // n_src) * (total // GROUP)
+        grouped = n_tgt == 2 * GROUP and n_src == 2 and stored <= STORED_LIMIT
+        return jax.shard_map(
+            per_device_grouped if grouped else per_device_general,
+            mesh=mesh,
+            in_specs=(P("conf", ("tgt", "src")), P("conf", None), P(), P(), P(("tgt", "src"))),
+            out_specs=(P("conf", ("tgt", "src")), P("conf", ("tgt", "src"))),
+            check_vma=False,
+        )(right_side, atom_centers, tessera_owner, tessera_angles, self_term)
+
+    return run

time: 393 us -> 89.1 us (0.23)
  blocking collectives: 246 us -> 0 us
  local copies, waits for them, and re-layouts: 51.4 us -> 3.91 us
  Pallas kernels: 0 us -> 43.3 us
  other arithmetic: 40.7 us -> 3.77 us
  matrix products: 25 us -> 0 us
  starting transfers between devices: 0.08 us -> 18.8 us
  between operations: 14.3 us -> 0.9 us
  waiting for transfers between devices: 13.4 us -> 18 us
    psum x3 -> x0, blocking collectives: 182 us -> none  [the longest x2 120 us: residual_norm(): return lax.psum(products(residual, residual), ('tgt', 'src'))]
    all_gather x2 -> x0, blocking collectives: 64.3 us -> none  [per_device(): piece = lax.all_gather(charges, 'tgt', axis=1, tiled=True)]
    pallas_call x0 -> x8, Pallas kernels: none -> 43.3 us  [the longest x1 13.7 us: entries(): pl.pallas_call(entry_kernel, grid=(n // step,), out_shape=jax.ShapeDtypeS...]
    gather x2 -> x0, local copies, waits for them, and re-layouts: 37.4 us -> none  [positions(): base = jnp.take(atom_centers, tessera_owner, axis=1)]
    another operation x15 -> x1, other arithmetic: 36.2 us -> 0.09 us  [unit_offsets(): jnp.stack([jnp.cos(azimuth) * sine, jnp.sin(azimuth) * sine, jnp.cos(pola...]
    dot_general x25 -> x0, matrix products: 23.8 us -> none  [the longest x16 16.2 us: tile_apply(): return total + jnp.dot(charges, kern, preferred_element_type=jnp.float32)]
    ppermute x0 -> x17, starting transfers between devices: none -> 18.8 us  [the longest x13 18.2 us: swap(): return lax.ppermute(value, 'tgt', [(i, i ^ bits) for i in range(n_tgt)])]
    ppermute x0 -> x17, waiting for transfers between devices: none -> 18 us  [the longest x13 12.9 us: swap(): return lax.ppermute(value, 'tgt', [(i, i ^ bits) for i in range(n_tgt)])]
  transfers between devices with their start and end apart: 2 -> 17, of which waited for: 2 -> 13; matrix products, arithmetic and copies ran while one was open for 0% -> 6% of each run, Pallas kernels for 0% -> 23%
where the time goes in v1:
time: 89.1 us; the launch traced here: 88.7 us
  Pallas kernels  43.3 us (49%)
  starting transfers between devices  18.8 us (21%)
  waiting for transfers between devices  18 us (20%)
  local copies, waits for them, and re-layouts  3.91 us (4%)
  other arithmetic  3.77 us (4%)
  between operations  0.9 us (1%)
    ppermute x13, starting transfers between devices, swap(): return lax.ppermute(value, 'tgt', [(i, i ^ bits) for i in range(n_tgt)])  18.2 us
    pallas_call x1, Pallas kernels, entries(): pl.pallas_call(entry_kernel, grid=(n // step,), out_shape=jax.ShapeDtypeS...  13.7 us
    ppermute x13, waiting for transfers between devices, swap(): return lax.ppermute(value, 'tgt', [(i, i ^ bits) for i in range(n_tgt)])  12.9 us
    pallas_call x2, Pallas kernels, apply_entries(): pl.pallas_call(functools.partial(apply_kernel, pieces=pieces, per=per), g...  8.3 us
    pallas_call x1, Pallas kernels, first_update(): pl.pallas_call(functools.partial(first_update_kernel, count=len(parts)),...  7.01 us
    pallas_call x1, Pallas kernels, last_update(): pl.pallas_call(functools.partial(last_update_kernel, count=len(parts)), o...  6.73 us
    pallas_call x1, Pallas kernels, chosen_positions(): pl.pallas_call(functools.partial(position_kernel, chunk=chunk, count=coun...  6.31 us
    ppermute x4, waiting for transfers between devices, swap_core(): return lax.ppermute(value, 'src', [(0, 1), (1, 0)])  5.14 us
  transfers between devices with their start and end apart: 17, of which 13 were waited for; matrix products, arithmetic and copies ran while one was open for 6% of the time, Pallas kernels for 23%

profile of v1, /device:TPU:0, one launch (start us, length us, event | category | flops | bytes accessed | tf_op | source)
XLA Modules:
  0.0 88.7 jit_solution(6757694781777600495)
XLA Ops:
  0.6 0.0 copy-start
  0.6 0.7 broadcast_in_dim.4
  1.4 0.9 %pad_maximum_fusion = f32[72,512]{1,0:T(8,128)S(1)} fusion(f32[8,512]{1,0:T(8,128)S(1)} %broadcast_in_dim.4, f32[64,512]{1,0:T(8,128)} %refs_5_.1), kind=kLoop, calls=%fused_computation.1 | loop fusion | flops 36864 | bytes 294912 | tf_op jit(solution)/shard_map/concatenate | solution.py:391
  2.3 4.1 %collective-permute-start = (f32[72,512]{1,0:T(8,128)S(1)}, f32[72,512]{1,0:T(8,128)S(1)}, u32[]{:S(2)}, u32[]{:S(2)}) collective-permute-start(f32[72,512]{1,0:T(8,128)S(1)} %pad_maximum_fusion), channel_id=1, source_target_pairs={{0,8},{2,10},{4,12},{6,14},{8,0},{10,2},{12,4},{14,6},{1,9},{3,11}... | collective-permute-start | bytes 442376 | tf_op jit(solution)/shard_map/ppermute | solution.py:386
  6.4 2.7 %cosine_multiply_fusion = (f32[1,8192]{1,0:T(1,128)S(1)}, f32[1,8192]{1,0:T(1,128)S(1)}, f32[1,8192]{1,0:T(1,128)S(1)}) fusion(f32[2,8192]{1,0:T(2,128)} %param.8), kind=kLoop, calls=%fused_computation.5 | loop fusion | flops 16384 | bytes 163840 | tf_op jit(solution)/shard_map/mul | solution.py:34
  9.1 1.2 %pad.4 = f32[3,40960]{1,0:T(4,128)S(1)} pad(f32[3,40000]{1,0:T(4,128)} %param.6, f32[]{:T(128)} %constant.43.clone.1), padding=0_0x0_960 | pad | bytes 971524 | tf_op jit(solution)/shard_map/jit(_pad)/pad | solution.py:398
  10.3 0.4 reshape.22.table_ref
  10.7 0.1 pad_maximum_fusion.1.offset_ref
  10.8 0.1 stack.49.starts
  10.9 0.0 copy-start.1
  10.9 0.8 copy-done.1
  11.6 6.3 %positions.1 = f32[3,5120]{1,0:T(4,128)S(1)} custom-call(s32[10]{0:T(128)S(1)} %stack.49.starts, f32[480,256]{1,0:T(8,128)S(1)} %reshape.22.table_ref, s32[1,8192]{1,0:T(1,128)S(1)} %bitcast.13, f32[3,8192]{1,0:T(4,128)S(1)} %pad_maximum_fusion.1.offset_ref), custom_call_target="tpu_custom_call" | custom-call | flops 3774873600 | bytes 480000 | tf_op jit(solution)/shard_map/positions/pallas_call | solution.py:145
  18.0 0.6 copy.7
  18.7 0.0 collective-permute-done
  18.7 0.0 copy-done
  18.7 1.6 %collective-permute-start.1 = (bf16[64,1024]{1,0:T(8,128)(2,1)S(1)}, bf16[64,1024]{1,0:T(8,128)(2,1)S(1)}, u32[]{:S(2)}, u32[]{:S(2)}) collective-permute-start(bf16[64,1024]{1,0:T(8,128)(2,1)S(1)} %slice.54.refs_0_), channel_id=1, source_target_pairs={{0,2},{2,0},{4,6},{6,4},{8,10},{10,8},{12,14},{14,12},{1,3},{3,1},... | collective-permute-start | bytes 393224 | tf_op jit(solution)/shard_map/ppermute | solution.py:386
  20.3 1.6 %collective-permute-start.2 = (bf16[64,1024]{1,0:T(8,128)(2,1)S(1)}, bf16[64,1024]{1,0:T(8,128)(2,1)S(1)}, u32[]{:S(2)}, u32[]{:S(2)}) collective-permute-start(bf16[64,1024]{1,0:T(8,128)(2,1)S(1)} %slice.54.refs_0_), channel_id=1, source_target_pairs={{0,4},{2,6},{4,0},{6,2},{8,12},{10,14},{12,8},{14,10},{1,5},{3,7},... | collective-permute-start | bytes 393224 | tf_op jit(solution)/shard_map/ppermute | solution.py:386
  21.9 0.4 collective-permute-start.3
  22.3 13.7 %entries.1.refs_4_ = bf16[4096,2048]{1,0:T(8,128)(2,1)S(1)} custom-call(f32[4096,3]{1,0:T(8,128)S(1)} %bitcast.12, f32[3,2048]{1,0:T(4,128)S(1)} %pad_maximum_fusion.2.target_ref), custom_call_target="tpu_custom_call" | custom-call | flops 100663296 | bytes 16777216 | tf_op jit(solution)/shard_map/entries/pallas_call | solution.py:168
  36.0 0.0 collective-permute-done.1.refs_1_
  36.0 0.0 collective-permute-done.2.refs_2_
  36.0 0.0 collective-permute-done.3.refs_3_
  36.1 4.2 %apply.2.own_ref = f32[64,2048]{1,0:T(8,128)S(1)} custom-call(bf16[64,1024]{1,0:T(8,128)(2,1)S(1)} %slice.54.refs_0_, bf16[64,1024]{1,0:T(8,128)(2,1)S(1)} %collective-permute-done.1.refs_1_, bf16[64,1024]{1,0:T(8,128)(2,1)S(1)} %collective-permute-done.2.refs_2_, bf16[64,1024]{1,0:T(8,128)(2,1)S(1)} %collective-permute-done.3.refs_3_, ...), custom_call_target="tpu_custom_call" | custom-call | flops 1073741824 | bytes 16777216 | tf_op jit(solution)/shard_map/apply/pallas_call | solution.py:204
  40.3 0.1 collective-permute-start.4
  40.4 1.5 %collective-permute-done.4.other_ref = f32[64,1024]{1,0:T(8,128)S(1)} collective-permute-done((f32[64,1024]{1,0:T(8,128)S(1)}, f32[64,1024]{1,0:T(8,128)S(1)}, u32[]{:S(2)}, u32[]{:S(2)}) %collective-permute-start.4) | collective-permute-done | bytes 262176 | tf_op jit(solution)/shard_map/ppermute | solution.py:389
  41.9 0.9 first_gram.1
  42.7 0.2 collective-permute-start.5
  42.9 1.1 %collective-permute-done.5 = f32[96,128]{1,0:T(8,128)S(1)} collective-permute-done((f32[96,128]{1,0:T(8,128)S(1)}, f32[96,128]{1,0:T(8,128)S(1)}, u32[]{:S(2)}, u32[]{:S(2)}) %collective-permute-start.5) | collective-permute-done | bytes 49184 | tf_op jit(solution)/shard_map/ppermute | solution.py:389
  44.0 1.6 %collective-permute-start.6 = (f32[96,128]{1,0:T(8,128)S(1)}, f32[96,128]{1,0:T(8,128)S(1)}, u32[]{:S(2)}, u32[]{:S(2)}) collective-permute-start(f32[96,128]{1,0:T(8,128)S(1)} %add.76.refs_0_), channel_id=1, source_target_pairs={{0,2},{2,0},{4,6},{6,4},{8,10},{10,8},{12,14},{14,12},{1,3},{3,1},... | collective-permute-start | bytes 147464 | tf_op jit(solution)/shard_map/ppermute | solution.py:386
  45.6 1.6 %collective-permute-start.7 = (f32[96,128]{1,0:T(8,128)S(1)}, f32[96,128]{1,0:T(8,128)S(1)}, u32[]{:S(2)}, u32[]{:S(2)}) collective-permute-start(f32[96,128]{1,0:T(8,128)S(1)} %add.76.refs_0_), channel_id=1, source_target_pairs={{0,4},{2,6},{4,0},{6,2},{8,12},{10,14},{12,8},{14,10},{1,5},{3,7},... | collective-permute-start | bytes 147464 | tf_op jit(solution)/shard_map/ppermute | solution.py:386
  47.2 0.4 collective-permute-start.8
  47.6 0.6 collective-permute-done.6.refs_1_
  48.2 1.9 %collective-permute-done.7.refs_2_ = f32[96,128]{1,0:T(8,128)S(1)} collective-permute-done((f32[96,128]{1,0:T(8,128)S(1)}, f32[96,128]{1,0:T(8,128)S(1)}, u32[]{:S(2)}, u32[]{:S(2)}) %collective-permute-start.7) | collective-permute-done | bytes 49184 | tf_op jit(solution)/shard_map/ppermute | solution.py:386
  50.1 2.1 %collective-permute-done.8.refs_3_ = f32[96,128]{1,0:T(8,128)S(1)} collective-permute-done((f32[96,128]{1,0:T(8,128)S(1)}, f32[96,128]{1,0:T(8,128)S(1)}, u32[]{:S(2)}, u32[]{:S(2)}) %collective-permute-start.8) | collective-permute-done | bytes 49184 | tf_op jit(solution)/shard_map/ppermute | solution.py:386
  52.2 7.0 %first_update.1 = (f32[64,128]{1,0:T(8,128)S(1)}, f32[64,1024]{1,0:T(8,128)S(1)}, f32[64,1024]{1,0:T(8,128)S(1)}, bf16[64,1024]{1,0:T(8,128)(2,1)S(1)}) custom-call(f32[96,128]{1,0:T(8,128)S(1)} %add.76.refs_0_, f32[96,128]{1,0:T(8,128)S(1)} %collective-permute-done.6.refs_1_, f32[96,128]{1,0:T(8,128)S(1)} %collective-permute-done.7.refs_2_, ...), custom_call_target="tpu_custom_call" | custom-call | flops 100663296 | bytes 1310720 | tf_op jit(solution)/shard_map/first_update/pallas_call | solution.py:308
  59.2 0.5 collective-permute-start.10
  59.7 1.5 %collective-permute-start.11 = (bf16[64,1024]{1,0:T(8,128)(2,1)S(1)}, bf16[64,1024]{1,0:T(8,128)(2,1)S(1)}, u32[]{:S(2)}, u32[]{:S(2)}) collective-permute-start(bf16[64,1024]{1,0:T(8,128)(2,1)S(1)} %get-tuple-element.12.refs_0_), channel_id=1, source_target_pairs={{0,6},{2,4},{4,2},{6,0},{8,14},{10,12},{12,10},{14,8},{1,7},{3,5},... | collective-permute-start | bytes 393224 | tf_op jit(solution)/shard_map/ppermute | solution.py:386
  61.2 1.5 %collective-permute-start.9 = (bf16[64,1024]{1,0:T(8,128)(2,1)S(1)}, bf16[64,1024]{1,0:T(8,128)(2,1)S(1)}, u32[]{:S(2)}, u32[]{:S(2)}) collective-permute-start(bf16[64,1024]{1,0:T(8,128)(2,1)S(1)} %get-tuple-element.12.refs_0_), channel_id=1, source_target_pairs={{0,2},{2,0},{4,6},{6,4},{8,10},{10,8},{12,14},{14,12},{1,3},{3,1},... | collective-permute-start | bytes 393224 | tf_op jit(solution)/shard_map/ppermute | solution.py:386
  62.8 1.8 %collective-permute-done.10.refs_2_ = bf16[64,1024]{1,0:T(8,128)(2,1)S(1)} collective-permute-done((bf16[64,1024]{1,0:T(8,128)(2,1)S(1)}, bf16[64,1024]{1,0:T(8,128)(2,1)S(1)}, u32[]{:S(2)}, u32[]{:S(2)}) %collective-permute-start.10) | collective-permute-done | bytes 131104 | tf_op jit(solution)/shard_map/ppermute | solution.py:386
  64.5 1.8 %collective-permute-done.11.refs_3_ = bf16[64,1024]{1,0:T(8,128)(2,1)S(1)} collective-permute-done((bf16[64,1024]{1,0:T(8,128)(2,1)S(1)}, bf16[64,1024]{1,0:T(8,128)(2,1)S(1)}, u32[]{:S(2)}, u32[]{:S(2)}) %collective-permute-start.11) | collective-permute-done | bytes 131104 | tf_op jit(solution)/shard_map/ppermute | solution.py:386
  66.4 1.3 %collective-permute-done.9.refs_1_ = bf16[64,1024]{1,0:T(8,128)(2,1)S(1)} collective-permute-done((bf16[64,1024]{1,0:T(8,128)(2,1)S(1)}, bf16[64,1024]{1,0:T(8,128)(2,1)S(1)}, u32[]{:S(2)}, u32[]{:S(2)}) %collective-permute-start.9) | collective-permute-done | bytes 131104 | tf_op jit(solution)/shard_map/ppermute | solution.py:386
  67.7 4.1 %apply.3.own_ref = f32[64,2048]{1,0:T(8,128)S(1)} custom-call(bf16[64,1024]{1,0:T(8,128)(2,1)S(1)} %get-tuple-element.12.refs_0_, bf16[64,1024]{1,0:T(8,128)(2,1)S(1)} %collective-permute-done.9.refs_1_, bf16[64,1024]{1,0:T(8,128)(2,1)S(1)} %collective-permute-done.10.refs_2_, bf16[64,1024]{1,0:T(8,128)(2,1)S(1)} %collective-permute-done.11.refs_3_, ...), custom_call_target="tpu_custom_call" | custom-call | flops 1073741824 | bytes 16777216 | tf_op jit(solution)/shard_map/apply/pallas_call | solution.py:204
  71.8 0.1 collective-permute-start.12
  71.9 1.5 %collective-permute-done.12.other_ref = f32[64,1024]{1,0:T(8,128)S(1)} collective-permute-done((f32[64,1024]{1,0:T(8,128)S(1)}, f32[64,1024]{1,0:T(8,128)S(1)}, u32[]{:S(2)}, u32[]{:S(2)}) %collective-permute-start.12) | collective-permute-done | bytes 262176 | tf_op jit(solution)/shard_map/ppermute | solution.py:389
  73.4 0.4 second_gram.1
  73.8 0.2 collective-permute-start.13
  74.0 1.1 %collective-permute-done.13 = f32[64,128]{1,0:T(8,128)S(1)} collective-permute-done((f32[64,128]{1,0:T(8,128)S(1)}, f32[64,128]{1,0:T(8,128)S(1)}, u32[]{:S(2)}, u32[]{:S(2)}) %collective-permute-start.13) | collective-permute-done | bytes 32800 | tf_op jit(solution)/shard_map/ppermute | solution.py:389
  75.1 1.1 %collective-permute-start.14 = (f32[64,128]{1,0:T(8,128)S(1)}, f32[64,128]{1,0:T(8,128)S(1)}, u32[]{:S(2)}, u32[]{:S(2)}) collective-permute-start(f32[64,128]{1,0:T(8,128)S(1)} %add.77.refs_0_), channel_id=1, source_target_pairs={{0,2},{2,0},{4,6},{6,4},{8,10},{10,8},{12,14},{14,12},{1,3},{3,1},... | collective-permute-start | bytes 98312 | tf_op jit(solution)/shard_map/ppermute | solution.py:386
  76.2 1.0 %collective-permute-start.15 = (f32[64,128]{1,0:T(8,128)S(1)}, f32[64,128]{1,0:T(8,128)S(1)}, u32[]{:S(2)}, u32[]{:S(2)}) collective-permute-start(f32[64,128]{1,0:T(8,128)S(1)} %add.77.refs_0_), channel_id=1, source_target_pairs={{0,4},{2,6},{4,0},{6,2},{8,12},{10,14},{12,8},{14,10},{1,5},{3,7},... | collective-permute-start | bytes 98312 | tf_op jit(solution)/shard_map/ppermute | solution.py:386
  77.2 1.4 %collective-permute-start.16 = (f32[64,128]{1,0:T(8,128)S(1)}, f32[64,128]{1,0:T(8,128)S(1)}, u32[]{:S(2)}, u32[]{:S(2)}) collective-permute-start(f32[64,128]{1,0:T(8,128)S(1)} %add.77.refs_0_), channel_id=1, source_target_pairs={{0,6},{2,4},{4,2},{6,0},{8,14},{10,12},{12,10},{14,8},{1,7},{3,5},... | collective-permute-start | bytes 98312 | tf_op jit(solution)/shard_map/ppermute | solution.py:386
  78.6 0.4 collective-permute-done.14.refs_1_
  79.0 1.1 %collective-permute-done.15.refs_2_ = f32[64,128]{1,0:T(8,128)S(1)} collective-permute-done((f32[64,128]{1,0:T(8,128)S(1)}, f32[64,128]{1,0:T(8,128)S(1)}, u32[]{:S(2)}, u32[]{:S(2)}) %collective-permute-start.15) | collective-permute-done | bytes 32800 | tf_op jit(solution)/shard_map/ppermute | solution.py:386
  80.1 1.9 %collective-permute-done.16.refs_3_ = f32[64,128]{1,0:T(8,128)S(1)} collective-permute-done((f32[64,128]{1,0:T(8,128)S(1)}, f32[64,128]{1,0:T(8,128)S(1)}, u32[]{:S(2)}, u32[]{:S(2)}) %collective-permute-start.16) | collective-permute-done | bytes 32800 | tf_op jit(solution)/shard_map/ppermute | solution.py:386
  82.0 6.7 %last_update.1 = (f32[64,512]{1,0:T(8,128)}, f32[64,512]{1,0:T(8,128)}) custom-call(f32[64,128]{1,0:T(8,128)S(1)} %add.77.refs_0_, f32[64,128]{1,0:T(8,128)S(1)} %collective-permute-done.14.refs_1_, f32[64,128]{1,0:T(8,128)S(1)} %collective-permute-done.15.refs_2_, f32[64,128]{1,0:T(8,128)S(1)} %collective-permute-done.16.refs_3_, ...), custom_call_target="tpu_custom_call" | custom-call | flops 75497472 | bytes 786432 | tf_op jit(solution)/shard_map/last_update/pallas_call | solution.py:363
  (13 shorter events, 0.2 us)
Async XLA Ops:
  0.6 18.0 %copy-start = (f32[64,512]{1,0:T(8,128)S(1)}, f32[64,512]{1,0:T(8,128)}, u32[]{:S(2)}) copy-start(f32[64,512]{1,0:T(8,128)} %refs_5_.1) | copy-start | bytes 393220
  2.3 16.4 %collective-permute-start = (f32[72,512]{1,0:T(8,128)S(1)}, f32[72,512]{1,0:T(8,128)S(1)}, u32[]{:S(2)}, u32[]{:S(2)}) collective-permute-start(f32[72,512]{1,0:T(8,128)S(1)} %pad_maximum_fusion), channel_id=1, source_target_pairs={{0,8},{2,10},{4,12},{6,14},{8,0},{10,2},{12,4},{14,6},{1,9},{3,11}... | collective-permute-start | bytes 442376 | tf_op jit(solution)/shard_map/ppermute | solution.py:386
  10.9 0.8 copy-start.1
  18.7 17.3 %collective-permute-start.1 = (bf16[64,1024]{1,0:T(8,128)(2,1)S(1)}, bf16[64,1024]{1,0:T(8,128)(2,1)S(1)}, u32[]{:S(2)}, u32[]{:S(2)}) collective-permute-start(bf16[64,1024]{1,0:T(8,128)(2,1)S(1)} %slice.54.refs_0_), channel_id=1, source_target_pairs={{0,2},{2,0},{4,6},{6,4},{8,10},{10,8},{12,14},{14,12},{1,3},{3,1},... | collective-permute-start | bytes 393224 | tf_op jit(solution)/shard_map/ppermute | solution.py:386
  20.3 15.7 %collective-permute-start.2 = (bf16[64,1024]{1,0:T(8,128)(2,1)S(1)}, bf16[64,1024]{1,0:T(8,128)(2,1)S(1)}, u32[]{:S(2)}, u32[]{:S(2)}) collective-permute-start(bf16[64,1024]{1,0:T(8,128)(2,1)S(1)} %slice.54.refs_0_), channel_id=1, source_target_pairs={{0,4},{2,6},{4,0},{6,2},{8,12},{10,14},{12,8},{14,10},{1,5},{3,7},... | collective-permute-start | bytes 393224 | tf_op jit(solution)/shard_map/ppermute | solution.py:386
  21.9 14.2 %collective-permute-start.3 = (bf16[64,1024]{1,0:T(8,128)(2,1)S(1)}, bf16[64,1024]{1,0:T(8,128)(2,1)S(1)}, u32[]{:S(2)}, u32[]{:S(2)}) collective-permute-start(bf16[64,1024]{1,0:T(8,128)(2,1)S(1)} %slice.54.refs_0_), channel_id=1, source_target_pairs={{0,6},{2,4},{4,2},{6,0},{8,14},{10,12},{12,10},{14,8},{1,7},{3,5},... | collective-permute-start | bytes 393224 | tf_op jit(solution)/shard_map/ppermute | solution.py:386
  40.3 1.6 %collective-permute-start.4 = (f32[64,1024]{1,0:T(8,128)S(1)}, f32[64,1024]{1,0:T(8,128)S(1)}, u32[]{:S(2)}, u32[]{:S(2)}) collective-permute-start(f32[64,1024]{1,0:T(8,128)S(1)} %slice.42), channel_id=1, source_target_pairs={{0,1},{1,0},{2,3},{3,2},{4,5},{5,4},{6,7},{7,6},{8,9},{9,8},{10,11... | collective-permute-start | bytes 786440 | tf_op jit(solution)/shard_map/ppermute | solution.py:389
  42.7 1.3 %collective-permute-start.5 = (f32[96,128]{1,0:T(8,128)S(1)}, f32[96,128]{1,0:T(8,128)S(1)}, u32[]{:S(2)}, u32[]{:S(2)}) collective-permute-start(f32[96,128]{1,0:T(8,128)S(1)} %get-tuple-element.10), channel_id=1, source_target_pairs={{0,1},{1,0},{2,3},{3,2},{4,5},{5,4},{6,7},{7,6},{8,9},{9,8},{10,11... | collective-permute-start | bytes 147464 | tf_op jit(solution)/shard_map/ppermute | solution.py:389
  44.0 4.2 %collective-permute-start.6 = (f32[96,128]{1,0:T(8,128)S(1)}, f32[96,128]{1,0:T(8,128)S(1)}, u32[]{:S(2)}, u32[]{:S(2)}) collective-permute-start(f32[96,128]{1,0:T(8,128)S(1)} %add.76.refs_0_), channel_id=1, source_target_pairs={{0,2},{2,0},{4,6},{6,4},{8,10},{10,8},{12,14},{14,12},{1,3},{3,1},... | collective-permute-start | bytes 147464 | tf_op jit(solution)/shard_map/ppermute | solution.py:386
  45.6 4.5 %collective-permute-start.7 = (f32[96,128]{1,0:T(8,128)S(1)}, f32[96,128]{1,0:T(8,128)S(1)}, u32[]{:S(2)}, u32[]{:S(2)}) collective-permute-start(f32[96,128]{1,0:T(8,128)S(1)} %add.76.refs_0_), channel_id=1, source_target_pairs={{0,4},{2,6},{4,0},{6,2},{8,12},{10,14},{12,8},{14,10},{1,5},{3,7},... | collective-permute-start | bytes 147464 | tf_op jit(solution)/shard_map/ppermute | solution.py:386
  47.2 5.0 %collective-permute-start.8 = (f32[96,128]{1,0:T(8,128)S(1)}, f32[96,128]{1,0:T(8,128)S(1)}, u32[]{:S(2)}, u32[]{:S(2)}) collective-permute-start(f32[96,128]{1,0:T(8,128)S(1)} %add.76.refs_0_), channel_id=1, source_target_pairs={{0,6},{2,4},{4,2},{6,0},{8,14},{10,12},{12,10},{14,8},{1,7},{3,5},... | collective-permute-start | bytes 147464 | tf_op jit(solution)/shard_map/ppermute | solution.py:386
  59.2 5.3 %collective-permute-start.10 = (bf16[64,1024]{1,0:T(8,128)(2,1)S(1)}, bf16[64,1024]{1,0:T(8,128)(2,1)S(1)}, u32[]{:S(2)}, u32[]{:S(2)}) collective-permute-start(bf16[64,1024]{1,0:T(8,128)(2,1)S(1)} %get-tuple-element.12.refs_0_), channel_id=1, source_target_pairs={{0,4},{2,6},{4,0},{6,2},{8,12},{10,14},{12,8},{14,10},{1,5},{3,7},... | collective-permute-start | bytes 393224 | tf_op jit(solution)/shard_map/ppermute | solution.py:386
  59.7 6.6 %collective-permute-start.11 = (bf16[64,1024]{1,0:T(8,128)(2,1)S(1)}, bf16[64,1024]{1,0:T(8,128)(2,1)S(1)}, u32[]{:S(2)}, u32[]{:S(2)}) collective-permute-start(bf16[64,1024]{1,0:T(8,128)(2,1)S(1)} %get-tuple-element.12.refs_0_), channel_id=1, source_target_pairs={{0,6},{2,4},{4,2},{6,0},{8,14},{10,12},{12,10},{14,8},{1,7},{3,5},... | collective-permute-start | bytes 393224 | tf_op jit(solution)/shard_map/ppermute | solution.py:386
  61.2 6.4 %collective-permute-start.9 = (bf16[64,1024]{1,0:T(8,128)(2,1)S(1)}, bf16[64,1024]{1,0:T(8,128)(2,1)S(1)}, u32[]{:S(2)}, u32[]{:S(2)}) collective-permute-start(bf16[64,1024]{1,0:T(8,128)(2,1)S(1)} %get-tuple-element.12.refs_0_), channel_id=1, source_target_pairs={{0,2},{2,0},{4,6},{6,4},{8,10},{10,8},{12,14},{14,12},{1,3},{3,1},... | collective-permute-start | bytes 393224 | tf_op jit(solution)/shard_map/ppermute | solution.py:386
  71.8 1.6 %collective-permute-start.12 = (f32[64,1024]{1,0:T(8,128)S(1)}, f32[64,1024]{1,0:T(8,128)S(1)}, u32[]{:S(2)}, u32[]{:S(2)}) collective-permute-start(f32[64,1024]{1,0:T(8,128)S(1)} %slice.44), channel_id=1, source_target_pairs={{0,1},{1,0},{2,3},{3,2},{4,5},{5,4},{6,7},{7,6},{8,9},{9,8},{10,11... | collective-permute-start | bytes 786440 | tf_op jit(solution)/shard_map/ppermute | solution.py:389
  73.8 1.3 %collective-permute-start.13 = (f32[64,128]{1,0:T(8,128)S(1)}, f32[64,128]{1,0:T(8,128)S(1)}, u32[]{:S(2)}, u32[]{:S(2)}) collective-permute-start(f32[64,128]{1,0:T(8,128)S(1)} %get-tuple-element.14), channel_id=1, source_target_pairs={{0,1},{1,0},{2,3},{3,2},{4,5},{5,4},{6,7},{7,6},{8,9},{9,8},{10,11... | collective-permute-start | bytes 98312 | tf_op jit(solution)/shard_map/ppermute | solution.py:389
  75.1 3.9 %collective-permute-start.14 = (f32[64,128]{1,0:T(8,128)S(1)}, f32[64,128]{1,0:T(8,128)S(1)}, u32[]{:S(2)}, u32[]{:S(2)}) collective-permute-start(f32[64,128]{1,0:T(8,128)S(1)} %add.77.refs_0_), channel_id=1, source_target_pairs={{0,2},{2,0},{4,6},{6,4},{8,10},{10,8},{12,14},{14,12},{1,3},{3,1},... | collective-permute-start | bytes 98312 | tf_op jit(solution)/shard_map/ppermute | solution.py:386
  76.2 3.9 %collective-permute-start.15 = (f32[64,128]{1,0:T(8,128)S(1)}, f32[64,128]{1,0:T(8,128)S(1)}, u32[]{:S(2)}, u32[]{:S(2)}) collective-permute-start(f32[64,128]{1,0:T(8,128)S(1)} %add.77.refs_0_), channel_id=1, source_target_pairs={{0,4},{2,6},{4,0},{6,2},{8,12},{10,14},{12,8},{14,10},{1,5},{3,7},... | collective-permute-start | bytes 98312 | tf_op jit(solution)/shard_map/ppermute | solution.py:386
  77.2 4.8 %collective-permute-start.16 = (f32[64,128]{1,0:T(8,128)S(1)}, f32[64,128]{1,0:T(8,128)S(1)}, u32[]{:S(2)}, u32[]{:S(2)}) collective-permute-start(f32[64,128]{1,0:T(8,128)S(1)} %add.77.refs_0_), channel_id=1, source_target_pairs={{0,6},{2,4},{4,2},{6,0},{8,14},{10,12},{12,10},{14,8},{1,7},{3,5},... | collective-permute-start | bytes 98312 | tf_op jit(solution)/shard_map/ppermute | solution.py:386

commit v2 on v1

--- a/solution.py
+++ b/solution.py
@@ -10,6 +10,7 @@
 ITERS = 2
 GROUP = 4
 LOW = 256
+FEATURES = 48
 STORED_LIMIT = 32 * 2**20
 
 soft_square = 0.09
@@ -117,21 +118,18 @@
 
 def position_kernel(starts, table_ref, owner_ref, offset_ref, out_ref, parts_ref, *, chunk, count, rows):
     for part, value in enumerate(three_parts(table_ref[...])):
-        parts_ref[part * 3 * rows : (part + 1) * 3 * rows, :] = value
+        parts_ref[:, part * LOW : (part + 1) * LOW] = value
 
     def one(j, carry):
         first = pl.multiple_of(starts[j], chunk)
         at = pl.multiple_of(j * chunk, chunk)
         owner = owner_ref[:, pl.ds(first, chunk)]
         low = lax.broadcasted_iota(jnp.int32, (LOW, chunk), 0) == (owner & (LOW - 1))
-        rows_of = jnp.dot(parts_ref[...], low.astype(jnp.bfloat16), preferred_element_type=jnp.float32)
+        low = low.astype(jnp.bfloat16)
+        rows_of = jnp.dot(parts_ref[...], jnp.concatenate([low] * 3, axis=0), preferred_element_type=jnp.float32)
         high = lax.broadcasted_iota(jnp.int32, (rows, chunk), 0) == (owner // LOW)
         for axis in range(3):
-            value = rows_of[axis * rows : (axis + 1) * rows]
-            for part in range(1, 3):
-                place = (part * 3 + axis) * rows
-                value = value + rows_of[place : place + rows]
-            base = jnp.sum(jnp.where(high, value, 0.0), axis=0, keepdims=True)
+            base = jnp.sum(jnp.where(high, rows_of[axis * rows : (axis + 1) * rows], 0.0), axis=0, keepdims=True)
             out_ref[axis : axis + 1, pl.ds(at, chunk)] = base + probe_radius * offset_ref[axis : axis + 1, pl.ds(first, chunk)]
         return carry
 
@@ -147,70 +145,91 @@
         out_shape=jax.ShapeDtypeStruct((3, count * chunk), jnp.float32),
         in_specs=[pl.BlockSpec(memory_space=pltpu.SMEM), whole, whole, whole],
         out_specs=whole,
-        scratch_shapes=[pltpu.VMEM((9 * rows, LOW), jnp.bfloat16)],
+        scratch_shapes=[pltpu.VMEM((3 * rows, 3 * LOW), jnp.bfloat16)],
         compiler_params=params(24),
         cost_estimate=pl.CostEstimate(flops=2 * 9 * rows * LOW * count * chunk, bytes_accessed=4 * 40000 * 3, transcendentals=0),
         name="positions",
     )(starts, table, owner, offsets)
 
 
-def entry_kernel(source_ref, target_ref, out_ref):
-    dist_sq = None
-    for axis in range(3):
-        diff = source_ref[:, axis : axis + 1] - target_ref[axis : axis + 1, :]
-        dist_sq = diff * diff if dist_sq is None else dist_sq + diff * diff
-    out_ref[...] = lax.rsqrt(dist_sq + soft_square).astype(jnp.bfloat16)
-
-
-def entries(source_pos, target_pos):
-    n, m = source_pos.shape[0], target_pos.shape[1]
-    step = 256
+def features(pos, source):
+    axes = [pos[axis : axis + 1] for axis in range(3)]
+    square = axes[0] * axes[0] + axes[1] * axes[1] + axes[2] * axes[2]
+    one = jnp.ones_like(square).astype(jnp.bfloat16)
+    rows = []
+    for value in axes:
+        parts = three_parts(-2.0 * value if source else value)
+        pairs = [(0, 0), (0, 1), (1, 0), (0, 2), (1, 1), (2, 0), (1, 2), (2, 1), (2, 2)]
+        rows += [parts[pair[0] if source else pair[1]] for pair in pairs]
+    if source:
+        rows += [*three_parts(square), one, one, one]
+    else:
+        rows += [one, one, one, *three_parts(square + soft_square)]
+    rows += [jnp.zeros_like(one)] * (FEATURES - len(rows))
+    return jnp.concatenate(rows, axis=0)
+
+
+def entry_kernel(source_ref, target_ref, *refs):
+    out_refs, (source_rows, target_cols) = refs[:-2], refs[-2:]
+    n = source_ref.shape[1]
+    source_rows[...] = features(source_ref[...], True).T
+    target_cols[...] = features(target_ref[...], False)
+    n_out, m = out_refs[0].shape
+    step, wide = 512, min(m, 1024)
+    for piece, out_ref in enumerate(out_refs):
+
+        def one(i, carry, piece=piece, out_ref=out_ref):
+            at = pl.multiple_of(i * step, step)
+            rows = source_rows[pl.ds(piece * n_out + at, step), :]
+            for j in range(0, m, wide):
+                dist_sq = jnp.dot(rows, target_cols[:, j : j + wide], preferred_element_type=jnp.float32)
+                out_ref[pl.ds(at, step), j : j + wide] = lax.rsqrt(dist_sq).astype(jnp.bfloat16)
+            return carry
+
+        lax.fori_loop(0, n_out // step, one, 0)
+
+
+def entries(source_pos, target_pos, pieces):
+    n, m = source_pos.shape[1], target_pos.shape[1]
+    whole = pl.BlockSpec(memory_space=pltpu.VMEM)
     return pl.pallas_call(
         entry_kernel,
-        grid=(n // step,),
-        out_shape=jax.ShapeDtypeStruct((n, m), jnp.bfloat16),
-        in_specs=[pl.BlockSpec((step, 3), lambda i: (i, 0)), pl.BlockSpec((3, m), lambda i: (0, 0))],
-        out_specs=pl.BlockSpec((step, m), lambda i: (i, 0)),
-        compiler_params=params(16),
+        out_shape=[jax.ShapeDtypeStruct((n // pieces, m), jnp.bfloat16)] * pieces,
+        in_specs=[whole, whole],
+        out_specs=[whole] * pieces,
+        scratch_shapes=[pltpu.VMEM((n, FEATURES), jnp.bfloat16), pltpu.VMEM((FEATURES, m), jnp.bfloat16)],
+        compiler_params=params(32),
         cost_estimate=pl.CostEstimate(flops=12 * n * m, bytes_accessed=2 * n * m, transcendentals=n * m),
         name="entries",
     )(source_pos, target_pos)
 
 
-def apply_kernel(*refs, pieces, per):
-    charge_refs, kern_ref, out_ref = refs[:pieces], refs[pieces], refs[pieces + 1]
-    j = pl.program_id(0)
-
-    @pl.when(j == 0)
-    def _():
-        out_ref[...] = jnp.zeros_like(out_ref)
-
-    for piece in range(pieces):
-        for part in range(per):
-
-            @pl.when(j == piece * per + part)
-            def _(piece=piece, part=part):
-                step = kern_ref.shape[0]
-                charges = charge_refs[piece][:, part * step : (part + 1) * step]
-                out_ref[...] += jnp.dot(charges, kern_ref[...], preferred_element_type=jnp.float32)
-
-
-def apply_entries(charges, kern):
+def apply_kernel(*refs, pieces, more):
+    charge_refs, kern_refs, out_ref = refs[:pieces], refs[pieces : 2 * pieces], refs[-1]
+    wide = 512
+    for j in range(0, out_ref.shape[1], wide):
+        total = refs[2 * pieces][:, j : j + wide] if more else None
+        for charge_ref, kern_ref in zip(charge_refs, kern_refs):
+            part = jnp.dot(charge_ref[...], kern_ref[:, j : j + wide], preferred_element_type=jnp.float32)
+            total = part if total is None else total + part
+        out_ref[:, j : j + wide] = total
+
+
+def apply_entries(charges, kerns, total=None):
     pieces = len(charges)
     k, n = charges[0].shape
-    m = kern.shape[1]
-    step = 512
-    per = n // step
-    return pl.pallas_call(
-        functools.partial(apply_kernel, pieces=pieces, per=per),
-        grid=(pieces * per,),
+    m = kerns[0].shape[1]
+    whole = pl.BlockSpec(memory_space=pltpu.VMEM)
+    more = [] if total is None else [total]
+    return pl.pallas_call(
+        functools.partial(apply_kernel, pieces=pieces, more=bool(more)),
         out_shape=jax.ShapeDtypeStruct((k, m), jnp.float32),
-        in_specs=[pl.BlockSpec((k, n), lambda j: (0, 0))] * pieces + [pl.BlockSpec((step, m), lambda j: (j, 0))],
-        out_specs=pl.BlockSpec((k, m), lambda j: (0, 0)),
-        compiler_params=params(24),
-        cost_estimate=pl.CostEstimate(flops=2 * k * n * pieces * m, bytes_accessed=2 * pieces * n * m, transcendentals=0),
+        in_specs=[whole] * (2 * pieces + len(more)),
+        out_specs=whole,
+        compiler_params=params(32),
+        cost_estimate=pl.CostEstimate(flops=8 * k * n * pieces * m, bytes_accessed=2 * pieces * n * m, transcendentals=0),
         name="apply",
-    )(*charges, kern)
+    )(*charges, *kerns, *more)
 
 
 def dots(left, right):
@@ -223,16 +242,44 @@
 
 def mul(left, right):
     return jnp.dot(left, right, precision=HIGHEST, preferred_element_type=jnp.float32)
+
+
+def inverse_of_pair(a, b, c):
+    scale = 1.0 / (a * c - b * b)
+    return c * scale, -b * scale, a * scale
+
+
+def eliminate_four(system, i, row_of):
+    col = [jnp.broadcast_to(system[:, i + j : i + j + 1], system.shape) for j in range(4)]
+    row = [system[i + j : i + j + 1, :] for j in range(4)]
+
+    def entry(r, c):
+        return col[c][i + r : i + r + 1]
+
+    a, b, d = inverse_of_pair(entry(0, 0), entry(1, 0), entry(1, 1))
+    t0, t1 = a * row[0] + b * row[1], b * row[0] + d * row[1]
+    b00, b01, b10, b11 = entry(2, 0), entry(3, 0), entry(2, 1), entry(3, 1)
+    e00, e10 = a * b00 + b * b10, b * b00 + d * b10
+    e01, e11 = a * b01 + b * b11, b * b01 + d * b11
+    u, v, w = inverse_of_pair(
+        entry(2, 2) - (b00 * e00 + b10 * e10),
+        entry(3, 2) - (b00 * e01 + b10 * e11),
+        entry(3, 3) - (b01 * e01 + b11 * e11),
+    )
+    y0, y1 = row[2] - (b00 * t0 + b10 * t1), row[3] - (b01 * t0 + b11 * t1)
+    q2, q3 = u * y0 + v * y1, v * y0 + w * y1
+    solved = [t0 - (e00 * q2 + e01 * q3), t1 - (e10 * q2 + e11 * q3), q2, q3]
+    rest = (system - (col[0] * solved[0] + col[1] * solved[1])) - (col[2] * solved[2] + col[3] * solved[3])
+    for j in range(4):
+        rest = jnp.where(row_of == i + j, solved[j], rest)
+    return rest
 
 
 def eliminate(systems):
     k = systems[0].shape[0]
     row_of = lax.broadcasted_iota(jnp.int32, systems[0].shape, 0)
-    systems = list(systems)
-    for i in range(k):
-        for s, system in enumerate(systems):
-            row = system[i : i + 1, :] / system[i : i + 1, i : i + 1]
-            systems[s] = jnp.where(row_of == i, row, system - system[:, i : i + 1] * row)
+    for i in range(0, k, 4):
+        systems = [eliminate_four(system, i, row_of) for system in systems]
     return [system[:, k:] for system in systems]
 
 
@@ -273,7 +320,7 @@
 
 
 def first_update_kernel(*refs, count):
-    part_refs, (image_ref, direction_ref, alpha_ref, residual_ref, next_ref, charges_ref) = refs[:count], refs[count:]
+    part_refs, (image_ref, direction_ref, alpha_ref, next_ref, charges_ref) = refs[:count], refs[count:]
     total = sum_of([ref[...] for ref in part_refs])
     k = total.shape[1] // 2
     gram, image_sq, norm = total[:k, :k], total[:k, k:], unfold(total[k:, :])
@@ -283,15 +330,15 @@
         jnp.concatenate([0.5 * (gram + gram.T), norm], axis=1),
         jnp.concatenate([norm, unit], axis=1),
     ])
-    cross = mul(gram, alpha)
-    norm_next = norm - cross - cross.T + left_t(alpha, mul(image_sq, alpha))
+    both = mul(jnp.concatenate([gram, image_sq], axis=0), alpha)
+    cross = both[:k]
+    norm_next = norm - cross - cross.T + left_t(alpha, both[k:])
     beta = mul(inverse, norm_next)
     alpha_ref[:, :k] = alpha
     alpha_ref[:, k:] = norm_next
     direction = direction_ref[...]
-    residual = direction - left_t(alpha, image_ref[...])
-    residual_ref[...] = residual
-    later = residual + left_t(beta, direction)
+    weights = jnp.concatenate([beta, -alpha], axis=0)
+    later = direction + left_t(weights, jnp.concatenate([direction, image_ref[...]], axis=0))
     next_ref[...] = later
     charges_ref[...] = later.astype(jnp.bfloat16)
 
@@ -310,11 +357,10 @@
         out_shape=[
             jax.ShapeDtypeStruct((k, 2 * k), jnp.float32),
             jax.ShapeDtypeStruct((k, n), jnp.float32),
-            jax.ShapeDtypeStruct((k, n), jnp.float32),
             jax.ShapeDtypeStruct((k, n), jnp.bfloat16),
         ],
         in_specs=[whole] * (len(parts) + 2),
-        out_specs=[whole] * 4,
+        out_specs=[whole] * 3,
         compiler_params=params(16),
         cost_estimate=pl.CostEstimate(flops=6 * 2 * 2 * k * k * n, bytes_accessed=4 * k * n * 5, transcendentals=0),
         name="first_update",
@@ -346,29 +392,53 @@
     )(partial, other, self_row, direction)
 
 
+def first_state_kernel(alpha_ref, direction_ref, image_ref, out_ref):
+    k, n = direction_ref.shape
+    alpha = alpha_ref[:, :k]
+    both = left_t(alpha, jnp.concatenate([direction_ref[...], image_ref[...]], axis=1))
+    out_ref[:, :n] = both[:, :n]
+    out_ref[:, n:] = direction_ref[...] - both[:, n:]
+
+
+def first_state(alpha, direction, image):
+    k, n = direction.shape
+    whole = pl.BlockSpec(memory_space=pltpu.VMEM)
+    return pl.pallas_call(
+        first_state_kernel,
+        out_shape=jax.ShapeDtypeStruct((k, 2 * n), jnp.float32),
+        in_specs=[whole] * 3,
+        out_specs=whole,
+        compiler_params=params(16),
+        cost_estimate=pl.CostEstimate(flops=6 * 2 * 2 * k * k * n, bytes_accessed=4 * k * n * 4, transcendentals=0),
+        name="first_state",
+    )(alpha, direction, image)
+
+
 def last_update_kernel(*refs, count):
     part_refs = refs[:count]
-    alpha_ref, first_ref, residual_ref, direction_ref, image_ref, charge_ref, out_ref = refs[count:]
+    alpha_ref, state_ref, direction_ref, image_ref, charge_ref, out_ref = refs[count:]
     total = sum_of([ref[...] for ref in part_refs])
     k = total.shape[0]
+    n = direction_ref.shape[1]
     gram = total[:, :k]
     (alpha,) = eliminate([jnp.concatenate([0.5 * (gram + gram.T), alpha_ref[:, k:]], axis=1)])
-    charge_ref[...] = left_t(alpha_ref[:, :k], first_ref[...]) + left_t(alpha, direction_ref[...])
-    out_ref[...] = residual_ref[...] - left_t(alpha, image_ref[...])
-
-
-def last_update(parts, alpha, first, residual, direction, image):
-    k, n = first.shape
+    both = left_t(alpha, jnp.concatenate([direction_ref[...], image_ref[...]], axis=1))
+    charge_ref[...] = state_ref[:, :n] + both[:, :n]
+    out_ref[...] = state_ref[:, n:] - both[:, n:]
+
+
+def last_update(parts, alpha, state, direction, image):
+    k, n = direction.shape
     whole = pl.BlockSpec(memory_space=pltpu.VMEM)
     return pl.pallas_call(
         functools.partial(last_update_kernel, count=len(parts)),
         out_shape=[jax.ShapeDtypeStruct((k, n), jnp.float32)] * 2,
-        in_specs=[whole] * (len(parts) + 5),
+        in_specs=[whole] * (len(parts) + 4),
         out_specs=[whole] * 2,
         compiler_params=params(16),
         cost_estimate=pl.CostEstimate(flops=6 * 3 * 2 * k * k * n, bytes_accessed=4 * k * n * 6, transcendentals=0),
         name="last_update",
-    )(*parts, alpha, first, residual, direction, image)
+    )(*parts, alpha, state, direction, image)
 
 
 def per_device_grouped(right_side, atom_centers, tessera_owner, tessera_angles, self_term):
@@ -388,7 +458,7 @@
     def swap_core(value):
         return lax.ppermute(value, "src", [(0, 1), (1, 0)])
 
-    near = jnp.concatenate([right_side, jnp.broadcast_to(self_term[None, :], (8, shard))], axis=0)
+    near = jnp.concatenate([right_side, self_term[None, :]], axis=0)
     far = swap(near, GROUP)
     both = jnp.where(ours == 0, jnp.concatenate([near, far], axis=1), jnp.concatenate([far, near], axis=1))
     direction, self_row = both[:columns], both[columns : columns + 1]
@@ -396,32 +466,34 @@
     gathered = [charges] + [swap(charges, bits) for bits in range(1, GROUP)]
 
     table = jnp.pad(atom_centers, ((0, 0), (0, -atom_centers.shape[1] % (LOW * 8)))).reshape(-1, LOW)
-    offsets = unit_offsets(tessera_angles.reshape(2, -1, 128)).reshape(3, -1)
+    angles = lax.optimization_barrier(tessera_angles.reshape(2, -1, 128))
+    offsets = lax.optimization_barrier(unit_offsets(angles)).reshape(3, -1)
     starts = [((member ^ bits) + GROUP * c) * width + s * shard for bits in range(GROUP) for c in range(copies)]
     starts += [(member + GROUP * c) * width + (1 - s) * shard for c in range(copies)]
     pos = chosen_positions(table, tessera_owner[None, :], offsets, jnp.stack(starts).astype(jnp.int32), shard)
     n_near = copies * shard
     n_all = GROUP * n_near
     target_pos = jnp.concatenate([pos[:, :n_near], pos[:, n_all:]], axis=1)
-    kern = entries(pos[:, :n_all].T, target_pos)
+    kerns = entries(pos[:, :n_all], target_pos, GROUP)
 
     def group_sum_parts(value):
         value = value + swap_core(value)
         return [value] + [swap(value, bits) for bits in range(1, GROUP)]
 
-    partial = apply_entries(gathered, kern)
-    image, gram = first_gram(partial, swap_core(partial[:, n_near:]), self_row, direction)
-    alpha, residual, later, charges = first_update(group_sum_parts(gram), image, direction)
-
-    gathered = [charges] + [swap(charges, bits) for bits in range(1, GROUP)]
-    partial = apply_entries(gathered, kern)
-    image, gram = second_gram(partial, swap_core(partial[:, n_near:]), self_row, later)
-    parts = group_sum_parts(gram)
-
     def mine(value):
         return lax.dynamic_slice_in_dim(value, ours * shard, shard, 1)
 
-    return tuple(last_update(parts, alpha, right_side, mine(residual), mine(later), mine(image)))
+    partial = apply_entries(gathered, kerns)
+    image, gram = first_gram(partial, swap_core(partial[:, n_near:]), self_row, direction)
+    alpha, later, charges = first_update(group_sum_parts(gram), image, direction)
+
+    gathered = [swap(charges, bits) for bits in range(1, GROUP)]
+    partial = apply_entries([charges], kerns[:1])
+    for piece, kern in zip(gathered, kerns[1:]):
+        partial = apply_entries([piece], [kern], partial)
+    state = first_state(alpha, right_side, mine(image))
+    image, gram = second_gram(partial, swap_core(partial[:, n_near:]), self_row, later)
+    return tuple(last_update(group_sum_parts(gram), alpha, state, mine(later), mine(image)))
 
 
 def solution(mesh):

time: 89.1 us -> 68.4 us (0.77)
  Pallas kernels: 43.3 us -> 29.2 us
  waiting for transfers between devices: 18 us -> 14.4 us
  other arithmetic: 3.77 us -> 1.23 us
    pallas_call x3 -> x7, Pallas kernels: 22 us -> 13.4 us  [the longest x1 6.54 us: entries(): pl.pallas_call(entry_kernel, out_shape=[jax.ShapeDtypeStruct((n // pieces...]
    pallas_call x1, Pallas kernels: 6.73 us -> 3.52 us  [last_update(): pl.pallas_call(functools.partial(last_update_kernel, count=len(parts)), o...]
    ppermute x13, waiting for transfers between devices: 12.9 us -> 9.72 us  [swap(): return lax.ppermute(value, 'tgt', [(i, i ^ bits) for i in range(n_tgt)])]
    mul x1, other arithmetic: 2.72 us -> 0.24 us  [unit_offsets(): jnp.cos(azimuth) * sine]
    pallas_call x1, Pallas kernels: 7.01 us -> 4.68 us  [first_update(): pl.pallas_call(functools.partial(first_update_kernel, count=len(parts)),...]
    unnamed x4 -> x8, local copies, waits for them, and re-layouts: 0.77 us -> 1.68 us
  transfers between devices with their start and end apart: 17 -> 17, of which waited for: 13 -> 13; matrix products, arithmetic and copies ran while one was open for 6% -> 4% of each run, Pallas kernels for 23% -> 23%
where the time goes in v2:
time: 68.4 us; the launch traced here: 68.1 us
  Pallas kernels  29.2 us (43%)
  starting transfers between devices  18.9 us (28%)
  waiting for transfers between devices  14.4 us (21%)
  local copies, waits for them, and re-layouts  3.47 us (5%)
  other arithmetic  1.23 us (2%)
  between operations  0.92 us (1%)
    ppermute x13, starting transfers between devices, swap(): return lax.ppermute(value, 'tgt', [(i, i ^ bits) for i in range(n_tgt)])  18.3 us
    ppermute x13, waiting for transfers between devices, swap(): return lax.ppermute(value, 'tgt', [(i, i ^ bits) for i in range(n_tgt)])  9.72 us
    pallas_call x1, Pallas kernels, entries(): pl.pallas_call(entry_kernel, out_shape=[jax.ShapeDtypeStruct((n // pieces...  6.54 us
    pallas_call x5, Pallas kernels, apply_entries(): pl.pallas_call(functools.partial(apply_kernel, pieces=pieces, more=bool(m...  6.4 us
    pallas_call x1, Pallas kernels, chosen_positions(): pl.pallas_call(functools.partial(position_kernel, chunk=chunk, count=coun...  6.38 us
    ppermute x4, waiting for transfers between devices, swap_core(): return lax.ppermute(value, 'src', [(0, 1), (1, 0)])  4.7 us
    pallas_call x1, Pallas kernels, first_update(): pl.pallas_call(functools.partial(first_update_kernel, count=len(parts)),...  4.68 us
    pallas_call x1, Pallas kernels, last_update(): pl.pallas_call(functools.partial(last_update_kernel, count=len(parts)), o...  3.52 us
  transfers between devices with their start and end apart: 17, of which 13 were waited for; matrix products, arithmetic and copies ran while one was open for 4% of the time, Pallas kernels for 23%

profile of v2, /device:TPU:0, one launch (start us, length us, event | category | flops | bytes accessed | tf_op | source)
XLA Modules:
  0.0 68.1 jit_solution(14517836779442201769)
XLA Ops:
  0.6 0.9 %pad_maximum_fusion = f32[65,512]{1,0:T(8,128)S(1)} fusion(f32[1,512]{1,0:T(1,128)} %bitcast.25, f32[64,512]{1,0:T(8,128)} %direction_ref.1), kind=kLoop, calls=%fused_computation.1 | loop fusion | flops 33280 | bytes 266240 | tf_op jit(solution)/shard_map/concatenate | solution.py:461
  1.6 4.1 %collective-permute-start = (f32[65,512]{1,0:T(8,128)S(1)}, f32[65,512]{1,0:T(8,128)S(1)}, u32[]{:S(2)}, u32[]{:S(2)}) collective-permute-start(f32[65,512]{1,0:T(8,128)S(1)} %pad_maximum_fusion), channel_id=1, source_target_pairs={{0,8},{2,10},{4,12},{6,14},{8,0},{10,2},{12,4},{14,6},{1,9},{3,11}... | collective-permute-start | bytes 399368 | tf_op jit(solution)/shard_map/ppermute | solution.py:456
  5.7 0.8 %copy.12 = f32[1,2,64,128]{3,2,1,0:T(8,128)S(1)} copy(f32[1,2,64,128]{3,1,2,0:T(2,128)} %bitcast.24) | data formatting | bytes 131072
  6.5 0.2 cosine_multiply_fusion
  6.8 0.1 copy.11
  6.8 1.2 %pad.4 = f32[3,40960]{1,0:T(4,128)S(1)} pad(f32[3,40000]{1,0:T(4,128)} %param.6, f32[]{:T(128)} %constant.43.clone.1), padding=0_0x0_960 | pad | bytes 971524 | tf_op jit(solution)/shard_map/jit(_pad)/pad | solution.py:468
  8.1 0.4 reshape.13.table_ref
  8.4 0.1 stack.49.starts
  8.5 0.0 copy-start.1
  8.5 0.8 %copy-done.1 = s32[8192]{0:T(1024)S(1)} copy-done((s32[8192]{0:T(1024)S(1)}, s32[8192]{0:T(1024)}, u32[]{:S(2)}) %copy-start.1) | copy-done | bytes 32792
  9.3 0.0 copy-start
  9.3 0.0 copy-start.2
  9.3 6.4 %positions.1 = f32[3,5120]{1,0:T(4,128)S(1)} custom-call(s32[10]{0:T(128)S(1)} %stack.49.starts, f32[480,256]{1,0:T(8,128)S(1)} %reshape.13.table_ref, s32[1,8192]{1,0:T(1,128)S(1)} %bitcast.21, f32[3,8192]{1,0:T(4,128)S(1)} %bitcast.20), custom_call_target="tpu_custom_call" | custom-call | flops 3774873600 | bytes 480000 | tf_op jit(solution)/shard_map/positions/pallas_call | solution.py:143
  15.7 0.0 collective-permute-done
  15.7 0.0 copy-done
  15.7 0.0 copy-done.2
  15.8 2.6 %collective-permute-start.3 = (bf16[64,1024]{1,0:T(8,128)(2,1)S(1)}, bf16[64,1024]{1,0:T(8,128)(2,1)S(1)}, u32[]{:S(2)}, u32[]{:S(2)}) collective-permute-start(bf16[64,1024]{1,0:T(8,128)(2,1)S(1)} %slice.54.refs_0_), channel_id=1, source_target_pairs={{0,6},{2,4},{4,2},{6,0},{8,14},{10,12},{12,10},{14,8},{1,7},{3,5},... | collective-permute-start | bytes 393224 | tf_op jit(solution)/shard_map/ppermute | solution.py:456
  18.4 0.4 collective-permute-start.2
  18.8 0.5 collective-permute-start.1
  19.4 6.5 %entries.1 = (bf16[1024,2048]{1,0:T(8,128)(2,1)S(1)}, bf16[1024,2048]{1,0:T(8,128)(2,1)S(1)}, bf16[1024,2048]{1,0:T(8,128)(2,1)S(1)}, bf16[1024,2048]{1,0:T(8,128)(2,1)S(1)}) custom-call(f32[3,4096]{1,0:T(4,128)S(1)} %slice.39.source_ref, f32[3,2048]{1,0:T(4,128)S(1)} %pad_maximum_fusion.2.target_ref), custom_call_target="tpu_custom_call" | custom-call | flops 100663296 | bytes 16777216 | tf_op jit(solution)/shard_map/entries/pallas_call | solution.py:195
  25.9 0.0 collective-permute-done.3.refs_3_
  25.9 0.0 collective-permute-done.2.refs_2_
  25.9 0.0 collective-permute-done.1.refs_1_
  25.9 3.0 %apply.5.own_ref = f32[64,2048]{1,0:T(8,128)S(1)} custom-call(bf16[64,1024]{1,0:T(8,128)(2,1)S(1)} %slice.54.refs_0_, bf16[64,1024]{1,0:T(8,128)(2,1)S(1)} %collective-permute-done.1.refs_1_, bf16[64,1024]{1,0:T(8,128)(2,1)S(1)} %collective-permute-done.2.refs_2_, bf16[64,1024]{1,0:T(8,128)(2,1)S(1)} %collective-permute-done.3.refs_3_, ...), custom_call_target="tpu_custom_call" | custom-call | flops 4294967296 | bytes 16777216 | tf_op jit(solution)/shard_map/apply/pallas_call | solution.py:224
  29.0 0.1 collective-permute-start.4
  29.1 1.5 %collective-permute-done.4.other_ref = f32[64,1024]{1,0:T(8,128)S(1)} collective-permute-done((f32[64,1024]{1,0:T(8,128)S(1)}, f32[64,1024]{1,0:T(8,128)S(1)}, u32[]{:S(2)}, u32[]{:S(2)}) %collective-permute-start.4) | collective-permute-done | bytes 262176 | tf_op jit(solution)/shard_map/ppermute | solution.py:459
  30.6 0.9 %first_gram.1 = (f32[64,1024]{1,0:T(8,128)S(1)}, f32[96,128]{1,0:T(8,128)S(1)}) custom-call(f32[64,2048]{1,0:T(8,128)S(1)} %apply.5.own_ref, f32[64,1024]{1,0:T(8,128)S(1)} %collective-permute-done.4.other_ref, f32[1,1024]{1,0:T(1,128)S(1)} %slice.43.self_ref, f32[64,1024]{1,0:T(8,128)S(1)} %slice.36.direction_ref.refs_5_), custom_call_target="tpu_custom_call" | custom-call | flops 150994944 | bytes 1048576 | tf_op jit(solution)/shard_map/first_gram/pallas_call | solution.py:310
  31.5 0.2 collective-permute-start.5
  31.7 1.1 %collective-permute-done.5 = f32[96,128]{1,0:T(8,128)S(1)} collective-permute-done((f32[96,128]{1,0:T(8,128)S(1)}, f32[96,128]{1,0:T(8,128)S(1)}, u32[]{:S(2)}, u32[]{:S(2)}) %collective-permute-start.5) | collective-permute-done | bytes 49184 | tf_op jit(solution)/shard_map/ppermute | solution.py:459
  32.8 2.6 %collective-permute-start.8 = (f32[96,128]{1,0:T(8,128)S(1)}, f32[96,128]{1,0:T(8,128)S(1)}, u32[]{:S(2)}, u32[]{:S(2)}) collective-permute-start(f32[96,128]{1,0:T(8,128)S(1)} %add.76.refs_0_), channel_id=1, source_target_pairs={{0,6},{2,4},{4,2},{6,0},{8,14},{10,12},{12,10},{14,8},{1,7},{3,5},... | collective-permute-start | bytes 147464 | tf_op jit(solution)/shard_map/ppermute | solution.py:456
  35.4 0.5 collective-permute-start.7
  35.8 0.5 collective-permute-start.6
  36.3 1.6 %collective-permute-done.8.refs_3_ = f32[96,128]{1,0:T(8,128)S(1)} collective-permute-done((f32[96,128]{1,0:T(8,128)S(1)}, f32[96,128]{1,0:T(8,128)S(1)}, u32[]{:S(2)}, u32[]{:S(2)}) %collective-permute-start.8) | collective-permute-done | bytes 49184 | tf_op jit(solution)/shard_map/ppermute | solution.py:456
  38.0 1.5 %collective-permute-done.7.refs_2_ = f32[96,128]{1,0:T(8,128)S(1)} collective-permute-done((f32[96,128]{1,0:T(8,128)S(1)}, f32[96,128]{1,0:T(8,128)S(1)}, u32[]{:S(2)}, u32[]{:S(2)}) %collective-permute-start.7) | collective-permute-done | bytes 49184 | tf_op jit(solution)/shard_map/ppermute | solution.py:456
  39.4 0.5 collective-permute-done.6.refs_1_
  39.9 4.7 %first_update.1 = (f32[64,128]{1,0:T(8,128)S(1)}, f32[64,1024]{1,0:T(8,128)S(1)}, bf16[64,1024]{1,0:T(8,128)(2,1)S(1)}) custom-call(f32[96,128]{1,0:T(8,128)S(1)} %add.76.refs_0_, f32[96,128]{1,0:T(8,128)S(1)} %collective-permute-done.6.refs_1_, f32[96,128]{1,0:T(8,128)S(1)} %collective-permute-done.7.refs_2_, f32[96,128]{1,0:T(8,128)S(1)} %collective-permute-done.8.refs_3_, ...), custom_call_target="tpu_custom_call" | custom-call | flops 100663296 | bytes 1310720 | tf_op jit(solution)/shard_map/first_update/pallas_call | solution.py:355
  44.6 0.6 collective-permute-start.11
  45.2 1.6 %collective-permute-start.10 = (bf16[64,1024]{1,0:T(8,128)(2,1)S(1)}, bf16[64,1024]{1,0:T(8,128)(2,1)S(1)}, u32[]{:S(2)}, u32[]{:S(2)}) collective-permute-start(bf16[64,1024]{1,0:T(8,128)(2,1)S(1)} %get-tuple-element.19.refs_0_), channel_id=1, source_target_pairs={{0,4},{2,6},{4,0},{6,2},{8,12},{10,14},{12,8},{14,10},{1,5},{3,7},... | collective-permute-start | bytes 393224 | tf_op jit(solution)/shard_map/ppermute | solution.py:456
  46.7 0.8 %apply.6.refs_2_ = f32[64,2048]{1,0:T(8,128)S(1)} custom-call(bf16[64,1024]{1,0:T(8,128)(2,1)S(1)} %get-tuple-element.19.refs_0_, bf16[1024,2048]{1,0:T(8,128)(2,1)S(1)} %get-tuple-element.13.refs_4_.refs_1_), custom_call_target="tpu_custom_call" | custom-call | flops 1073741824 | bytes 4194304 | tf_op jit(solution)/shard_map/apply/pallas_call | solution.py:224
  47.6 1.5 %collective-permute-start.9 = (bf16[64,1024]{1,0:T(8,128)(2,1)S(1)}, bf16[64,1024]{1,0:T(8,128)(2,1)S(1)}, u32[]{:S(2)}, u32[]{:S(2)}) collective-permute-start(bf16[64,1024]{1,0:T(8,128)(2,1)S(1)} %get-tuple-element.19.refs_0_), channel_id=1, source_target_pairs={{0,6},{2,4},{4,2},{6,0},{8,14},{10,12},{12,10},{14,8},{1,7},{3,5},... | collective-permute-start | bytes 393224 | tf_op jit(solution)/shard_map/ppermute | solution.py:456
  49.1 0.6 collective-permute-done.11.refs_0_
  49.6 0.8 %apply.7.refs_2_ = f32[64,2048]{1,0:T(8,128)S(1)} custom-call(bf16[64,1024]{1,0:T(8,128)(2,1)S(1)} %collective-permute-done.11.refs_0_, bf16[1024,2048]{1,0:T(8,128)(2,1)S(1)} %get-tuple-element.14.refs_5_.refs_1_, f32[64,2048]{1,0:T(8,128)S(1)} %apply.6.refs_2_), custom_call_target="tpu_custom_call" | custom-call | flops 1073741824 | bytes 4194304 | tf_op jit(solution)/shard_map/apply/pallas_call | solution.py:224
  50.5 0.4 collective-permute-done.10.refs_0_
  50.9 0.8 %apply.8.refs_2_ = f32[64,2048]{1,0:T(8,128)S(1)} custom-call(bf16[64,1024]{1,0:T(8,128)(2,1)S(1)} %collective-permute-done.10.refs_0_, bf16[1024,2048]{1,0:T(8,128)(2,1)S(1)} %get-tuple-element.15.refs_6_.refs_1_, f32[64,2048]{1,0:T(8,128)S(1)} %apply.7.refs_2_), custom_call_target="tpu_custom_call" | custom-call | flops 1073741824 | bytes 4194304 | tf_op jit(solution)/shard_map/apply/pallas_call | solution.py:224
  51.7 2.0 %collective-permute-done.9.refs_0_ = bf16[64,1024]{1,0:T(8,128)(2,1)S(1)} collective-permute-done((bf16[64,1024]{1,0:T(8,128)(2,1)S(1)}, bf16[64,1024]{1,0:T(8,128)(2,1)S(1)}, u32[]{:S(2)}, u32[]{:S(2)}) %collective-permute-start.9) | collective-permute-done | bytes 131104 | tf_op jit(solution)/shard_map/ppermute | solution.py:456
  53.8 0.8 %apply.9.own_ref = f32[64,2048]{1,0:T(8,128)S(1)} custom-call(bf16[64,1024]{1,0:T(8,128)(2,1)S(1)} %collective-permute-done.9.refs_0_, bf16[1024,2048]{1,0:T(8,128)(2,1)S(1)} %get-tuple-element.16.refs_7_.refs_1_, f32[64,2048]{1,0:T(8,128)S(1)} %apply.8.refs_2_), custom_call_target="tpu_custom_call" | custom-call | flops 1073741824 | bytes 4194304 | tf_op jit(solution)/shard_map/apply/pallas_call | solution.py:224
  54.7 0.1 collective-permute-start.12
  54.8 1.5 %collective-permute-done.12.other_ref = f32[64,1024]{1,0:T(8,128)S(1)} collective-permute-done((f32[64,1024]{1,0:T(8,128)S(1)}, f32[64,1024]{1,0:T(8,128)S(1)}, u32[]{:S(2)}, u32[]{:S(2)}) %collective-permute-start.12) | collective-permute-done | bytes 262176 | tf_op jit(solution)/shard_map/ppermute | solution.py:459
  56.3 0.4 second_gram.1
  56.7 0.2 collective-permute-start.13
  56.9 0.4 first_state.1.refs_5_
  57.3 0.6 collective-permute-done.13
  57.9 1.1 %collective-permute-start.16 = (f32[64,128]{1,0:T(8,128)S(1)}, f32[64,128]{1,0:T(8,128)S(1)}, u32[]{:S(2)}, u32[]{:S(2)}) collective-permute-start(f32[64,128]{1,0:T(8,128)S(1)} %add.77.refs_0_), channel_id=1, source_target_pairs={{0,6},{2,4},{4,2},{6,0},{8,14},{10,12},{12,10},{14,8},{1,7},{3,5},... | collective-permute-start | bytes 98312 | tf_op jit(solution)/shard_map/ppermute | solution.py:456
  59.1 1.5 %collective-permute-start.15 = (f32[64,128]{1,0:T(8,128)S(1)}, f32[64,128]{1,0:T(8,128)S(1)}, u32[]{:S(2)}, u32[]{:S(2)}) collective-permute-start(f32[64,128]{1,0:T(8,128)S(1)} %add.77.refs_0_), channel_id=1, source_target_pairs={{0,4},{2,6},{4,0},{6,2},{8,12},{10,14},{12,8},{14,10},{1,5},{3,7},... | collective-permute-start | bytes 98312 | tf_op jit(solution)/shard_map/ppermute | solution.py:456
  60.6 0.8 %collective-permute-start.14 = (f32[64,128]{1,0:T(8,128)S(1)}, f32[64,128]{1,0:T(8,128)S(1)}, u32[]{:S(2)}, u32[]{:S(2)}) collective-permute-start(f32[64,128]{1,0:T(8,128)S(1)} %add.77.refs_0_), channel_id=1, source_target_pairs={{0,2},{2,0},{4,6},{6,4},{8,10},{10,8},{12,14},{14,12},{1,3},{3,1},... | collective-permute-start | bytes 98312 | tf_op jit(solution)/shard_map/ppermute | solution.py:456
  61.4 1.3 %collective-permute-done.16.refs_3_ = f32[64,128]{1,0:T(8,128)S(1)} collective-permute-done((f32[64,128]{1,0:T(8,128)S(1)}, f32[64,128]{1,0:T(8,128)S(1)}, u32[]{:S(2)}, u32[]{:S(2)}) %collective-permute-start.16) | collective-permute-done | bytes 32800 | tf_op jit(solution)/shard_map/ppermute | solution.py:456
  62.8 0.2 collective-permute-done.15.refs_2_
  63.0 1.5 %collective-permute-done.14.refs_1_ = f32[64,128]{1,0:T(8,128)S(1)} collective-permute-done((f32[64,128]{1,0:T(8,128)S(1)}, f32[64,128]{1,0:T(8,128)S(1)}, u32[]{:S(2)}, u32[]{:S(2)}) %collective-permute-start.14) | collective-permute-done | bytes 32800 | tf_op jit(solution)/shard_map/ppermute | solution.py:456
  64.5 3.5 %last_update.1 = (f32[64,512]{1,0:T(8,128)}, f32[64,512]{1,0:T(8,128)}) custom-call(f32[64,128]{1,0:T(8,128)S(1)} %add.77.refs_0_, f32[64,128]{1,0:T(8,128)S(1)} %collective-permute-done.14.refs_1_, f32[64,128]{1,0:T(8,128)S(1)} %collective-permute-done.15.refs_2_, f32[64,128]{1,0:T(8,128)S(1)} %collective-permute-done.16.refs_3_, ...), custom_call_target="tpu_custom_call" | custom-call | flops 75497472 | bytes 786432 | tf_op jit(solution)/shard_map/last_update/pallas_call | solution.py:433
  (15 shorter events, 0.2 us)
Async XLA Ops:
  1.6 14.1 %collective-permute-start = (f32[65,512]{1,0:T(8,128)S(1)}, f32[65,512]{1,0:T(8,128)S(1)}, u32[]{:S(2)}, u32[]{:S(2)}) collective-permute-start(f32[65,512]{1,0:T(8,128)S(1)} %pad_maximum_fusion), channel_id=1, source_target_pairs={{0,8},{2,10},{4,12},{6,14},{8,0},{10,2},{12,4},{14,6},{1,9},{3,11}... | collective-permute-start | bytes 399368 | tf_op jit(solution)/shard_map/ppermute | solution.py:456
  8.5 0.8 %copy-start.1 = (s32[8192]{0:T(1024)S(1)}, s32[8192]{0:T(1024)}, u32[]{:S(2)}) copy-start(s32[8192]{0:T(1024)} %param.7) | copy-start | bytes 98308
  9.3 6.4 %copy-start = (f32[64,512]{1,0:T(8,128)S(1)}, f32[64,512]{1,0:T(8,128)}, u32[]{:S(2)}) copy-start(f32[64,512]{1,0:T(8,128)} %direction_ref.1) | copy-start | bytes 393220
  9.3 6.4 %copy-start.2 = (f32[512]{0:T(512)S(1)}, f32[512]{0:T(512)}, u32[]{:S(2)}) copy-start(f32[512]{0:T(512)} %param.9) | copy-start | bytes 6148
  15.8 10.1 %collective-permute-start.3 = (bf16[64,1024]{1,0:T(8,128)(2,1)S(1)}, bf16[64,1024]{1,0:T(8,128)(2,1)S(1)}, u32[]{:S(2)}, u32[]{:S(2)}) collective-permute-start(bf16[64,1024]{1,0:T(8,128)(2,1)S(1)} %slice.54.refs_0_), channel_id=1, source_target_pairs={{0,6},{2,4},{4,2},{6,0},{8,14},{10,12},{12,10},{14,8},{1,7},{3,5},... | collective-permute-start | bytes 393224 | tf_op jit(solution)/shard_map/ppermute | solution.py:456
  18.4 7.5 %collective-permute-start.2 = (bf16[64,1024]{1,0:T(8,128)(2,1)S(1)}, bf16[64,1024]{1,0:T(8,128)(2,1)S(1)}, u32[]{:S(2)}, u32[]{:S(2)}) collective-permute-start(bf16[64,1024]{1,0:T(8,128)(2,1)S(1)} %slice.54.refs_0_), channel_id=1, source_target_pairs={{0,4},{2,6},{4,0},{6,2},{8,12},{10,14},{12,8},{14,10},{1,5},{3,7},... | collective-permute-start | bytes 393224 | tf_op jit(solution)/shard_map/ppermute | solution.py:456
  18.8 7.1 %collective-permute-start.1 = (bf16[64,1024]{1,0:T(8,128)(2,1)S(1)}, bf16[64,1024]{1,0:T(8,128)(2,1)S(1)}, u32[]{:S(2)}, u32[]{:S(2)}) collective-permute-start(bf16[64,1024]{1,0:T(8,128)(2,1)S(1)} %slice.54.refs_0_), channel_id=1, source_target_pairs={{0,2},{2,0},{4,6},{6,4},{8,10},{10,8},{12,14},{14,12},{1,3},{3,1},... | collective-permute-start | bytes 393224 | tf_op jit(solution)/shard_map/ppermute | solution.py:456
  29.0 1.6 %collective-permute-start.4 = (f32[64,1024]{1,0:T(8,128)S(1)}, f32[64,1024]{1,0:T(8,128)S(1)}, u32[]{:S(2)}, u32[]{:S(2)}) collective-permute-start(f32[64,1024]{1,0:T(8,128)S(1)} %slice.42), channel_id=1, source_target_pairs={{0,1},{1,0},{2,3},{3,2},{4,5},{5,4},{6,7},{7,6},{8,9},{9,8},{10,11... | collective-permute-start | bytes 786440 | tf_op jit(solution)/shard_map/ppermute | solution.py:459
  31.5 1.3 %collective-permute-start.5 = (f32[96,128]{1,0:T(8,128)S(1)}, f32[96,128]{1,0:T(8,128)S(1)}, u32[]{:S(2)}, u32[]{:S(2)}) collective-permute-start(f32[96,128]{1,0:T(8,128)S(1)} %get-tuple-element.17), channel_id=1, source_target_pairs={{0,1},{1,0},{2,3},{3,2},{4,5},{5,4},{6,7},{7,6},{8,9},{9,8},{10,11... | collective-permute-start | bytes 147464 | tf_op jit(solution)/shard_map/ppermute | solution.py:459
  32.8 5.2 %collective-permute-start.8 = (f32[96,128]{1,0:T(8,128)S(1)}, f32[96,128]{1,0:T(8,128)S(1)}, u32[]{:S(2)}, u32[]{:S(2)}) collective-permute-start(f32[96,128]{1,0:T(8,128)S(1)} %add.76.refs_0_), channel_id=1, source_target_pairs={{0,6},{2,4},{4,2},{6,0},{8,14},{10,12},{12,10},{14,8},{1,7},{3,5},... | collective-permute-start | bytes 147464 | tf_op jit(solution)/shard_map/ppermute | solution.py:456
  35.4 4.1 %collective-permute-start.7 = (f32[96,128]{1,0:T(8,128)S(1)}, f32[96,128]{1,0:T(8,128)S(1)}, u32[]{:S(2)}, u32[]{:S(2)}) collective-permute-start(f32[96,128]{1,0:T(8,128)S(1)} %add.76.refs_0_), channel_id=1, source_target_pairs={{0,4},{2,6},{4,0},{6,2},{8,12},{10,14},{12,8},{14,10},{1,5},{3,7},... | collective-permute-start | bytes 147464 | tf_op jit(solution)/shard_map/ppermute | solution.py:456
  35.8 4.1 %collective-permute-start.6 = (f32[96,128]{1,0:T(8,128)S(1)}, f32[96,128]{1,0:T(8,128)S(1)}, u32[]{:S(2)}, u32[]{:S(2)}) collective-permute-start(f32[96,128]{1,0:T(8,128)S(1)} %add.76.refs_0_), channel_id=1, source_target_pairs={{0,2},{2,0},{4,6},{6,4},{8,10},{10,8},{12,14},{14,12},{1,3},{3,1},... | collective-permute-start | bytes 147464 | tf_op jit(solution)/shard_map/ppermute | solution.py:456
  44.6 5.0 %collective-permute-start.11 = (bf16[64,1024]{1,0:T(8,128)(2,1)S(1)}, bf16[64,1024]{1,0:T(8,128)(2,1)S(1)}, u32[]{:S(2)}, u32[]{:S(2)}) collective-permute-start(bf16[64,1024]{1,0:T(8,128)(2,1)S(1)} %get-tuple-element.19.refs_0_), channel_id=1, source_target_pairs={{0,2},{2,0},{4,6},{6,4},{8,10},{10,8},{12,14},{14,12},{1,3},{3,1},... | collective-permute-start | bytes 393224 | tf_op jit(solution)/shard_map/ppermute | solution.py:456
  45.2 5.7 %collective-permute-start.10 = (bf16[64,1024]{1,0:T(8,128)(2,1)S(1)}, bf16[64,1024]{1,0:T(8,128)(2,1)S(1)}, u32[]{:S(2)}, u32[]{:S(2)}) collective-permute-start(bf16[64,1024]{1,0:T(8,128)(2,1)S(1)} %get-tuple-element.19.refs_0_), channel_id=1, source_target_pairs={{0,4},{2,6},{4,0},{6,2},{8,12},{10,14},{12,8},{14,10},{1,5},{3,7},... | collective-permute-start | bytes 393224 | tf_op jit(solution)/shard_map/ppermute | solution.py:456
  47.6 6.2 %collective-permute-start.9 = (bf16[64,1024]{1,0:T(8,128)(2,1)S(1)}, bf16[64,1024]{1,0:T(8,128)(2,1)S(1)}, u32[]{:S(2)}, u32[]{:S(2)}) collective-permute-start(bf16[64,1024]{1,0:T(8,128)(2,1)S(1)} %get-tuple-element.19.refs_0_), channel_id=1, source_target_pairs={{0,6},{2,4},{4,2},{6,0},{8,14},{10,12},{12,10},{14,8},{1,7},{3,5},... | collective-permute-start | bytes 393224 | tf_op jit(solution)/shard_map/ppermute | solution.py:456
  54.7 1.6 %collective-permute-start.12 = (f32[64,1024]{1,0:T(8,128)S(1)}, f32[64,1024]{1,0:T(8,128)S(1)}, u32[]{:S(2)}, u32[]{:S(2)}) collective-permute-start(f32[64,1024]{1,0:T(8,128)S(1)} %slice.44), channel_id=1, source_target_pairs={{0,1},{1,0},{2,3},{3,2},{4,5},{5,4},{6,7},{7,6},{8,9},{9,8},{10,11... | collective-permute-start | bytes 786440 | tf_op jit(solution)/shard_map/ppermute | solution.py:459
  56.7 1.3 %collective-permute-start.13 = (f32[64,128]{1,0:T(8,128)S(1)}, f32[64,128]{1,0:T(8,128)S(1)}, u32[]{:S(2)}, u32[]{:S(2)}) collective-permute-start(f32[64,128]{1,0:T(8,128)S(1)} %get-tuple-element.21), channel_id=1, source_target_pairs={{0,1},{1,0},{2,3},{3,2},{4,5},{5,4},{6,7},{7,6},{8,9},{9,8},{10,11... | collective-permute-start | bytes 98312 | tf_op jit(solution)/shard_map/ppermute | solution.py:459
  57.9 4.8 %collective-permute-start.16 = (f32[64,128]{1,0:T(8,128)S(1)}, f32[64,128]{1,0:T(8,128)S(1)}, u32[]{:S(2)}, u32[]{:S(2)}) collective-permute-start(f32[64,128]{1,0:T(8,128)S(1)} %add.77.refs_0_), channel_id=1, source_target_pairs={{0,6},{2,4},{4,2},{6,0},{8,14},{10,12},{12,10},{14,8},{1,7},{3,5},... | collective-permute-start | bytes 98312 | tf_op jit(solution)/shard_map/ppermute | solution.py:456
  59.1 3.9 %collective-permute-start.15 = (f32[64,128]{1,0:T(8,128)S(1)}, f32[64,128]{1,0:T(8,128)S(1)}, u32[]{:S(2)}, u32[]{:S(2)}) collective-permute-start(f32[64,128]{1,0:T(8,128)S(1)} %add.77.refs_0_), channel_id=1, source_target_pairs={{0,4},{2,6},{4,0},{6,2},{8,12},{10,14},{12,8},{14,10},{1,5},{3,7},... | collective-permute-start | bytes 98312 | tf_op jit(solution)/shard_map/ppermute | solution.py:456
  60.6 3.9 %collective-permute-start.14 = (f32[64,128]{1,0:T(8,128)S(1)}, f32[64,128]{1,0:T(8,128)S(1)}, u32[]{:S(2)}, u32[]{:S(2)}) collective-permute-start(f32[64,128]{1,0:T(8,128)S(1)} %add.77.refs_0_), channel_id=1, source_target_pairs={{0,2},{2,0},{4,6},{6,4},{8,10},{10,8},{12,14},{14,12},{1,3},{3,1},... | collective-permute-start | bytes 98312 | tf_op jit(solution)/shard_map/ppermute | solution.py:456

commit v3 on v2

--- a/solution.py
+++ b/solution.py
@@ -11,6 +11,7 @@
 GROUP = 4
 LOW = 256
 FEATURES = 48
+UNROLL = 2
 STORED_LIMIT = 32 * 2**20
 
 soft_square = 0.09
@@ -116,9 +117,17 @@
     return first, second, third
 
 
-def position_kernel(starts, table_ref, owner_ref, offset_ref, out_ref, parts_ref, *, chunk, count, rows):
-    for part, value in enumerate(three_parts(table_ref[...])):
-        parts_ref[:, part * LOW : (part + 1) * LOW] = value
+def position_kernel(starts, table_ref, tail_ref, owner_ref, offset_ref, out_ref, parts_ref, *, chunk, count, rows):
+    full = table_ref.shape[0] // 3
+    tail = tail_ref.shape[1]
+    for axis in range(3):
+        first = axis * rows
+        if full < rows:
+            parts_ref[first + full // 8 * 8 : first + rows, :] = jnp.zeros((rows - full // 8 * 8, 3 * LOW), jnp.bfloat16)
+        for part, value in enumerate(three_parts(table_ref[axis * full : (axis + 1) * full])):
+            parts_ref[first : first + full, part * LOW : (part + 1) * LOW] = value
+        for part, value in enumerate(three_parts(tail_ref[axis : axis + 1])):
+            parts_ref[first + full : first + full + 1, part * LOW : part * LOW + tail] = value
 
     def one(j, carry):
         first = pl.multiple_of(starts[j], chunk)
@@ -133,40 +142,50 @@
             out_ref[axis : axis + 1, pl.ds(at, chunk)] = base + probe_radius * offset_ref[axis : axis + 1, pl.ds(first, chunk)]
         return carry
 
-    lax.fori_loop(0, count, one, 0)
-
-
-def chosen_positions(table, owner, offsets, starts, chunk):
+    lax.fori_loop(0, count, one, 0, unroll=UNROLL)
+
+
+def chosen_positions(atom_centers, owner, offsets, starts, chunk):
     count = starts.shape[0]
-    rows = table.shape[0] // 3
+    atoms = atom_centers.shape[1]
+    full = (atoms - 1) // LOW
+    rows = -(-(full + 1) // 16) * 16
+    table = atom_centers[:, : full * LOW].reshape(3 * full, LOW)
     whole = pl.BlockSpec(memory_space=pltpu.VMEM)
     return pl.pallas_call(
         functools.partial(position_kernel, chunk=chunk, count=count, rows=rows),
         out_shape=jax.ShapeDtypeStruct((3, count * chunk), jnp.float32),
-        in_specs=[pl.BlockSpec(memory_space=pltpu.SMEM), whole, whole, whole],
+        in_specs=[pl.BlockSpec(memory_space=pltpu.SMEM), whole, whole, whole, whole],
         out_specs=whole,
         scratch_shapes=[pltpu.VMEM((3 * rows, 3 * LOW), jnp.bfloat16)],
         compiler_params=params(24),
-        cost_estimate=pl.CostEstimate(flops=2 * 9 * rows * LOW * count * chunk, bytes_accessed=4 * 40000 * 3, transcendentals=0),
+        cost_estimate=pl.CostEstimate(flops=2 * 9 * rows * LOW * count * chunk, bytes_accessed=4 * atoms * 3, transcendentals=0),
         name="positions",
-    )(starts, table, owner, offsets)
+    )(starts, table, atom_centers[:, full * LOW :], owner, offsets)
 
 
 def features(pos, source):
-    axes = [pos[axis : axis + 1] for axis in range(3)]
-    square = axes[0] * axes[0] + axes[1] * axes[1] + axes[2] * axes[2]
-    one = jnp.ones_like(square).astype(jnp.bfloat16)
-    rows = []
-    for value in axes:
-        parts = three_parts(-2.0 * value if source else value)
-        pairs = [(0, 0), (0, 1), (1, 0), (0, 2), (1, 1), (2, 0), (1, 2), (2, 1), (2, 2)]
-        rows += [parts[pair[0] if source else pair[1]] for pair in pairs]
-    if source:
-        rows += [*three_parts(square), one, one, one]
-    else:
-        rows += [one, one, one, *three_parts(square + soft_square)]
-    rows += [jnp.zeros_like(one)] * (FEATURES - len(rows))
-    return jnp.concatenate(rows, axis=0)
+    first, second, third = three_parts(pos)
+    x1, x2, x3 = (part.astype(jnp.float32) for part in (first, second, third))
+    square_high, square_low, _ = three_parts(x1 * x1)
+    rest = 2.0 * (x1 * x2) + (2.0 * (x1 * x3) + x2 * x2) + 2.0 * (x2 * x3)
+    rest = rest[0:1] + rest[1:2] + rest[2:3]
+    rest = list(three_parts(rest if source else rest + soft_square))
+    one = jnp.ones_like(rest[0])
+    ones = [one] * 9
+    squares = [square_high, square_low, *rest]
+    scale = -2.0 if source else 1.0
+    parts = [(scale * part).astype(jnp.bfloat16) for part in (x1, x2, x3)]
+    large, small = [], []
+    for axis in range(3):
+        c = slice(axis, axis + 1)
+        mine = [square_high[c], square_low[c]]
+        large += [parts[0][c], *(mine + [one, one] if source else [one, one] + mine)]
+    for pair in [(0, 1), (1, 0), (1, 1), (0, 2), (2, 0), (1, 2), (2, 1), (2, 2)]:
+        small.append(parts[pair[0] if source else pair[1]])
+    small += rest + [one] * 3 if source else [one] * 3 + rest
+    pad = [jnp.zeros_like(one)] * (FEATURES - 45)
+    return jnp.concatenate(large + small + pad, axis=0)
 
 
 def entry_kernel(source_ref, target_ref, *refs):
@@ -204,25 +223,26 @@
     )(source_pos, target_pos)
 
 
-def apply_kernel(*refs, pieces, more):
+def apply_kernel(*refs, pieces, more, first):
     charge_refs, kern_refs, out_ref = refs[:pieces], refs[pieces : 2 * pieces], refs[-1]
     wide = 512
     for j in range(0, out_ref.shape[1], wide):
         total = refs[2 * pieces][:, j : j + wide] if more else None
         for charge_ref, kern_ref in zip(charge_refs, kern_refs):
-            part = jnp.dot(charge_ref[...], kern_ref[:, j : j + wide], preferred_element_type=jnp.float32)
+            kern = kern_ref[:, first + j : first + j + wide]
+            part = jnp.dot(charge_ref[...], kern, preferred_element_type=jnp.float32)
             total = part if total is None else total + part
         out_ref[:, j : j + wide] = total
 
 
-def apply_entries(charges, kerns, total=None):
+def apply_entries(charges, kerns, total=None, first=0, m=None):
     pieces = len(charges)
     k, n = charges[0].shape
-    m = kerns[0].shape[1]
+    m = kerns[0].shape[1] if m is None else m
     whole = pl.BlockSpec(memory_space=pltpu.VMEM)
     more = [] if total is None else [total]
     return pl.pallas_call(
-        functools.partial(apply_kernel, pieces=pieces, more=bool(more)),
+        functools.partial(apply_kernel, pieces=pieces, more=bool(more), first=first),
         out_shape=jax.ShapeDtypeStruct((k, m), jnp.float32),
         in_specs=[whole] * (2 * pieces + len(more)),
         out_specs=whole,
@@ -305,15 +325,13 @@
 
 def first_gram(partial, other, self_row, direction):
     k, n = direction.shape
-    mine = pl.BlockSpec((k, n), lambda i: (0, 0))
     whole = pl.BlockSpec(memory_space=pltpu.VMEM)
     return pl.pallas_call(
         first_gram_kernel,
-        grid=(1,),
         out_shape=[jax.ShapeDtypeStruct((k, n), jnp.float32), jax.ShapeDtypeStruct((k + k // 2, 2 * k), jnp.float32)],
-        in_specs=[mine, whole, whole, whole],
+        in_specs=[whole] * 4,
         out_specs=[whole, whole],
-        compiler_params=params(16),
+        compiler_params=params(8),
         cost_estimate=pl.CostEstimate(flops=6 * 2 * 3 * k * k * n, bytes_accessed=4 * k * n * 4, transcendentals=0),
         name="first_gram",
     )(partial, other, self_row, direction)
@@ -465,12 +483,11 @@
     charges = direction.astype(jnp.bfloat16)
     gathered = [charges] + [swap(charges, bits) for bits in range(1, GROUP)]
 
-    table = jnp.pad(atom_centers, ((0, 0), (0, -atom_centers.shape[1] % (LOW * 8)))).reshape(-1, LOW)
     angles = lax.optimization_barrier(tessera_angles.reshape(2, -1, 128))
     offsets = lax.optimization_barrier(unit_offsets(angles)).reshape(3, -1)
     starts = [((member ^ bits) + GROUP * c) * width + s * shard for bits in range(GROUP) for c in range(copies)]
     starts += [(member + GROUP * c) * width + (1 - s) * shard for c in range(copies)]
-    pos = chosen_positions(table, tessera_owner[None, :], offsets, jnp.stack(starts).astype(jnp.int32), shard)
+    pos = chosen_positions(atom_centers, tessera_owner[None, :], offsets, jnp.stack(starts).astype(jnp.int32), shard)
     n_near = copies * shard
     n_all = GROUP * n_near
     target_pos = jnp.concatenate([pos[:, :n_near], pos[:, n_all:]], axis=1)
@@ -483,8 +500,9 @@
     def mine(value):
         return lax.dynamic_slice_in_dim(value, ours * shard, shard, 1)
 
-    partial = apply_entries(gathered, kerns)
-    image, gram = first_gram(partial, swap_core(partial[:, n_near:]), self_row, direction)
+    to_other = apply_entries(gathered, kerns, first=n_near, m=n_near)
+    other = swap_core(to_other)
+    image, gram = first_gram(apply_entries(gathered, kerns, m=n_near), other, self_row, direction)
     alpha, later, charges = first_update(group_sum_parts(gram), image, direction)
 
     gathered = [swap(charges, bits) for bits in range(1, GROUP)]

time: 68.4 us -> 66.9 us (0.978)
  waiting for transfers between devices: 14.4 us -> 12.8 us
  Pallas kernels: 29.2 us -> 28.4 us
    slice x0 -> x2, local copies, waits for them, and re-layouts: none -> 1.87 us  [the longest x1 1.19 us: chosen_positions(): table = atom_centers[:, :full * LOW].reshape(3 * full, LOW)]
    ppermute x4, waiting for transfers between devices: 4.7 us -> 3 us  [swap_core(): return lax.ppermute(value, 'src', [(0, 1), (1, 0)])]
    pad x1 -> x0, local copies, waits for them, and re-layouts: 1.2 us -> none  [per_device_grouped(): jnp.pad(atom_centers, ((0, 0), (0, -atom_centers.shape[1] % (LOW * 8))))]
    pallas_call x1, Pallas kernels: 6.38 us -> 5.62 us  [chosen_positions(): pl.pallas_call(functools.partial(position_kernel, chunk=chunk, count=coun...]
    pallas_call x5 -> x6, Pallas kernels: 6.4 us -> 6.51 us  [apply_entries(): pl.pallas_call(functools.partial(apply_kernel, pieces=pieces, more=bool(m...]
  transfers between devices with their start and end apart: 17 -> 17, of which waited for: 13 -> 12; matrix products, arithmetic and copies ran while one was open for 4% -> 5% of each run, Pallas kernels for 23% -> 25%
where the time goes in v3:
time: 66.9 us; the launch traced here: 66.6 us
  Pallas kernels  28.4 us (42%)
  starting transfers between devices  19.1 us (29%)
  waiting for transfers between devices  12.8 us (19%)
  local copies, waits for them, and re-layouts  4.1 us (6%)
  other arithmetic  1.23 us (2%)
  between operations  0.96 us (1%)
    ppermute x13, starting transfers between devices, swap(): return lax.ppermute(value, 'tgt', [(i, i ^ bits) for i in range(n_tgt)])  18.2 us
    ppermute x13, waiting for transfers between devices, swap(): return lax.ppermute(value, 'tgt', [(i, i ^ bits) for i in range(n_tgt)])  9.77 us
    pallas_call x6, Pallas kernels, apply_entries(): pl.pallas_call(functools.partial(apply_kernel, pieces=pieces, more=bool(m...  6.51 us
    pallas_call x1, Pallas kernels, entries(): pl.pallas_call(entry_kernel, out_shape=[jax.ShapeDtypeStruct((n // pieces...  6.44 us
    pallas_call x1, Pallas kernels, chosen_positions(): pl.pallas_call(functools.partial(position_kernel, chunk=chunk, count=coun...  5.62 us
    pallas_call x1, Pallas kernels, first_update(): pl.pallas_call(functools.partial(first_update_kernel, count=len(parts)),...  4.68 us
    pallas_call x1, Pallas kernels, last_update(): pl.pallas_call(functools.partial(last_update_kernel, count=len(parts)), o...  3.52 us
    ppermute x4, waiting for transfers between devices, swap_core(): return lax.ppermute(value, 'src', [(0, 1), (1, 0)])  3 us
  transfers between devices with their start and end apart: 17, of which 12 were waited for; matrix products, arithmetic and copies ran while one was open for 5% of the time, Pallas kernels for 25%

profile of v3, /device:TPU:0, one launch (start us, length us, event | category | flops | bytes accessed | tf_op | source)
XLA Modules:
  0.0 66.6 jit_solution(8298542102776821753)
XLA Ops:
  0.6 0.9 %pad_maximum_fusion = f32[65,512]{1,0:T(8,128)S(1)} fusion(f32[1,512]{1,0:T(1,128)} %bitcast.25, f32[64,512]{1,0:T(8,128)} %direction_ref.1), kind=kLoop, calls=%fused_computation.1 | loop fusion | flops 33280 | bytes 266240 | tf_op jit(solution)/shard_map/concatenate | solution.py:479
  1.6 4.1 %collective-permute-start = (f32[65,512]{1,0:T(8,128)S(1)}, f32[65,512]{1,0:T(8,128)S(1)}, u32[]{:S(2)}, u32[]{:S(2)}) collective-permute-start(f32[65,512]{1,0:T(8,128)S(1)} %pad_maximum_fusion), channel_id=1, source_target_pairs={{0,8},{2,10},{4,12},{6,14},{8,0},{10,2},{12,4},{14,6},{1,9},{3,11}... | collective-permute-start | bytes 399368 | tf_op jit(solution)/shard_map/ppermute | solution.py:474
  5.7 0.7 %slice.32.tail_ref = f32[3,64]{1,0:T(4,128)S(1)} slice(f32[3,40000]{1,0:T(4,128)} %param.6), slice={[0:3], [39936:40000]} | slice | bytes 1536 | tf_op jit(solution)/shard_map/slice | solution.py:164
  6.4 1.2 %slice.31 = f32[3,39936]{1,0:T(4,128)S(1)} slice(f32[3,40000]{1,0:T(4,128)} %param.6), slice={[0:3], [0:39936]} | slice | bytes 958464 | tf_op jit(solution)/shard_map/slice | solution.py:153
  7.6 0.8 %copy.12 = f32[1,2,64,128]{3,2,1,0:T(8,128)S(1)} copy(f32[1,2,64,128]{3,1,2,0:T(2,128)} %bitcast.24) | data formatting | bytes 131072
  8.4 0.2 cosine_multiply_fusion
  8.7 0.1 copy.11
  8.8 0.3 reshape.13.table_ref
  9.1 0.1 stack.49.starts
  9.2 0.0 copy-start.1
  9.2 0.8 %copy-done.1 = s32[8192]{0:T(1024)S(1)} copy-done((s32[8192]{0:T(1024)S(1)}, s32[8192]{0:T(1024)}, u32[]{:S(2)}) %copy-start.1) | copy-done | bytes 32792
  10.0 0.0 copy-start
  10.0 0.0 copy-start.2
  10.0 5.6 %positions.1 = f32[3,5120]{1,0:T(4,128)S(1)} custom-call(s32[10]{0:T(128)S(1)} %stack.49.starts, f32[468,256]{1,0:T(8,128)S(1)} %reshape.13.table_ref, f32[3,64]{1,0:T(4,128)S(1)} %slice.32.tail_ref, s32[1,8192]{1,0:T(1,128)S(1)} %bitcast.21, f32[3,8192]{1,0:T(4,128)S(1)} %bitcast.20), custom_call_target="tpu_custom_call" | custom-call | flops 3774873600 | bytes 480000 | tf_op jit(solution)/shard_map/positions/pallas_call | solution.py:155
  15.6 0.0 collective-permute-done
  15.6 0.0 copy-done
  15.6 0.0 copy-done.2
  15.7 2.6 %collective-permute-start.3 = (bf16[64,1024]{1,0:T(8,128)(2,1)S(1)}, bf16[64,1024]{1,0:T(8,128)(2,1)S(1)}, u32[]{:S(2)}, u32[]{:S(2)}) collective-permute-start(bf16[64,1024]{1,0:T(8,128)(2,1)S(1)} %slice.57.refs_0_), channel_id=1, source_target_pairs={{0,6},{2,4},{4,2},{6,0},{8,14},{10,12},{12,10},{14,8},{1,7},{3,5},... | collective-permute-start | bytes 393224 | tf_op jit(solution)/shard_map/ppermute | solution.py:474
  18.3 0.5 collective-permute-start.2
  18.8 0.5 collective-permute-start.1
  19.3 6.4 %entries.1 = (bf16[1024,2048]{1,0:T(8,128)(2,1)S(1)}, bf16[1024,2048]{1,0:T(8,128)(2,1)S(1)}, bf16[1024,2048]{1,0:T(8,128)(2,1)S(1)}, bf16[1024,2048]{1,0:T(8,128)(2,1)S(1)}) custom-call(f32[3,4096]{1,0:T(4,128)S(1)} %slice.43.source_ref, f32[3,2048]{1,0:T(4,128)S(1)} %pad_maximum_fusion.2.target_ref), custom_call_target="tpu_custom_call" | custom-call | flops 100663296 | bytes 16777216 | tf_op jit(solution)/shard_map/entries/pallas_call | solution.py:214
  25.7 0.0 collective-permute-done.3.refs_3_
  25.7 0.0 collective-permute-done.2.refs_2_
  25.7 0.0 collective-permute-done.1.refs_1_
  25.8 1.6 %apply.7 = f32[64,1024]{1,0:T(8,128)S(1)} custom-call(bf16[64,1024]{1,0:T(8,128)(2,1)S(1)} %slice.57.refs_0_, bf16[64,1024]{1,0:T(8,128)(2,1)S(1)} %collective-permute-done.1.refs_1_, bf16[64,1024]{1,0:T(8,128)(2,1)S(1)} %collective-permute-done.2.refs_2_, bf16[64,1024]{1,0:T(8,128)(2,1)S(1)} %collective-permute-done.3.refs_3_, ...), custom_call_target="tpu_custom_call" | custom-call | flops 2147483648 | bytes 8388608 | tf_op jit(solution)/shard_map/apply/pallas_call | solution.py:244
  27.3 0.1 collective-permute-start.4
  27.5 1.6 %apply.6.own_ref = f32[64,1024]{1,0:T(8,128)S(1)} custom-call(bf16[64,1024]{1,0:T(8,128)(2,1)S(1)} %slice.57.refs_0_, bf16[64,1024]{1,0:T(8,128)(2,1)S(1)} %collective-permute-done.1.refs_1_, bf16[64,1024]{1,0:T(8,128)(2,1)S(1)} %collective-permute-done.2.refs_2_, bf16[64,1024]{1,0:T(8,128)(2,1)S(1)} %collective-permute-done.3.refs_3_, ...), custom_call_target="tpu_custom_call" | custom-call | flops 2147483648 | bytes 8388608 | tf_op jit(solution)/shard_map/apply/pallas_call | solution.py:244
  29.0 0.0 collective-permute-done.4.other_ref
  29.0 0.9 %first_gram.1 = (f32[64,1024]{1,0:T(8,128)S(1)}, f32[96,128]{1,0:T(8,128)S(1)}) custom-call(f32[64,1024]{1,0:T(8,128)S(1)} %apply.6.own_ref, f32[64,1024]{1,0:T(8,128)S(1)} %collective-permute-done.4.other_ref, f32[1,1024]{1,0:T(1,128)S(1)} %slice.46.self_ref, f32[64,1024]{1,0:T(8,128)S(1)} %slice.40.direction_ref.refs_5_), custom_call_target="tpu_custom_call" | custom-call | flops 150994944 | bytes 1048576 | tf_op jit(solution)/shard_map/first_gram/pallas_call | solution.py:329
  29.9 0.5 collective-permute-start.5
  30.5 0.9 %collective-permute-done.5 = f32[96,128]{1,0:T(8,128)S(1)} collective-permute-done((f32[96,128]{1,0:T(8,128)S(1)}, f32[96,128]{1,0:T(8,128)S(1)}, u32[]{:S(2)}, u32[]{:S(2)}) %collective-permute-start.5) | collective-permute-done | bytes 49184 | tf_op jit(solution)/shard_map/ppermute | solution.py:477
  31.3 2.6 %collective-permute-start.8 = (f32[96,128]{1,0:T(8,128)S(1)}, f32[96,128]{1,0:T(8,128)S(1)}, u32[]{:S(2)}, u32[]{:S(2)}) collective-permute-start(f32[96,128]{1,0:T(8,128)S(1)} %add.74.refs_0_), channel_id=1, source_target_pairs={{0,6},{2,4},{4,2},{6,0},{8,14},{10,12},{12,10},{14,8},{1,7},{3,5},... | collective-permute-start | bytes 147464 | tf_op jit(solution)/shard_map/ppermute | solution.py:474
  33.9 0.4 collective-permute-start.7
  34.3 0.5 collective-permute-start.6
  34.8 1.5 %collective-permute-done.8.refs_3_ = f32[96,128]{1,0:T(8,128)S(1)} collective-permute-done((f32[96,128]{1,0:T(8,128)S(1)}, f32[96,128]{1,0:T(8,128)S(1)}, u32[]{:S(2)}, u32[]{:S(2)}) %collective-permute-start.8) | collective-permute-done | bytes 49184 | tf_op jit(solution)/shard_map/ppermute | solution.py:474
  36.3 1.7 %collective-permute-done.7.refs_2_ = f32[96,128]{1,0:T(8,128)S(1)} collective-permute-done((f32[96,128]{1,0:T(8,128)S(1)}, f32[96,128]{1,0:T(8,128)S(1)}, u32[]{:S(2)}, u32[]{:S(2)}) %collective-permute-start.7) | collective-permute-done | bytes 49184 | tf_op jit(solution)/shard_map/ppermute | solution.py:474
  38.0 0.4 collective-permute-done.6.refs_1_
  38.4 4.7 %first_update.1 = (f32[64,128]{1,0:T(8,128)S(1)}, f32[64,1024]{1,0:T(8,128)S(1)}, bf16[64,1024]{1,0:T(8,128)(2,1)S(1)}) custom-call(f32[96,128]{1,0:T(8,128)S(1)} %add.74.refs_0_, f32[96,128]{1,0:T(8,128)S(1)} %collective-permute-done.6.refs_1_, f32[96,128]{1,0:T(8,128)S(1)} %collective-permute-done.7.refs_2_, f32[96,128]{1,0:T(8,128)S(1)} %collective-permute-done.8.refs_3_, ...), custom_call_target="tpu_custom_call" | custom-call | flops 100663296 | bytes 1310720 | tf_op jit(solution)/shard_map/first_update/pallas_call | solution.py:373
  43.1 0.6 collective-permute-start.11
  43.7 1.6 %collective-permute-start.10 = (bf16[64,1024]{1,0:T(8,128)(2,1)S(1)}, bf16[64,1024]{1,0:T(8,128)(2,1)S(1)}, u32[]{:S(2)}, u32[]{:S(2)}) collective-permute-start(bf16[64,1024]{1,0:T(8,128)(2,1)S(1)} %get-tuple-element.19.refs_0_), channel_id=1, source_target_pairs={{0,4},{2,6},{4,0},{6,2},{8,12},{10,14},{12,8},{14,10},{1,5},{3,7},... | collective-permute-start | bytes 393224 | tf_op jit(solution)/shard_map/ppermute | solution.py:474
  45.3 0.8 %apply.8.refs_2_ = f32[64,2048]{1,0:T(8,128)S(1)} custom-call(bf16[64,1024]{1,0:T(8,128)(2,1)S(1)} %get-tuple-element.19.refs_0_, bf16[1024,2048]{1,0:T(8,128)(2,1)S(1)} %get-tuple-element.13.refs_4_.refs_1_), custom_call_target="tpu_custom_call" | custom-call | flops 1073741824 | bytes 4194304 | tf_op jit(solution)/shard_map/apply/pallas_call | solution.py:244
  46.1 1.5 %collective-permute-start.9 = (bf16[64,1024]{1,0:T(8,128)(2,1)S(1)}, bf16[64,1024]{1,0:T(8,128)(2,1)S(1)}, u32[]{:S(2)}, u32[]{:S(2)}) collective-permute-start(bf16[64,1024]{1,0:T(8,128)(2,1)S(1)} %get-tuple-element.19.refs_0_), channel_id=1, source_target_pairs={{0,6},{2,4},{4,2},{6,0},{8,14},{10,12},{12,10},{14,8},{1,7},{3,5},... | collective-permute-start | bytes 393224 | tf_op jit(solution)/shard_map/ppermute | solution.py:474
  47.6 0.6 collective-permute-done.11.refs_0_
  48.2 0.8 %apply.9.refs_2_ = f32[64,2048]{1,0:T(8,128)S(1)} custom-call(bf16[64,1024]{1,0:T(8,128)(2,1)S(1)} %collective-permute-done.11.refs_0_, bf16[1024,2048]{1,0:T(8,128)(2,1)S(1)} %get-tuple-element.14.refs_5_.refs_1_, f32[64,2048]{1,0:T(8,128)S(1)} %apply.8.refs_2_), custom_call_target="tpu_custom_call" | custom-call | flops 1073741824 | bytes 4194304 | tf_op jit(solution)/shard_map/apply/pallas_call | solution.py:244
  49.0 0.1 collective-permute-done.10.refs_0_
  49.1 0.8 %apply.10.refs_2_ = f32[64,2048]{1,0:T(8,128)S(1)} custom-call(bf16[64,1024]{1,0:T(8,128)(2,1)S(1)} %collective-permute-done.10.refs_0_, bf16[1024,2048]{1,0:T(8,128)(2,1)S(1)} %get-tuple-element.15.refs_6_.refs_1_, f32[64,2048]{1,0:T(8,128)S(1)} %apply.9.refs_2_), custom_call_target="tpu_custom_call" | custom-call | flops 1073741824 | bytes 4194304 | tf_op jit(solution)/shard_map/apply/pallas_call | solution.py:244
  50.0 2.5 %collective-permute-done.9.refs_0_ = bf16[64,1024]{1,0:T(8,128)(2,1)S(1)} collective-permute-done((bf16[64,1024]{1,0:T(8,128)(2,1)S(1)}, bf16[64,1024]{1,0:T(8,128)(2,1)S(1)}, u32[]{:S(2)}, u32[]{:S(2)}) %collective-permute-start.9) | collective-permute-done | bytes 131104 | tf_op jit(solution)/shard_map/ppermute | solution.py:474
  52.4 0.8 %apply.11.own_ref = f32[64,2048]{1,0:T(8,128)S(1)} custom-call(bf16[64,1024]{1,0:T(8,128)(2,1)S(1)} %collective-permute-done.9.refs_0_, bf16[1024,2048]{1,0:T(8,128)(2,1)S(1)} %get-tuple-element.16.refs_7_.refs_1_, f32[64,2048]{1,0:T(8,128)S(1)} %apply.10.refs_2_), custom_call_target="tpu_custom_call" | custom-call | flops 1073741824 | bytes 4194304 | tf_op jit(solution)/shard_map/apply/pallas_call | solution.py:244
  53.3 0.1 collective-permute-start.12
  53.4 1.5 %collective-permute-done.12.other_ref = f32[64,1024]{1,0:T(8,128)S(1)} collective-permute-done((f32[64,1024]{1,0:T(8,128)S(1)}, f32[64,1024]{1,0:T(8,128)S(1)}, u32[]{:S(2)}, u32[]{:S(2)}) %collective-permute-start.12) | collective-permute-done | bytes 262176 | tf_op jit(solution)/shard_map/ppermute | solution.py:477
  54.9 0.4 second_gram.1
  55.3 0.2 collective-permute-start.13
  55.5 0.4 first_state.1.refs_5_
  55.9 0.6 collective-permute-done.13
  56.6 1.2 %collective-permute-start.16 = (f32[64,128]{1,0:T(8,128)S(1)}, f32[64,128]{1,0:T(8,128)S(1)}, u32[]{:S(2)}, u32[]{:S(2)}) collective-permute-start(f32[64,128]{1,0:T(8,128)S(1)} %add.75.refs_0_), channel_id=1, source_target_pairs={{0,6},{2,4},{4,2},{6,0},{8,14},{10,12},{12,10},{14,8},{1,7},{3,5},... | collective-permute-start | bytes 98312 | tf_op jit(solution)/shard_map/ppermute | solution.py:474
  57.8 1.4 %collective-permute-start.15 = (f32[64,128]{1,0:T(8,128)S(1)}, f32[64,128]{1,0:T(8,128)S(1)}, u32[]{:S(2)}, u32[]{:S(2)}) collective-permute-start(f32[64,128]{1,0:T(8,128)S(1)} %add.75.refs_0_), channel_id=1, source_target_pairs={{0,4},{2,6},{4,0},{6,2},{8,12},{10,14},{12,8},{14,10},{1,5},{3,7},... | collective-permute-start | bytes 98312 | tf_op jit(solution)/shard_map/ppermute | solution.py:474
  59.2 0.9 %collective-permute-start.14 = (f32[64,128]{1,0:T(8,128)S(1)}, f32[64,128]{1,0:T(8,128)S(1)}, u32[]{:S(2)}, u32[]{:S(2)}) collective-permute-start(f32[64,128]{1,0:T(8,128)S(1)} %add.75.refs_0_), channel_id=1, source_target_pairs={{0,2},{2,0},{4,6},{6,4},{8,10},{10,8},{12,14},{14,12},{1,3},{3,1},... | collective-permute-start | bytes 98312 | tf_op jit(solution)/shard_map/ppermute | solution.py:474
  60.1 1.5 %collective-permute-done.16.refs_3_ = f32[64,128]{1,0:T(8,128)S(1)} collective-permute-done((f32[64,128]{1,0:T(8,128)S(1)}, f32[64,128]{1,0:T(8,128)S(1)}, u32[]{:S(2)}, u32[]{:S(2)}) %collective-permute-start.16) | collective-permute-done | bytes 32800 | tf_op jit(solution)/shard_map/ppermute | solution.py:474
  61.6 0.1 collective-permute-done.15.refs_2_
  61.7 1.4 %collective-permute-done.14.refs_1_ = f32[64,128]{1,0:T(8,128)S(1)} collective-permute-done((f32[64,128]{1,0:T(8,128)S(1)}, f32[64,128]{1,0:T(8,128)S(1)}, u32[]{:S(2)}, u32[]{:S(2)}) %collective-permute-start.14) | collective-permute-done | bytes 32800 | tf_op jit(solution)/shard_map/ppermute | solution.py:474
  63.1 3.5 %last_update.1 = (f32[64,512]{1,0:T(8,128)}, f32[64,512]{1,0:T(8,128)}) custom-call(f32[64,128]{1,0:T(8,128)S(1)} %add.75.refs_0_, f32[64,128]{1,0:T(8,128)S(1)} %collective-permute-done.14.refs_1_, f32[64,128]{1,0:T(8,128)S(1)} %collective-permute-done.15.refs_2_, f32[64,128]{1,0:T(8,128)S(1)} %collective-permute-done.16.refs_3_, ...), custom_call_target="tpu_custom_call" | custom-call | flops 75497472 | bytes 786432 | tf_op jit(solution)/shard_map/last_update/pallas_call | solution.py:451
  (14 shorter events, 0.2 us)
Async XLA Ops:
  1.6 14.1 %collective-permute-start = (f32[65,512]{1,0:T(8,128)S(1)}, f32[65,512]{1,0:T(8,128)S(1)}, u32[]{:S(2)}, u32[]{:S(2)}) collective-permute-start(f32[65,512]{1,0:T(8,128)S(1)} %pad_maximum_fusion), channel_id=1, source_target_pairs={{0,8},{2,10},{4,12},{6,14},{8,0},{10,2},{12,4},{14,6},{1,9},{3,11}... | collective-permute-start | bytes 399368 | tf_op jit(solution)/shard_map/ppermute | solution.py:474
  9.2 0.8 %copy-start.1 = (s32[8192]{0:T(1024)S(1)}, s32[8192]{0:T(1024)}, u32[]{:S(2)}) copy-start(s32[8192]{0:T(1024)} %param.7) | copy-start | bytes 98308
  10.0 5.7 %copy-start = (f32[64,512]{1,0:T(8,128)S(1)}, f32[64,512]{1,0:T(8,128)}, u32[]{:S(2)}) copy-start(f32[64,512]{1,0:T(8,128)} %direction_ref.1) | copy-start | bytes 393220
  10.0 5.7 %copy-start.2 = (f32[512]{0:T(512)S(1)}, f32[512]{0:T(512)}, u32[]{:S(2)}) copy-start(f32[512]{0:T(512)} %param.9) | copy-start | bytes 6148
  15.7 10.0 %collective-permute-start.3 = (bf16[64,1024]{1,0:T(8,128)(2,1)S(1)}, bf16[64,1024]{1,0:T(8,128)(2,1)S(1)}, u32[]{:S(2)}, u32[]{:S(2)}) collective-permute-start(bf16[64,1024]{1,0:T(8,128)(2,1)S(1)} %slice.57.refs_0_), channel_id=1, source_target_pairs={{0,6},{2,4},{4,2},{6,0},{8,14},{10,12},{12,10},{14,8},{1,7},{3,5},... | collective-permute-start | bytes 393224 | tf_op jit(solution)/shard_map/ppermute | solution.py:474
  18.3 7.4 %collective-permute-start.2 = (bf16[64,1024]{1,0:T(8,128)(2,1)S(1)}, bf16[64,1024]{1,0:T(8,128)(2,1)S(1)}, u32[]{:S(2)}, u32[]{:S(2)}) collective-permute-start(bf16[64,1024]{1,0:T(8,128)(2,1)S(1)} %slice.57.refs_0_), channel_id=1, source_target_pairs={{0,4},{2,6},{4,0},{6,2},{8,12},{10,14},{12,8},{14,10},{1,5},{3,7},... | collective-permute-start | bytes 393224 | tf_op jit(solution)/shard_map/ppermute | solution.py:474
  18.8 7.0 %collective-permute-start.1 = (bf16[64,1024]{1,0:T(8,128)(2,1)S(1)}, bf16[64,1024]{1,0:T(8,128)(2,1)S(1)}, u32[]{:S(2)}, u32[]{:S(2)}) collective-permute-start(bf16[64,1024]{1,0:T(8,128)(2,1)S(1)} %slice.57.refs_0_), channel_id=1, source_target_pairs={{0,2},{2,0},{4,6},{6,4},{8,10},{10,8},{12,14},{14,12},{1,3},{3,1},... | collective-permute-start | bytes 393224 | tf_op jit(solution)/shard_map/ppermute | solution.py:474
  27.3 1.7 %collective-permute-start.4 = (f32[64,1024]{1,0:T(8,128)S(1)}, f32[64,1024]{1,0:T(8,128)S(1)}, u32[]{:S(2)}, u32[]{:S(2)}) collective-permute-start(f32[64,1024]{1,0:T(8,128)S(1)} %apply.7), channel_id=1, source_target_pairs={{0,1},{1,0},{2,3},{3,2},{4,5},{5,4},{6,7},{7,6},{8,9},{9,8},{10,11... | collective-permute-start | bytes 786440 | tf_op jit(solution)/shard_map/ppermute | solution.py:477
  29.9 1.4 %collective-permute-start.5 = (f32[96,128]{1,0:T(8,128)S(1)}, f32[96,128]{1,0:T(8,128)S(1)}, u32[]{:S(2)}, u32[]{:S(2)}) collective-permute-start(f32[96,128]{1,0:T(8,128)S(1)} %get-tuple-element.17), channel_id=1, source_target_pairs={{0,1},{1,0},{2,3},{3,2},{4,5},{5,4},{6,7},{7,6},{8,9},{9,8},{10,11... | collective-permute-start | bytes 147464 | tf_op jit(solution)/shard_map/ppermute | solution.py:477
  31.3 5.0 %collective-permute-start.8 = (f32[96,128]{1,0:T(8,128)S(1)}, f32[96,128]{1,0:T(8,128)S(1)}, u32[]{:S(2)}, u32[]{:S(2)}) collective-permute-start(f32[96,128]{1,0:T(8,128)S(1)} %add.74.refs_0_), channel_id=1, source_target_pairs={{0,6},{2,4},{4,2},{6,0},{8,14},{10,12},{12,10},{14,8},{1,7},{3,5},... | collective-permute-start | bytes 147464 | tf_op jit(solution)/shard_map/ppermute | solution.py:474
  33.9 4.1 %collective-permute-start.7 = (f32[96,128]{1,0:T(8,128)S(1)}, f32[96,128]{1,0:T(8,128)S(1)}, u32[]{:S(2)}, u32[]{:S(2)}) collective-permute-start(f32[96,128]{1,0:T(8,128)S(1)} %add.74.refs_0_), channel_id=1, source_target_pairs={{0,4},{2,6},{4,0},{6,2},{8,12},{10,14},{12,8},{14,10},{1,5},{3,7},... | collective-permute-start | bytes 147464 | tf_op jit(solution)/shard_map/ppermute | solution.py:474
  34.3 4.1 %collective-permute-start.6 = (f32[96,128]{1,0:T(8,128)S(1)}, f32[96,128]{1,0:T(8,128)S(1)}, u32[]{:S(2)}, u32[]{:S(2)}) collective-permute-start(f32[96,128]{1,0:T(8,128)S(1)} %add.74.refs_0_), channel_id=1, source_target_pairs={{0,2},{2,0},{4,6},{6,4},{8,10},{10,8},{12,14},{14,12},{1,3},{3,1},... | collective-permute-start | bytes 147464 | tf_op jit(solution)/shard_map/ppermute | solution.py:474
  43.1 5.0 %collective-permute-start.11 = (bf16[64,1024]{1,0:T(8,128)(2,1)S(1)}, bf16[64,1024]{1,0:T(8,128)(2,1)S(1)}, u32[]{:S(2)}, u32[]{:S(2)}) collective-permute-start(bf16[64,1024]{1,0:T(8,128)(2,1)S(1)} %get-tuple-element.19.refs_0_), channel_id=1, source_target_pairs={{0,2},{2,0},{4,6},{6,4},{8,10},{10,8},{12,14},{14,12},{1,3},{3,1},... | collective-permute-start | bytes 393224 | tf_op jit(solution)/shard_map/ppermute | solution.py:474
  43.7 5.4 %collective-permute-start.10 = (bf16[64,1024]{1,0:T(8,128)(2,1)S(1)}, bf16[64,1024]{1,0:T(8,128)(2,1)S(1)}, u32[]{:S(2)}, u32[]{:S(2)}) collective-permute-start(bf16[64,1024]{1,0:T(8,128)(2,1)S(1)} %get-tuple-element.19.refs_0_), channel_id=1, source_target_pairs={{0,4},{2,6},{4,0},{6,2},{8,12},{10,14},{12,8},{14,10},{1,5},{3,7},... | collective-permute-start | bytes 393224 | tf_op jit(solution)/shard_map/ppermute | solution.py:474
  46.1 6.3 %collective-permute-start.9 = (bf16[64,1024]{1,0:T(8,128)(2,1)S(1)}, bf16[64,1024]{1,0:T(8,128)(2,1)S(1)}, u32[]{:S(2)}, u32[]{:S(2)}) collective-permute-start(bf16[64,1024]{1,0:T(8,128)(2,1)S(1)} %get-tuple-element.19.refs_0_), channel_id=1, source_target_pairs={{0,6},{2,4},{4,2},{6,0},{8,14},{10,12},{12,10},{14,8},{1,7},{3,5},... | collective-permute-start | bytes 393224 | tf_op jit(solution)/shard_map/ppermute | solution.py:474
  53.3 1.6 %collective-permute-start.12 = (f32[64,1024]{1,0:T(8,128)S(1)}, f32[64,1024]{1,0:T(8,128)S(1)}, u32[]{:S(2)}, u32[]{:S(2)}) collective-permute-start(f32[64,1024]{1,0:T(8,128)S(1)} %slice.47), channel_id=1, source_target_pairs={{0,1},{1,0},{2,3},{3,2},{4,5},{5,4},{6,7},{7,6},{8,9},{9,8},{10,11... | collective-permute-start | bytes 786440 | tf_op jit(solution)/shard_map/ppermute | solution.py:477
  55.3 1.3 %collective-permute-start.13 = (f32[64,128]{1,0:T(8,128)S(1)}, f32[64,128]{1,0:T(8,128)S(1)}, u32[]{:S(2)}, u32[]{:S(2)}) collective-permute-start(f32[64,128]{1,0:T(8,128)S(1)} %get-tuple-element.21), channel_id=1, source_target_pairs={{0,1},{1,0},{2,3},{3,2},{4,5},{5,4},{6,7},{7,6},{8,9},{9,8},{10,11... | collective-permute-start | bytes 98312 | tf_op jit(solution)/shard_map/ppermute | solution.py:477
  56.6 5.0 %collective-permute-start.16 = (f32[64,128]{1,0:T(8,128)S(1)}, f32[64,128]{1,0:T(8,128)S(1)}, u32[]{:S(2)}, u32[]{:S(2)}) collective-permute-start(f32[64,128]{1,0:T(8,128)S(1)} %add.75.refs_0_), channel_id=1, source_target_pairs={{0,6},{2,4},{4,2},{6,0},{8,14},{10,12},{12,10},{14,8},{1,7},{3,5},... | collective-permute-start | bytes 98312 | tf_op jit(solution)/shard_map/ppermute | solution.py:474
  57.8 3.9 %collective-permute-start.15 = (f32[64,128]{1,0:T(8,128)S(1)}, f32[64,128]{1,0:T(8,128)S(1)}, u32[]{:S(2)}, u32[]{:S(2)}) collective-permute-start(f32[64,128]{1,0:T(8,128)S(1)} %add.75.refs_0_), channel_id=1, source_target_pairs={{0,4},{2,6},{4,0},{6,2},{8,12},{10,14},{12,8},{14,10},{1,5},{3,7},... | collective-permute-start | bytes 98312 | tf_op jit(solution)/shard_map/ppermute | solution.py:474
  59.2 3.9 %collective-permute-start.14 = (f32[64,128]{1,0:T(8,128)S(1)}, f32[64,128]{1,0:T(8,128)S(1)}, u32[]{:S(2)}, u32[]{:S(2)}) collective-permute-start(f32[64,128]{1,0:T(8,128)S(1)} %add.75.refs_0_), channel_id=1, source_target_pairs={{0,2},{2,0},{4,6},{6,4},{8,10},{10,8},{12,14},{14,12},{1,3},{3,1},... | collective-permute-start | bytes 98312 | tf_op jit(solution)/shard_map/ppermute | solution.py:474

commit v4 on v3

--- a/solution.py
+++ b/solution.py
@@ -11,7 +11,8 @@
 GROUP = 4
 LOW = 256
 FEATURES = 48
-UNROLL = 2
+UNROLL = 10
+BLOCK = 8
 STORED_LIMIT = 32 * 2**20
 
 soft_square = 0.09
@@ -117,17 +118,28 @@
     return first, second, third
 
 
-def position_kernel(starts, table_ref, tail_ref, owner_ref, offset_ref, out_ref, parts_ref, *, chunk, count, rows):
-    full = table_ref.shape[0] // 3
-    tail = tail_ref.shape[1]
+def position_kernel(
+    starts, table_hbm, owner_hbm, offset_ref, out_ref, table_ref, owner_ref, rows_ref, parts_ref, table_sem, owner_sem, *, chunk, count, rows
+):
+    table_copy = pltpu.make_async_copy(table_hbm, table_ref, table_sem)
+    owner_copy = pltpu.make_async_copy(owner_hbm, owner_ref, owner_sem)
+    table_copy.start()
+    owner_copy.start()
+    atoms = table_ref.shape[1]
+    last = (atoms - 1) // LOW
     for axis in range(3):
-        first = axis * rows
-        if full < rows:
-            parts_ref[first + full // 8 * 8 : first + rows, :] = jnp.zeros((rows - full // 8 * 8, 3 * LOW), jnp.bfloat16)
-        for part, value in enumerate(three_parts(table_ref[axis * full : (axis + 1) * full])):
-            parts_ref[first : first + full, part * LOW : (part + 1) * LOW] = value
-        for part, value in enumerate(three_parts(tail_ref[axis : axis + 1])):
-            parts_ref[first + full : first + full + 1, part * LOW : part * LOW + tail] = value
+        at = axis * rows + last
+        rows_ref[at : (axis + 1) * rows, :] = jnp.zeros((rows - last, LOW), jnp.float32)
+    table_copy.wait()
+    owner_copy.wait()
+    for row in range(last + 1):
+        wide = min(LOW, atoms - row * LOW)
+        values = table_ref[:, row * LOW : row * LOW + wide]
+        for axis in range(3):
+            at = axis * rows + row
+            rows_ref[at : at + 1, :wide] = values[axis : axis + 1]
+    for part, value in enumerate(three_parts(rows_ref[...])):
+        parts_ref[:, part * LOW : (part + 1) * LOW] = value
 
     def one(j, carry):
         first = pl.multiple_of(starts[j], chunk)
@@ -145,23 +157,33 @@
     lax.fori_loop(0, count, one, 0, unroll=UNROLL)
 
 
+def in_hbm(array):
+    return pltpu.with_memory_space_constraint(array, pltpu.HBM)
+
+
 def chosen_positions(atom_centers, owner, offsets, starts, chunk):
     count = starts.shape[0]
     atoms = atom_centers.shape[1]
-    full = (atoms - 1) // LOW
-    rows = -(-(full + 1) // 16) * 16
-    table = atom_centers[:, : full * LOW].reshape(3 * full, LOW)
-    whole = pl.BlockSpec(memory_space=pltpu.VMEM)
+    rows = -(-atoms // (16 * LOW)) * 16
+    whole = pl.BlockSpec(memory_space=pltpu.VMEM)
+    far = pl.BlockSpec(memory_space=pltpu.HBM)
     return pl.pallas_call(
         functools.partial(position_kernel, chunk=chunk, count=count, rows=rows),
         out_shape=jax.ShapeDtypeStruct((3, count * chunk), jnp.float32),
-        in_specs=[pl.BlockSpec(memory_space=pltpu.SMEM), whole, whole, whole, whole],
+        in_specs=[pl.BlockSpec(memory_space=pltpu.SMEM), far, far, whole],
         out_specs=whole,
-        scratch_shapes=[pltpu.VMEM((3 * rows, 3 * LOW), jnp.bfloat16)],
+        scratch_shapes=[
+            pltpu.VMEM(atom_centers.shape, jnp.float32),
+            pltpu.VMEM(owner.shape, jnp.int32),
+            pltpu.VMEM((3 * rows, LOW), jnp.float32),
+            pltpu.VMEM((3 * rows, 3 * LOW), jnp.bfloat16),
+            pltpu.SemaphoreType.DMA,
+            pltpu.SemaphoreType.DMA,
+        ],
         compiler_params=params(24),
         cost_estimate=pl.CostEstimate(flops=2 * 9 * rows * LOW * count * chunk, bytes_accessed=4 * atoms * 3, transcendentals=0),
         name="positions",
-    )(starts, table, atom_centers[:, full * LOW :], owner, offsets)
+    )(starts, in_hbm(atom_centers), in_hbm(owner), offsets)
 
 
 def features(pos, source):
@@ -247,7 +269,7 @@
         in_specs=[whole] * (2 * pieces + len(more)),
         out_specs=whole,
         compiler_params=params(32),
-        cost_estimate=pl.CostEstimate(flops=8 * k * n * pieces * m, bytes_accessed=2 * pieces * n * m, transcendentals=0),
+        cost_estimate=pl.CostEstimate(flops=k * n, bytes_accessed=n, transcendentals=0),
         name="apply",
     )(*charges, *kerns, *more)
 
@@ -269,37 +291,44 @@
     return c * scale, -b * scale, a * scale
 
 
-def eliminate_four(system, i, row_of):
-    col = [jnp.broadcast_to(system[:, i + j : i + j + 1], system.shape) for j in range(4)]
-    row = [system[i + j : i + j + 1, :] for j in range(4)]
+def eliminate_block(system, first, row_of):
+    col = [jnp.broadcast_to(system[:, first + j : first + j + 1], system.shape) for j in range(BLOCK)]
+    row = [system[first + j : first + j + 1, :] for j in range(BLOCK)]
+    lower = {(r, c): col[c][first + r : first + r + 1] for c in range(BLOCK) for r in range(c, BLOCK)}
 
     def entry(r, c):
-        return col[c][i + r : i + r + 1]
-
-    a, b, d = inverse_of_pair(entry(0, 0), entry(1, 0), entry(1, 1))
-    t0, t1 = a * row[0] + b * row[1], b * row[0] + d * row[1]
-    b00, b01, b10, b11 = entry(2, 0), entry(3, 0), entry(2, 1), entry(3, 1)
-    e00, e10 = a * b00 + b * b10, b * b00 + d * b10
-    e01, e11 = a * b01 + b * b11, b * b01 + d * b11
-    u, v, w = inverse_of_pair(
-        entry(2, 2) - (b00 * e00 + b10 * e10),
-        entry(3, 2) - (b00 * e01 + b10 * e11),
-        entry(3, 3) - (b01 * e01 + b11 * e11),
-    )
-    y0, y1 = row[2] - (b00 * t0 + b10 * t1), row[3] - (b01 * t0 + b11 * t1)
-    q2, q3 = u * y0 + v * y1, v * y0 + w * y1
-    solved = [t0 - (e00 * q2 + e01 * q3), t1 - (e10 * q2 + e11 * q3), q2, q3]
-    rest = (system - (col[0] * solved[0] + col[1] * solved[1])) - (col[2] * solved[2] + col[3] * solved[3])
-    for j in range(4):
-        rest = jnp.where(row_of == i + j, solved[j], rest)
+        return lower[max(r, c), min(r, c)]
+
+    inverses = []
+    for p in range(0, BLOCK, 2):
+        a, b, d = inverse_of_pair(entry(p, p), entry(p + 1, p), entry(p + 1, p + 1))
+        inverses.append((a, b, d))
+        for r in range(BLOCK - 1, p + 1, -1):
+            x, y = entry(r, p), entry(r, p + 1)
+            f0, f1 = x * a + y * b, x * b + y * d
+            for c in range(p + 2, r + 1):
+                lower[r, c] = lower[r, c] - (f0 * entry(c, p) + f1 * entry(c, p + 1))
+            row[r] = row[r] - (f0 * row[p] + f1 * row[p + 1])
+    solved = [None] * BLOCK
+    for p in range(BLOCK - 2, -1, -2):
+        y0, y1 = row[p], row[p + 1]
+        for c in range(p + 2, BLOCK):
+            y0, y1 = y0 - entry(c, p) * solved[c], y1 - entry(c, p + 1) * solved[c]
+        a, b, d = inverses[p // 2]
+        solved[p], solved[p + 1] = a * y0 + b * y1, b * y0 + d * y1
+    rest = system
+    for j in range(0, BLOCK, 2):
+        rest = rest - (col[j] * solved[j] + col[j + 1] * solved[j + 1])
+    for j in range(BLOCK):
+        rest = jnp.where(row_of == first + j, solved[j], rest)
     return rest
 
 
 def eliminate(systems):
     k = systems[0].shape[0]
     row_of = lax.broadcasted_iota(jnp.int32, systems[0].shape, 0)
-    for i in range(0, k, 4):
-        systems = [eliminate_four(system, i, row_of) for system in systems]
+    for first in range(0, k, BLOCK):
+        systems = [eliminate_block(system, first, row_of) for system in systems]
     return [system[:, k:] for system in systems]
 
 
@@ -476,13 +505,6 @@
     def swap_core(value):
         return lax.ppermute(value, "src", [(0, 1), (1, 0)])
 
-    near = jnp.concatenate([right_side, self_term[None, :]], axis=0)
-    far = swap(near, GROUP)
-    both = jnp.where(ours == 0, jnp.concatenate([near, far], axis=1), jnp.concatenate([far, near], axis=1))
-    direction, self_row = both[:columns], both[columns : columns + 1]
-    charges = direction.astype(jnp.bfloat16)
-    gathered = [charges] + [swap(charges, bits) for bits in range(1, GROUP)]
-
     angles = lax.optimization_barrier(tessera_angles.reshape(2, -1, 128))
     offsets = lax.optimization_barrier(unit_offsets(angles)).reshape(3, -1)
     starts = [((member ^ bits) + GROUP * c) * width + s * shard for bits in range(GROUP) for c in range(copies)]
@@ -491,7 +513,18 @@
     n_near = copies * shard
     n_all = GROUP * n_near
     target_pos = jnp.concatenate([pos[:, :n_near], pos[:, n_all:]], axis=1)
-    kerns = entries(pos[:, :n_all], target_pos, GROUP)
+    kerns = entries(pos[:, :n_near], target_pos, 1)
+
+    def beside(near, far):
+        return jnp.where(ours == 0, jnp.concatenate([near, far], axis=1), jnp.concatenate([far, near], axis=1))
+
+    self_near = self_term[None, :]
+    right_far, self_far, kerns = lax.optimization_barrier((swap(right_side, GROUP), swap(self_near, GROUP), kerns))
+    direction = beside(right_side, right_far)
+    self_row = beside(self_near, self_far)
+    charges = direction.astype(jnp.bfloat16)
+    gathered = [charges] + [swap(charges, bits) for bits in range(1, GROUP)]
+    kerns = [*kerns, *entries(pos[:, n_near:n_all], target_pos, GROUP - 1)]
 
     def group_sum_parts(value):
         value = value + swap_core(value)

time: 66.9 us -> 62.5 us (0.934)
  local copies, waits for them, and re-layouts: 4.1 us -> 1.09 us
  other arithmetic: 1.23 us -> 0.31 us
    slice x6 -> x1, local copies, waits for them, and re-layouts: 1.93 us -> 0.01 us  [per_device_grouped(): kerns = [*kerns, *entries(pos[:, n_near:n_all], target_pos, GROUP - 1)]]
    concatenate x1 -> x0, other arithmetic: 0.93 us -> none  [per_device_grouped(): near = jnp.concatenate([right_side, self_term[None, :]], axis=0)]
    pallas_call x1, Pallas kernels: 4.68 us -> 3.85 us  [first_update(): pl.pallas_call(functools.partial(first_update_kernel, count=len(parts)),...]
    unnamed x8 -> x6, local copies, waits for them, and re-layouts: 1.69 us -> 0.92 us
    pallas_call x1 -> x2, Pallas kernels: 6.44 us -> 6.82 us  [entries(): pl.pallas_call(entry_kernel, out_shape=[jax.ShapeDtypeStruct((n // pieces...]
    ppermute x13 -> x14, waiting for transfers between devices: 9.77 us -> 9.4 us  [swap(): return lax.ppermute(value, 'tgt', [(i, i ^ bits) for i in range(n_tgt)])]
    ppermute x13 -> x14, starting transfers between devices: 18.2 us -> 18.3 us  [swap(): return lax.ppermute(value, 'tgt', [(i, i ^ bits) for i in range(n_tgt)])]
  transfers between devices with their start and end apart: 17 -> 18, of which waited for: 12 -> 13; matrix products, arithmetic and copies ran while one was open for 5% -> 2% of each run, Pallas kernels for 25% -> 28%
where the time goes in v4:
time: 62.5 us; the launch traced here: 62.3 us
  Pallas kernels  28.4 us (45%)
  starting transfers between devices  19.2 us (31%)
  waiting for transfers between devices  12.4 us (20%)
  local copies, waits for them, and re-layouts  1.09 us (2%)
  between operations  0.9 us (1%)
    ppermute x14, starting transfers between devices, swap(): return lax.ppermute(value, 'tgt', [(i, i ^ bits) for i in range(n_tgt)])  18.3 us
    ppermute x14, waiting for transfers between devices, swap(): return lax.ppermute(value, 'tgt', [(i, i ^ bits) for i in range(n_tgt)])  9.4 us
    pallas_call x2, Pallas kernels, entries(): pl.pallas_call(entry_kernel, out_shape=[jax.ShapeDtypeStruct((n // pieces...  6.82 us
    pallas_call x6, Pallas kernels, apply_entries(): pl.pallas_call(functools.partial(apply_kernel, pieces=pieces, more=bool(m...  6.5 us
    pallas_call x1, Pallas kernels, chosen_positions(): pl.pallas_call(functools.partial(position_kernel, chunk=chunk, count=coun...  6.1 us
    pallas_call x1, Pallas kernels, first_update(): pl.pallas_call(functools.partial(first_update_kernel, count=len(parts)),...  3.85 us
    pallas_call x1, Pallas kernels, last_update(): pl.pallas_call(functools.partial(last_update_kernel, count=len(parts)), o...  3.5 us
    ppermute x4, waiting for transfers between devices, swap_core(): return lax.ppermute(value, 'src', [(0, 1), (1, 0)])  3 us
  transfers between devices with their start and end apart: 18, of which 13 were waited for; matrix products, arithmetic and copies ran while one was open for 2% of the time, Pallas kernels for 28%

profile of v4, /device:TPU:0, one launch (start us, length us, event | category | flops | bytes accessed | tf_op | source)
XLA Modules:
  0.0 62.3 jit_solution(1917902920450229492)
XLA Ops:
  0.6 4.1 %collective-permute-start.1 = (f32[1,512]{1,0:T(1,128)}, f32[1,512]{1,0:T(1,128)S(1)}, u32[]{:S(2)}, u32[]{:S(2)}) collective-permute-start(f32[1,512]{1,0:T(1,128)} %bitcast.24), channel_id=1, source_target_pairs={{0,8},{2,10},{4,12},{6,14},{8,0},{10,2},{12,4},{14,6},{1,9},{3,11}... | collective-permute-start | bytes 6152 | tf_op jit(solution)/shard_map/ppermute | solution.py:503
  4.7 0.1 collective-permute-start
  4.8 0.8 %copy.12 = f32[1,2,64,128]{3,2,1,0:T(8,128)S(1)} copy(f32[1,2,64,128]{3,1,2,0:T(2,128)} %bitcast.23) | data formatting | bytes 131072
  5.7 0.2 cosine_multiply_fusion
  5.9 0.1 copy.11
  6.0 0.1 stack.49.starts
  6.1 6.1 %positions.1 = f32[3,5120]{1,0:T(4,128)S(1)} custom-call(s32[10]{0:T(128)S(1)} %stack.49.starts, f32[3,40000]{1,0:T(4,128)} %table_hbm.1, s32[1,8192]{1,0:T(1,128)} %bitcast.26, f32[3,8192]{1,0:T(4,128)S(1)} %bitcast.20), custom_call_target="tpu_custom_call" | custom-call | flops 3774873600 | bytes 480000 | tf_op jit(solution)/shard_map/positions/pallas_call | solution.py:170
  12.2 0.0 copy-start
  12.2 1.8 %entries.2.refs_4_.refs_1_ = bf16[1024,2048]{1,0:T(8,128)(2,1)S(1)} custom-call(f32[3,1024]{1,0:T(4,128)S(1)} %get-tuple-element.31.source_ref, f32[3,2048]{1,0:T(4,128)S(1)} %pad_maximum_fusion.1.target_ref), custom_call_target="tpu_custom_call" | custom-call | flops 25165824 | bytes 4194304 | tf_op jit(solution)/shard_map/entries/pallas_call | solution.py:236
  14.1 0.0 collective-permute-done.1
  14.1 0.0 collective-permute-done
  14.1 0.0 copy-done
  14.1 2.9 %collective-permute-start.4 = (bf16[64,1024]{1,0:T(8,128)(2,1)S(1)}, bf16[64,1024]{1,0:T(8,128)(2,1)S(1)}, u32[]{:S(2)}, u32[]{:S(2)}) collective-permute-start(bf16[64,1024]{1,0:T(8,128)(2,1)S(1)} %get-tuple-element.28.refs_0_), channel_id=1, source_target_pairs={{0,6},{2,4},{4,2},{6,0},{8,14},{10,12},{12,10},{14,8},{1,7},{3,5},... | collective-permute-start | bytes 393224 | tf_op jit(solution)/shard_map/ppermute | solution.py:503
  17.0 0.4 collective-permute-start.3
  17.4 0.3 collective-permute-start.2
  17.7 5.0 %entries.3 = (bf16[1024,2048]{1,0:T(8,128)(2,1)S(1)}, bf16[1024,2048]{1,0:T(8,128)(2,1)S(1)}, bf16[1024,2048]{1,0:T(8,128)(2,1)S(1)}) custom-call(f32[3,3072]{1,0:T(4,128)S(1)} %slice.29.source_ref, f32[3,2048]{1,0:T(4,128)S(1)} %pad_maximum_fusion.1.target_ref), custom_call_target="tpu_custom_call" | custom-call | flops 75497472 | bytes 12582912 | tf_op jit(solution)/shard_map/entries/pallas_call | solution.py:236
  22.7 0.0 collective-permute-done.4.refs_3_
  22.7 0.2 collective-permute-done.3.refs_2_
  22.9 0.0 collective-permute-done.2.refs_1_
  23.0 0.0 copy-start.1
  23.0 1.6 %apply.7 = f32[64,1024]{1,0:T(8,128)S(1)} custom-call(bf16[64,1024]{1,0:T(8,128)(2,1)S(1)} %get-tuple-element.28.refs_0_, bf16[64,1024]{1,0:T(8,128)(2,1)S(1)} %collective-permute-done.2.refs_1_, bf16[64,1024]{1,0:T(8,128)(2,1)S(1)} %collective-permute-done.3.refs_2_, bf16[64,1024]{1,0:T(8,128)(2,1)S(1)} %collective-permute-done.4.refs_3_, ...), custom_call_target="tpu_custom_call" | custom-call | flops 65536 | bytes 1024 | tf_op jit(solution)/shard_map/apply/pallas_call | solution.py:266
  24.5 0.1 collective-permute-start.5
  24.6 0.0 copy-done.1
  24.6 1.6 %apply.6.own_ref = f32[64,1024]{1,0:T(8,128)S(1)} custom-call(bf16[64,1024]{1,0:T(8,128)(2,1)S(1)} %get-tuple-element.28.refs_0_, bf16[64,1024]{1,0:T(8,128)(2,1)S(1)} %collective-permute-done.2.refs_1_, bf16[64,1024]{1,0:T(8,128)(2,1)S(1)} %collective-permute-done.3.refs_2_, bf16[64,1024]{1,0:T(8,128)(2,1)S(1)} %collective-permute-done.4.refs_3_, ...), custom_call_target="tpu_custom_call" | custom-call | flops 65536 | bytes 1024 | tf_op jit(solution)/shard_map/apply/pallas_call | solution.py:266
  26.2 0.0 collective-permute-done.5.other_ref
  26.2 0.9 %first_gram.1 = (f32[64,1024]{1,0:T(8,128)S(1)}, f32[96,128]{1,0:T(8,128)S(1)}) custom-call(f32[64,1024]{1,0:T(8,128)S(1)} %apply.6.own_ref, f32[64,1024]{1,0:T(8,128)S(1)} %collective-permute-done.5.other_ref, f32[1,1024]{1,0:T(1,128)S(1)} %broadcast_select_fusion.self_ref, f32[64,1024]{1,0:T(8,128)S(1)} %get-tuple-element.29.direction_ref.refs_5_), custom_call_target="tpu_custom_call" | custom-call | flops 150994944 | bytes 1048576 | tf_op jit(solution)/shard_map/first_gram/pallas_call | solution.py:358
  27.1 0.5 collective-permute-start.6
  27.6 0.9 %collective-permute-done.6 = f32[96,128]{1,0:T(8,128)S(1)} collective-permute-done((f32[96,128]{1,0:T(8,128)S(1)}, f32[96,128]{1,0:T(8,128)S(1)}, u32[]{:S(2)}, u32[]{:S(2)}) %collective-permute-start.6) | collective-permute-done | bytes 49184 | tf_op jit(solution)/shard_map/ppermute | solution.py:506
  28.5 2.6 %collective-permute-start.9 = (f32[96,128]{1,0:T(8,128)S(1)}, f32[96,128]{1,0:T(8,128)S(1)}, u32[]{:S(2)}, u32[]{:S(2)}) collective-permute-start(f32[96,128]{1,0:T(8,128)S(1)} %add.74.refs_0_), channel_id=1, source_target_pairs={{0,6},{2,4},{4,2},{6,0},{8,14},{10,12},{12,10},{14,8},{1,7},{3,5},... | collective-permute-start | bytes 147464 | tf_op jit(solution)/shard_map/ppermute | solution.py:503
  31.1 0.4 collective-permute-start.8
  31.5 0.5 collective-permute-start.7
  32.0 1.5 %collective-permute-done.9.refs_3_ = f32[96,128]{1,0:T(8,128)S(1)} collective-permute-done((f32[96,128]{1,0:T(8,128)S(1)}, f32[96,128]{1,0:T(8,128)S(1)}, u32[]{:S(2)}, u32[]{:S(2)}) %collective-permute-start.9) | collective-permute-done | bytes 49184 | tf_op jit(solution)/shard_map/ppermute | solution.py:503
  33.5 1.7 %collective-permute-done.8.refs_2_ = f32[96,128]{1,0:T(8,128)S(1)} collective-permute-done((f32[96,128]{1,0:T(8,128)S(1)}, f32[96,128]{1,0:T(8,128)S(1)}, u32[]{:S(2)}, u32[]{:S(2)}) %collective-permute-start.8) | collective-permute-done | bytes 49184 | tf_op jit(solution)/shard_map/ppermute | solution.py:503
  35.2 0.4 collective-permute-done.7.refs_1_
  35.6 3.8 %first_update.1 = (f32[64,128]{1,0:T(8,128)S(1)}, f32[64,1024]{1,0:T(8,128)S(1)}, bf16[64,1024]{1,0:T(8,128)(2,1)S(1)}) custom-call(f32[96,128]{1,0:T(8,128)S(1)} %add.74.refs_0_, f32[96,128]{1,0:T(8,128)S(1)} %collective-permute-done.7.refs_1_, f32[96,128]{1,0:T(8,128)S(1)} %collective-permute-done.8.refs_2_, f32[96,128]{1,0:T(8,128)S(1)} %collective-permute-done.9.refs_3_, ...), custom_call_target="tpu_custom_call" | custom-call | flops 100663296 | bytes 1310720 | tf_op jit(solution)/shard_map/first_update/pallas_call | solution.py:402
  39.5 0.5 collective-permute-start.12
  40.0 1.6 %collective-permute-start.11 = (bf16[64,1024]{1,0:T(8,128)(2,1)S(1)}, bf16[64,1024]{1,0:T(8,128)(2,1)S(1)}, u32[]{:S(2)}, u32[]{:S(2)}) collective-permute-start(bf16[64,1024]{1,0:T(8,128)(2,1)S(1)} %get-tuple-element.23.refs_0_), channel_id=1, source_target_pairs={{0,4},{2,6},{4,0},{6,2},{8,12},{10,14},{12,8},{14,10},{1,5},{3,7},... | collective-permute-start | bytes 393224 | tf_op jit(solution)/shard_map/ppermute | solution.py:503
  41.7 1.4 %collective-permute-start.10 = (bf16[64,1024]{1,0:T(8,128)(2,1)S(1)}, bf16[64,1024]{1,0:T(8,128)(2,1)S(1)}, u32[]{:S(2)}, u32[]{:S(2)}) collective-permute-start(bf16[64,1024]{1,0:T(8,128)(2,1)S(1)} %get-tuple-element.23.refs_0_), channel_id=1, source_target_pairs={{0,6},{2,4},{4,2},{6,0},{8,14},{10,12},{12,10},{14,8},{1,7},{3,5},... | collective-permute-start | bytes 393224 | tf_op jit(solution)/shard_map/ppermute | solution.py:503
  43.0 0.8 %apply.8.refs_2_ = f32[64,2048]{1,0:T(8,128)S(1)} custom-call(bf16[64,1024]{1,0:T(8,128)(2,1)S(1)} %get-tuple-element.23.refs_0_, bf16[1024,2048]{1,0:T(8,128)(2,1)S(1)} %entries.2.refs_4_.refs_1_), custom_call_target="tpu_custom_call" | custom-call | flops 65536 | bytes 1024 | tf_op jit(solution)/shard_map/apply/pallas_call | solution.py:266
  43.9 1.5 %collective-permute-done.12.refs_0_ = bf16[64,1024]{1,0:T(8,128)(2,1)S(1)} collective-permute-done((bf16[64,1024]{1,0:T(8,128)(2,1)S(1)}, bf16[64,1024]{1,0:T(8,128)(2,1)S(1)}, u32[]{:S(2)}, u32[]{:S(2)}) %collective-permute-start.12) | collective-permute-done | bytes 131104 | tf_op jit(solution)/shard_map/ppermute | solution.py:503
  45.4 0.8 %apply.9.refs_2_ = f32[64,2048]{1,0:T(8,128)S(1)} custom-call(bf16[64,1024]{1,0:T(8,128)(2,1)S(1)} %collective-permute-done.12.refs_0_, bf16[1024,2048]{1,0:T(8,128)(2,1)S(1)} %get-tuple-element.17.refs_5_.refs_1_, f32[64,2048]{1,0:T(8,128)S(1)} %apply.8.refs_2_), custom_call_target="tpu_custom_call" | custom-call | flops 65536 | bytes 1024 | tf_op jit(solution)/shard_map/apply/pallas_call | solution.py:266
  46.3 0.1 collective-permute-done.11.refs_0_
  46.3 0.8 %apply.10.refs_2_ = f32[64,2048]{1,0:T(8,128)S(1)} custom-call(bf16[64,1024]{1,0:T(8,128)(2,1)S(1)} %collective-permute-done.11.refs_0_, bf16[1024,2048]{1,0:T(8,128)(2,1)S(1)} %get-tuple-element.18.refs_6_.refs_1_, f32[64,2048]{1,0:T(8,128)S(1)} %apply.9.refs_2_), custom_call_target="tpu_custom_call" | custom-call | flops 65536 | bytes 1024 | tf_op jit(solution)/shard_map/apply/pallas_call | solution.py:266
  47.2 1.1 %collective-permute-done.10.refs_0_ = bf16[64,1024]{1,0:T(8,128)(2,1)S(1)} collective-permute-done((bf16[64,1024]{1,0:T(8,128)(2,1)S(1)}, bf16[64,1024]{1,0:T(8,128)(2,1)S(1)}, u32[]{:S(2)}, u32[]{:S(2)}) %collective-permute-start.10) | collective-permute-done | bytes 131104 | tf_op jit(solution)/shard_map/ppermute | solution.py:503
  48.3 0.8 %apply.11.own_ref = f32[64,2048]{1,0:T(8,128)S(1)} custom-call(bf16[64,1024]{1,0:T(8,128)(2,1)S(1)} %collective-permute-done.10.refs_0_, bf16[1024,2048]{1,0:T(8,128)(2,1)S(1)} %get-tuple-element.19.refs_7_.refs_1_, f32[64,2048]{1,0:T(8,128)S(1)} %apply.10.refs_2_), custom_call_target="tpu_custom_call" | custom-call | flops 65536 | bytes 1024 | tf_op jit(solution)/shard_map/apply/pallas_call | solution.py:266
  49.2 0.1 collective-permute-start.13
  49.3 1.5 %collective-permute-done.13.other_ref = f32[64,1024]{1,0:T(8,128)S(1)} collective-permute-done((f32[64,1024]{1,0:T(8,128)S(1)}, f32[64,1024]{1,0:T(8,128)S(1)}, u32[]{:S(2)}, u32[]{:S(2)}) %collective-permute-start.13) | collective-permute-done | bytes 262176 | tf_op jit(solution)/shard_map/ppermute | solution.py:506
  50.8 0.4 second_gram.1
  51.2 0.2 collective-permute-start.14
  51.4 0.4 first_state.1.refs_5_
  51.8 0.6 %collective-permute-done.14 = f32[64,128]{1,0:T(8,128)S(1)} collective-permute-done((f32[64,128]{1,0:T(8,128)S(1)}, f32[64,128]{1,0:T(8,128)S(1)}, u32[]{:S(2)}, u32[]{:S(2)}) %collective-permute-start.14) | collective-permute-done | bytes 32800 | tf_op jit(solution)/shard_map/ppermute | solution.py:506
  52.4 1.7 %collective-permute-start.17 = (f32[64,128]{1,0:T(8,128)S(1)}, f32[64,128]{1,0:T(8,128)S(1)}, u32[]{:S(2)}, u32[]{:S(2)}) collective-permute-start(f32[64,128]{1,0:T(8,128)S(1)} %add.75.refs_0_), channel_id=1, source_target_pairs={{0,6},{2,4},{4,2},{6,0},{8,14},{10,12},{12,10},{14,8},{1,7},{3,5},... | collective-permute-start | bytes 98312 | tf_op jit(solution)/shard_map/ppermute | solution.py:503
  54.1 0.8 %collective-permute-start.16 = (f32[64,128]{1,0:T(8,128)S(1)}, f32[64,128]{1,0:T(8,128)S(1)}, u32[]{:S(2)}, u32[]{:S(2)}) collective-permute-start(f32[64,128]{1,0:T(8,128)S(1)} %add.75.refs_0_), channel_id=1, source_target_pairs={{0,4},{2,6},{4,0},{6,2},{8,12},{10,14},{12,8},{14,10},{1,5},{3,7},... | collective-permute-start | bytes 98312 | tf_op jit(solution)/shard_map/ppermute | solution.py:503
  54.9 1.0 %collective-permute-start.15 = (f32[64,128]{1,0:T(8,128)S(1)}, f32[64,128]{1,0:T(8,128)S(1)}, u32[]{:S(2)}, u32[]{:S(2)}) collective-permute-start(f32[64,128]{1,0:T(8,128)S(1)} %add.75.refs_0_), channel_id=1, source_target_pairs={{0,2},{2,0},{4,6},{6,4},{8,10},{10,8},{12,14},{14,12},{1,3},{3,1},... | collective-permute-start | bytes 98312 | tf_op jit(solution)/shard_map/ppermute | solution.py:503
  55.9 1.5 %collective-permute-done.17.refs_3_ = f32[64,128]{1,0:T(8,128)S(1)} collective-permute-done((f32[64,128]{1,0:T(8,128)S(1)}, f32[64,128]{1,0:T(8,128)S(1)}, u32[]{:S(2)}, u32[]{:S(2)}) %collective-permute-start.17) | collective-permute-done | bytes 32800 | tf_op jit(solution)/shard_map/ppermute | solution.py:503
  57.4 0.6 collective-permute-done.16.refs_2_
  58.0 0.8 %collective-permute-done.15.refs_1_ = f32[64,128]{1,0:T(8,128)S(1)} collective-permute-done((f32[64,128]{1,0:T(8,128)S(1)}, f32[64,128]{1,0:T(8,128)S(1)}, u32[]{:S(2)}, u32[]{:S(2)}) %collective-permute-start.15) | collective-permute-done | bytes 32800 | tf_op jit(solution)/shard_map/ppermute | solution.py:503
  58.8 3.5 %last_update.1 = (f32[64,512]{1,0:T(8,128)}, f32[64,512]{1,0:T(8,128)}) custom-call(f32[64,128]{1,0:T(8,128)S(1)} %add.75.refs_0_, f32[64,128]{1,0:T(8,128)S(1)} %collective-permute-done.15.refs_1_, f32[64,128]{1,0:T(8,128)S(1)} %collective-permute-done.16.refs_2_, f32[64,128]{1,0:T(8,128)S(1)} %collective-permute-done.17.refs_3_, ...), custom_call_target="tpu_custom_call" | custom-call | flops 75497472 | bytes 786432 | tf_op jit(solution)/shard_map/last_update/pallas_call | solution.py:480
  (12 shorter events, 0.1 us)
Async XLA Ops:
  0.6 13.4 %collective-permute-start.1 = (f32[1,512]{1,0:T(1,128)}, f32[1,512]{1,0:T(1,128)S(1)}, u32[]{:S(2)}, u32[]{:S(2)}) collective-permute-start(f32[1,512]{1,0:T(1,128)} %bitcast.24), channel_id=1, source_target_pairs={{0,8},{2,10},{4,12},{6,14},{8,0},{10,2},{12,4},{14,6},{1,9},{3,11}... | collective-permute-start | bytes 6152 | tf_op jit(solution)/shard_map/ppermute | solution.py:503
  4.7 9.3 %collective-permute-start = (f32[64,512]{1,0:T(8,128)}, f32[64,512]{1,0:T(8,128)S(1)}, u32[]{:S(2)}, u32[]{:S(2)}) collective-permute-start(f32[64,512]{1,0:T(8,128)} %direction_ref.1), channel_id=1, source_target_pairs={{0,8},{2,10},{4,12},{6,14},{8,0},{10,2},{12,4},{14,6},{1,9},{3,11}... | collective-permute-start | bytes 393224 | tf_op jit(solution)/shard_map/ppermute | solution.py:503
  12.2 1.9 %copy-start = (f32[64,512]{1,0:T(8,128)S(1)}, f32[64,512]{1,0:T(8,128)}, u32[]{:S(2)}) copy-start(f32[64,512]{1,0:T(8,128)} %direction_ref.1) | copy-start | bytes 393220
  14.1 8.6 %collective-permute-start.4 = (bf16[64,1024]{1,0:T(8,128)(2,1)S(1)}, bf16[64,1024]{1,0:T(8,128)(2,1)S(1)}, u32[]{:S(2)}, u32[]{:S(2)}) collective-permute-start(bf16[64,1024]{1,0:T(8,128)(2,1)S(1)} %get-tuple-element.28.refs_0_), channel_id=1, source_target_pairs={{0,6},{2,4},{4,2},{6,0},{8,14},{10,12},{12,10},{14,8},{1,7},{3,5},... | collective-permute-start | bytes 393224 | tf_op jit(solution)/shard_map/ppermute | solution.py:503
  17.0 5.9 %collective-permute-start.3 = (bf16[64,1024]{1,0:T(8,128)(2,1)S(1)}, bf16[64,1024]{1,0:T(8,128)(2,1)S(1)}, u32[]{:S(2)}, u32[]{:S(2)}) collective-permute-start(bf16[64,1024]{1,0:T(8,128)(2,1)S(1)} %get-tuple-element.28.refs_0_), channel_id=1, source_target_pairs={{0,4},{2,6},{4,0},{6,2},{8,12},{10,14},{12,8},{14,10},{1,5},{3,7},... | collective-permute-start | bytes 393224 | tf_op jit(solution)/shard_map/ppermute | solution.py:503
  17.4 5.5 %collective-permute-start.2 = (bf16[64,1024]{1,0:T(8,128)(2,1)S(1)}, bf16[64,1024]{1,0:T(8,128)(2,1)S(1)}, u32[]{:S(2)}, u32[]{:S(2)}) collective-permute-start(bf16[64,1024]{1,0:T(8,128)(2,1)S(1)} %get-tuple-element.28.refs_0_), channel_id=1, source_target_pairs={{0,2},{2,0},{4,6},{6,4},{8,10},{10,8},{12,14},{14,12},{1,3},{3,1},... | collective-permute-start | bytes 393224 | tf_op jit(solution)/shard_map/ppermute | solution.py:503
  23.0 1.7 %copy-start.1 = (f32[512]{0:T(512)S(1)}, f32[512]{0:T(512)}, u32[]{:S(2)}) copy-start(f32[512]{0:T(512)} %param.9) | copy-start | bytes 6148
  24.5 1.7 %collective-permute-start.5 = (f32[64,1024]{1,0:T(8,128)S(1)}, f32[64,1024]{1,0:T(8,128)S(1)}, u32[]{:S(2)}, u32[]{:S(2)}) collective-permute-start(f32[64,1024]{1,0:T(8,128)S(1)} %apply.7), channel_id=1, source_target_pairs={{0,1},{1,0},{2,3},{3,2},{4,5},{5,4},{6,7},{7,6},{8,9},{9,8},{10,11... | collective-permute-start | bytes 786440 | tf_op jit(solution)/shard_map/ppermute | solution.py:506
  27.1 1.4 %collective-permute-start.6 = (f32[96,128]{1,0:T(8,128)S(1)}, f32[96,128]{1,0:T(8,128)S(1)}, u32[]{:S(2)}, u32[]{:S(2)}) collective-permute-start(f32[96,128]{1,0:T(8,128)S(1)} %get-tuple-element.21), channel_id=1, source_target_pairs={{0,1},{1,0},{2,3},{3,2},{4,5},{5,4},{6,7},{7,6},{8,9},{9,8},{10,11... | collective-permute-start | bytes 147464 | tf_op jit(solution)/shard_map/ppermute | solution.py:506
  28.5 5.0 %collective-permute-start.9 = (f32[96,128]{1,0:T(8,128)S(1)}, f32[96,128]{1,0:T(8,128)S(1)}, u32[]{:S(2)}, u32[]{:S(2)}) collective-permute-start(f32[96,128]{1,0:T(8,128)S(1)} %add.74.refs_0_), channel_id=1, source_target_pairs={{0,6},{2,4},{4,2},{6,0},{8,14},{10,12},{12,10},{14,8},{1,7},{3,5},... | collective-permute-start | bytes 147464 | tf_op jit(solution)/shard_map/ppermute | solution.py:503
  31.1 4.1 %collective-permute-start.8 = (f32[96,128]{1,0:T(8,128)S(1)}, f32[96,128]{1,0:T(8,128)S(1)}, u32[]{:S(2)}, u32[]{:S(2)}) collective-permute-start(f32[96,128]{1,0:T(8,128)S(1)} %add.74.refs_0_), channel_id=1, source_target_pairs={{0,4},{2,6},{4,0},{6,2},{8,12},{10,14},{12,8},{14,10},{1,5},{3,7},... | collective-permute-start | bytes 147464 | tf_op jit(solution)/shard_map/ppermute | solution.py:503
  31.5 4.1 %collective-permute-start.7 = (f32[96,128]{1,0:T(8,128)S(1)}, f32[96,128]{1,0:T(8,128)S(1)}, u32[]{:S(2)}, u32[]{:S(2)}) collective-permute-start(f32[96,128]{1,0:T(8,128)S(1)} %add.74.refs_0_), channel_id=1, source_target_pairs={{0,2},{2,0},{4,6},{6,4},{8,10},{10,8},{12,14},{14,12},{1,3},{3,1},... | collective-permute-start | bytes 147464 | tf_op jit(solution)/shard_map/ppermute | solution.py:503
  39.5 5.9 %collective-permute-start.12 = (bf16[64,1024]{1,0:T(8,128)(2,1)S(1)}, bf16[64,1024]{1,0:T(8,128)(2,1)S(1)}, u32[]{:S(2)}, u32[]{:S(2)}) collective-permute-start(bf16[64,1024]{1,0:T(8,128)(2,1)S(1)} %get-tuple-element.23.refs_0_), channel_id=1, source_target_pairs={{0,2},{2,0},{4,6},{6,4},{8,10},{10,8},{12,14},{14,12},{1,3},{3,1},... | collective-permute-start | bytes 393224 | tf_op jit(solution)/shard_map/ppermute | solution.py:503
  40.0 6.3 %collective-permute-start.11 = (bf16[64,1024]{1,0:T(8,128)(2,1)S(1)}, bf16[64,1024]{1,0:T(8,128)(2,1)S(1)}, u32[]{:S(2)}, u32[]{:S(2)}) collective-permute-start(bf16[64,1024]{1,0:T(8,128)(2,1)S(1)} %get-tuple-element.23.refs_0_), channel_id=1, source_target_pairs={{0,4},{2,6},{4,0},{6,2},{8,12},{10,14},{12,8},{14,10},{1,5},{3,7},... | collective-permute-start | bytes 393224 | tf_op jit(solution)/shard_map/ppermute | solution.py:503
  41.7 6.6 %collective-permute-start.10 = (bf16[64,1024]{1,0:T(8,128)(2,1)S(1)}, bf16[64,1024]{1,0:T(8,128)(2,1)S(1)}, u32[]{:S(2)}, u32[]{:S(2)}) collective-permute-start(bf16[64,1024]{1,0:T(8,128)(2,1)S(1)} %get-tuple-element.23.refs_0_), channel_id=1, source_target_pairs={{0,6},{2,4},{4,2},{6,0},{8,14},{10,12},{12,10},{14,8},{1,7},{3,5},... | collective-permute-start | bytes 393224 | tf_op jit(solution)/shard_map/ppermute | solution.py:503
  49.2 1.6 %collective-permute-start.13 = (f32[64,1024]{1,0:T(8,128)S(1)}, f32[64,1024]{1,0:T(8,128)S(1)}, u32[]{:S(2)}, u32[]{:S(2)}) collective-permute-start(f32[64,1024]{1,0:T(8,128)S(1)} %slice.30), channel_id=1, source_target_pairs={{0,1},{1,0},{2,3},{3,2},{4,5},{5,4},{6,7},{7,6},{8,9},{9,8},{10,11... | collective-permute-start | bytes 786440 | tf_op jit(solution)/shard_map/ppermute | solution.py:506
  51.2 1.3 %collective-permute-start.14 = (f32[64,128]{1,0:T(8,128)S(1)}, f32[64,128]{1,0:T(8,128)S(1)}, u32[]{:S(2)}, u32[]{:S(2)}) collective-permute-start(f32[64,128]{1,0:T(8,128)S(1)} %get-tuple-element.25), channel_id=1, source_target_pairs={{0,1},{1,0},{2,3},{3,2},{4,5},{5,4},{6,7},{7,6},{8,9},{9,8},{10,11... | collective-permute-start | bytes 98312 | tf_op jit(solution)/shard_map/ppermute | solution.py:506
  52.4 5.0 %collective-permute-start.17 = (f32[64,128]{1,0:T(8,128)S(1)}, f32[64,128]{1,0:T(8,128)S(1)}, u32[]{:S(2)}, u32[]{:S(2)}) collective-permute-start(f32[64,128]{1,0:T(8,128)S(1)} %add.75.refs_0_), channel_id=1, source_target_pairs={{0,6},{2,4},{4,2},{6,0},{8,14},{10,12},{12,10},{14,8},{1,7},{3,5},... | collective-permute-start | bytes 98312 | tf_op jit(solution)/shard_map/ppermute | solution.py:503
  54.1 3.9 %collective-permute-start.16 = (f32[64,128]{1,0:T(8,128)S(1)}, f32[64,128]{1,0:T(8,128)S(1)}, u32[]{:S(2)}, u32[]{:S(2)}) collective-permute-start(f32[64,128]{1,0:T(8,128)S(1)} %add.75.refs_0_), channel_id=1, source_target_pairs={{0,4},{2,6},{4,0},{6,2},{8,12},{10,14},{12,8},{14,10},{1,5},{3,7},... | collective-permute-start | bytes 98312 | tf_op jit(solution)/shard_map/ppermute | solution.py:503
  54.9 3.9 %collective-permute-start.15 = (f32[64,128]{1,0:T(8,128)S(1)}, f32[64,128]{1,0:T(8,128)S(1)}, u32[]{:S(2)}, u32[]{:S(2)}) collective-permute-start(f32[64,128]{1,0:T(8,128)S(1)} %add.75.refs_0_), channel_id=1, source_target_pairs={{0,2},{2,0},{4,6},{6,4},{8,10},{10,8},{12,14},{14,12},{1,3},{3,1},... | collective-permute-start | bytes 98312 | tf_op jit(solution)/shard_map/ppermute | solution.py:503

commit v5 on v4

--- a/solution.py
+++ b/solution.py
@@ -419,8 +419,7 @@
     image = own_ref[...] + other_ref[...] + self_ref[...] * direction
     image_ref[...] = image
     k = direction.shape[0]
-    gram_ref[:, :k] = dots(direction, image)
-    gram_ref[:, k:] = jnp.zeros((k, k), jnp.float32)
+    gram_ref[...] = fold(dots(direction, image))
 
 
 def second_gram(partial, other, self_row, direction):
@@ -430,7 +429,7 @@
     return pl.pallas_call(
         second_gram_kernel,
         grid=(1,),
-        out_shape=[jax.ShapeDtypeStruct((k, n), jnp.float32), jax.ShapeDtypeStruct((k, 2 * k), jnp.float32)],
+        out_shape=[jax.ShapeDtypeStruct((k, n), jnp.float32), jax.ShapeDtypeStruct((k // 2, 2 * k), jnp.float32)],
         in_specs=[mine, whole, whole, whole],
         out_specs=[whole, whole],
         compiler_params=params(16),
@@ -465,9 +464,8 @@
     part_refs = refs[:count]
     alpha_ref, state_ref, direction_ref, image_ref, charge_ref, out_ref = refs[count:]
     total = sum_of([ref[...] for ref in part_refs])
-    k = total.shape[0]
-    n = direction_ref.shape[1]
-    gram = total[:, :k]
+    k, n = direction_ref.shape
+    gram = unfold(total)
     (alpha,) = eliminate([jnp.concatenate([0.5 * (gram + gram.T), alpha_ref[:, k:]], axis=1)])
     both = left_t(alpha, jnp.concatenate([direction_ref[...], image_ref[...]], axis=1))
     charge_ref[...] = state_ref[:, :n] + both[:, :n]
@@ -540,8 +538,8 @@
 
     gathered = [swap(charges, bits) for bits in range(1, GROUP)]
     partial = apply_entries([charges], kerns[:1])
-    for piece, kern in zip(gathered, kerns[1:]):
-        partial = apply_entries([piece], [kern], partial)
+    for j in (2, 1, 0):
+        partial = apply_entries([gathered[j]], [kerns[j + 1]], partial)
     state = first_state(alpha, right_side, mine(image))
     image, gram = second_gram(partial, swap_core(partial[:, n_near:]), self_row, later)
     return tuple(last_update(group_sum_parts(gram), alpha, state, mine(later), mine(image)))

time: 62.5 us -> 62.1 us (level)
  transfers between devices with their start and end apart: 18 -> 18, of which waited for: 13 -> 12; matrix products, arithmetic and copies ran while one was open for 2% -> 2% of each run, Pallas kernels for 28% -> 28%
where the time goes in v5:
time: 62.1 us; the launch traced here: 61.9 us
  Pallas kernels  28.6 us (46%)
  starting transfers between devices  19.1 us (31%)
  waiting for transfers between devices  12 us (19%)
  local copies, waits for them, and re-layouts  1.09 us (2%)
  between operations  0.9 us (1%)
    ppermute x14, starting transfers between devices, swap(): return lax.ppermute(value, 'tgt', [(i, i ^ bits) for i in range(n_tgt)])  18.3 us
    ppermute x14, waiting for transfers between devices, swap(): return lax.ppermute(value, 'tgt', [(i, i ^ bits) for i in range(n_tgt)])  9 us
    pallas_call x2, Pallas kernels, entries(): pl.pallas_call(entry_kernel, out_shape=[jax.ShapeDtypeStruct((n // pieces...  6.82 us
    pallas_call x6, Pallas kernels, apply_entries(): pl.pallas_call(functools.partial(apply_kernel, pieces=pieces, more=bool(m...  6.51 us
    pallas_call x1, Pallas kernels, chosen_positions(): pl.pallas_call(functools.partial(position_kernel, chunk=chunk, count=coun...  6.1 us
    pallas_call x1, Pallas kernels, first_update(): pl.pallas_call(functools.partial(first_update_kernel, count=len(parts)),...  3.85 us
    pallas_call x1, Pallas kernels, last_update(): pl.pallas_call(functools.partial(last_update_kernel, count=len(parts)), o...  3.57 us
    ppermute x4, waiting for transfers between devices, swap_core(): return lax.ppermute(value, 'src', [(0, 1), (1, 0)])  2.98 us
  transfers between devices with their start and end apart: 18, of which 12 were waited for; matrix products, arithmetic and copies ran while one was open for 2% of the time, Pallas kernels for 28%

profile of v5, /device:TPU:0, one launch (start us, length us, event | category | flops | bytes accessed | tf_op | source)
XLA Modules:
  0.0 61.9 jit_solution(8694863568614836483)
XLA Ops:
  0.6 4.1 %collective-permute-start.1 = (f32[1,512]{1,0:T(1,128)}, f32[1,512]{1,0:T(1,128)S(1)}, u32[]{:S(2)}, u32[]{:S(2)}) collective-permute-start(f32[1,512]{1,0:T(1,128)} %bitcast.24), channel_id=1, source_target_pairs={{0,8},{2,10},{4,12},{6,14},{8,0},{10,2},{12,4},{14,6},{1,9},{3,11}... | collective-permute-start | bytes 6152 | tf_op jit(solution)/shard_map/ppermute | solution.py:501
  4.7 0.1 collective-permute-start
  4.8 0.8 %copy.12 = f32[1,2,64,128]{3,2,1,0:T(8,128)S(1)} copy(f32[1,2,64,128]{3,1,2,0:T(2,128)} %bitcast.23) | data formatting | bytes 131072
  5.7 0.2 cosine_multiply_fusion
  5.9 0.1 copy.11
  6.0 0.1 stack.49.starts
  6.1 6.1 %positions.1 = f32[3,5120]{1,0:T(4,128)S(1)} custom-call(s32[10]{0:T(128)S(1)} %stack.49.starts, f32[3,40000]{1,0:T(4,128)} %table_hbm.1, s32[1,8192]{1,0:T(1,128)} %bitcast.26, f32[3,8192]{1,0:T(4,128)S(1)} %bitcast.20), custom_call_target="tpu_custom_call" | custom-call | flops 3774873600 | bytes 480000 | tf_op jit(solution)/shard_map/positions/pallas_call | solution.py:170
  12.2 0.0 copy-start
  12.2 1.8 %entries.2.refs_4_.refs_1_ = bf16[1024,2048]{1,0:T(8,128)(2,1)S(1)} custom-call(f32[3,1024]{1,0:T(4,128)S(1)} %get-tuple-element.31.source_ref, f32[3,2048]{1,0:T(4,128)S(1)} %pad_maximum_fusion.1.target_ref), custom_call_target="tpu_custom_call" | custom-call | flops 25165824 | bytes 4194304 | tf_op jit(solution)/shard_map/entries/pallas_call | solution.py:236
  14.1 0.0 collective-permute-done.1
  14.1 0.0 collective-permute-done
  14.1 0.0 copy-done
  14.1 2.9 %collective-permute-start.4 = (bf16[64,1024]{1,0:T(8,128)(2,1)S(1)}, bf16[64,1024]{1,0:T(8,128)(2,1)S(1)}, u32[]{:S(2)}, u32[]{:S(2)}) collective-permute-start(bf16[64,1024]{1,0:T(8,128)(2,1)S(1)} %get-tuple-element.28.refs_0_), channel_id=1, source_target_pairs={{0,6},{2,4},{4,2},{6,0},{8,14},{10,12},{12,10},{14,8},{1,7},{3,5},... | collective-permute-start | bytes 393224 | tf_op jit(solution)/shard_map/ppermute | solution.py:501
  17.0 0.4 collective-permute-start.3
  17.4 0.3 collective-permute-start.2
  17.7 5.0 %entries.3 = (bf16[1024,2048]{1,0:T(8,128)(2,1)S(1)}, bf16[1024,2048]{1,0:T(8,128)(2,1)S(1)}, bf16[1024,2048]{1,0:T(8,128)(2,1)S(1)}) custom-call(f32[3,3072]{1,0:T(4,128)S(1)} %slice.29.source_ref, f32[3,2048]{1,0:T(4,128)S(1)} %pad_maximum_fusion.1.target_ref), custom_call_target="tpu_custom_call" | custom-call | flops 75497472 | bytes 12582912 | tf_op jit(solution)/shard_map/entries/pallas_call | solution.py:236
  22.7 0.0 collective-permute-done.4.refs_3_
  22.7 0.2 collective-permute-done.3.refs_2_
  22.9 0.0 collective-permute-done.2.refs_1_
  23.0 0.0 copy-start.1
  23.0 1.6 %apply.7 = f32[64,1024]{1,0:T(8,128)S(1)} custom-call(bf16[64,1024]{1,0:T(8,128)(2,1)S(1)} %get-tuple-element.28.refs_0_, bf16[64,1024]{1,0:T(8,128)(2,1)S(1)} %collective-permute-done.2.refs_1_, bf16[64,1024]{1,0:T(8,128)(2,1)S(1)} %collective-permute-done.3.refs_2_, bf16[64,1024]{1,0:T(8,128)(2,1)S(1)} %collective-permute-done.4.refs_3_, ...), custom_call_target="tpu_custom_call" | custom-call | flops 65536 | bytes 1024 | tf_op jit(solution)/shard_map/apply/pallas_call | solution.py:266
  24.5 0.1 collective-permute-start.5
  24.6 0.0 copy-done.1
  24.6 1.6 %apply.6.own_ref = f32[64,1024]{1,0:T(8,128)S(1)} custom-call(bf16[64,1024]{1,0:T(8,128)(2,1)S(1)} %get-tuple-element.28.refs_0_, bf16[64,1024]{1,0:T(8,128)(2,1)S(1)} %collective-permute-done.2.refs_1_, bf16[64,1024]{1,0:T(8,128)(2,1)S(1)} %collective-permute-done.3.refs_2_, bf16[64,1024]{1,0:T(8,128)(2,1)S(1)} %collective-permute-done.4.refs_3_, ...), custom_call_target="tpu_custom_call" | custom-call | flops 65536 | bytes 1024 | tf_op jit(solution)/shard_map/apply/pallas_call | solution.py:266
  26.2 0.0 collective-permute-done.5.other_ref
  26.2 0.9 %first_gram.1 = (f32[64,1024]{1,0:T(8,128)S(1)}, f32[96,128]{1,0:T(8,128)S(1)}) custom-call(f32[64,1024]{1,0:T(8,128)S(1)} %apply.6.own_ref, f32[64,1024]{1,0:T(8,128)S(1)} %collective-permute-done.5.other_ref, f32[1,1024]{1,0:T(1,128)S(1)} %broadcast_select_fusion.self_ref, f32[64,1024]{1,0:T(8,128)S(1)} %get-tuple-element.29.direction_ref.refs_5_), custom_call_target="tpu_custom_call" | custom-call | flops 150994944 | bytes 1048576 | tf_op jit(solution)/shard_map/first_gram/pallas_call | solution.py:358
  27.1 0.5 collective-permute-start.6
  27.6 0.9 %collective-permute-done.6 = f32[96,128]{1,0:T(8,128)S(1)} collective-permute-done((f32[96,128]{1,0:T(8,128)S(1)}, f32[96,128]{1,0:T(8,128)S(1)}, u32[]{:S(2)}, u32[]{:S(2)}) %collective-permute-start.6) | collective-permute-done | bytes 49184 | tf_op jit(solution)/shard_map/ppermute | solution.py:504
  28.5 2.6 %collective-permute-start.9 = (f32[96,128]{1,0:T(8,128)S(1)}, f32[96,128]{1,0:T(8,128)S(1)}, u32[]{:S(2)}, u32[]{:S(2)}) collective-permute-start(f32[96,128]{1,0:T(8,128)S(1)} %add.74.refs_0_), channel_id=1, source_target_pairs={{0,6},{2,4},{4,2},{6,0},{8,14},{10,12},{12,10},{14,8},{1,7},{3,5},... | collective-permute-start | bytes 147464 | tf_op jit(solution)/shard_map/ppermute | solution.py:501
  31.1 0.4 collective-permute-start.8
  31.5 0.5 collective-permute-start.7
  32.0 1.5 %collective-permute-done.9.refs_3_ = f32[96,128]{1,0:T(8,128)S(1)} collective-permute-done((f32[96,128]{1,0:T(8,128)S(1)}, f32[96,128]{1,0:T(8,128)S(1)}, u32[]{:S(2)}, u32[]{:S(2)}) %collective-permute-start.9) | collective-permute-done | bytes 49184 | tf_op jit(solution)/shard_map/ppermute | solution.py:501
  33.5 1.7 %collective-permute-done.8.refs_2_ = f32[96,128]{1,0:T(8,128)S(1)} collective-permute-done((f32[96,128]{1,0:T(8,128)S(1)}, f32[96,128]{1,0:T(8,128)S(1)}, u32[]{:S(2)}, u32[]{:S(2)}) %collective-permute-start.8) | collective-permute-done | bytes 49184 | tf_op jit(solution)/shard_map/ppermute | solution.py:501
  35.2 0.4 collective-permute-done.7.refs_1_
  35.6 3.8 %first_update.1 = (f32[64,128]{1,0:T(8,128)S(1)}, f32[64,1024]{1,0:T(8,128)S(1)}, bf16[64,1024]{1,0:T(8,128)(2,1)S(1)}) custom-call(f32[96,128]{1,0:T(8,128)S(1)} %add.74.refs_0_, f32[96,128]{1,0:T(8,128)S(1)} %collective-permute-done.7.refs_1_, f32[96,128]{1,0:T(8,128)S(1)} %collective-permute-done.8.refs_2_, f32[96,128]{1,0:T(8,128)S(1)} %collective-permute-done.9.refs_3_, ...), custom_call_target="tpu_custom_call" | custom-call | flops 100663296 | bytes 1310720 | tf_op jit(solution)/shard_map/first_update/pallas_call | solution.py:402
  39.5 1.6 %collective-permute-start.12 = (bf16[64,1024]{1,0:T(8,128)(2,1)S(1)}, bf16[64,1024]{1,0:T(8,128)(2,1)S(1)}, u32[]{:S(2)}, u32[]{:S(2)}) collective-permute-start(bf16[64,1024]{1,0:T(8,128)(2,1)S(1)} %get-tuple-element.23.refs_0_), channel_id=1, source_target_pairs={{0,6},{2,4},{4,2},{6,0},{8,14},{10,12},{12,10},{14,8},{1,7},{3,5},... | collective-permute-start | bytes 393224 | tf_op jit(solution)/shard_map/ppermute | solution.py:501
  41.1 0.4 collective-permute-start.11
  41.5 1.6 %collective-permute-start.10 = (bf16[64,1024]{1,0:T(8,128)(2,1)S(1)}, bf16[64,1024]{1,0:T(8,128)(2,1)S(1)}, u32[]{:S(2)}, u32[]{:S(2)}) collective-permute-start(bf16[64,1024]{1,0:T(8,128)(2,1)S(1)} %get-tuple-element.23.refs_0_), channel_id=1, source_target_pairs={{0,2},{2,0},{4,6},{6,4},{8,10},{10,8},{12,14},{14,12},{1,3},{3,1},... | collective-permute-start | bytes 393224 | tf_op jit(solution)/shard_map/ppermute | solution.py:501
  43.0 0.8 %apply.8.refs_2_ = f32[64,2048]{1,0:T(8,128)S(1)} custom-call(bf16[64,1024]{1,0:T(8,128)(2,1)S(1)} %get-tuple-element.23.refs_0_, bf16[1024,2048]{1,0:T(8,128)(2,1)S(1)} %entries.2.refs_4_.refs_1_), custom_call_target="tpu_custom_call" | custom-call | flops 65536 | bytes 1024 | tf_op jit(solution)/shard_map/apply/pallas_call | solution.py:266
  43.9 2.4 %collective-permute-done.12.refs_0_ = bf16[64,1024]{1,0:T(8,128)(2,1)S(1)} collective-permute-done((bf16[64,1024]{1,0:T(8,128)(2,1)S(1)}, bf16[64,1024]{1,0:T(8,128)(2,1)S(1)}, u32[]{:S(2)}, u32[]{:S(2)}) %collective-permute-start.12) | collective-permute-done | bytes 131104 | tf_op jit(solution)/shard_map/ppermute | solution.py:501
  46.2 0.8 %apply.9.refs_2_ = f32[64,2048]{1,0:T(8,128)S(1)} custom-call(bf16[64,1024]{1,0:T(8,128)(2,1)S(1)} %collective-permute-done.12.refs_0_, bf16[1024,2048]{1,0:T(8,128)(2,1)S(1)} %get-tuple-element.19.refs_7_.refs_1_, f32[64,2048]{1,0:T(8,128)S(1)} %apply.8.refs_2_), custom_call_target="tpu_custom_call" | custom-call | flops 65536 | bytes 1024 | tf_op jit(solution)/shard_map/apply/pallas_call | solution.py:266
  47.1 0.2 collective-permute-done.11.refs_0_
  47.3 0.8 %apply.10.refs_2_ = f32[64,2048]{1,0:T(8,128)S(1)} custom-call(bf16[64,1024]{1,0:T(8,128)(2,1)S(1)} %collective-permute-done.11.refs_0_, bf16[1024,2048]{1,0:T(8,128)(2,1)S(1)} %get-tuple-element.18.refs_6_.refs_1_, f32[64,2048]{1,0:T(8,128)S(1)} %apply.9.refs_2_), custom_call_target="tpu_custom_call" | custom-call | flops 65536 | bytes 1024 | tf_op jit(solution)/shard_map/apply/pallas_call | solution.py:266
  48.1 0.0 collective-permute-done.10.refs_0_
  48.1 0.8 %apply.11.own_ref = f32[64,2048]{1,0:T(8,128)S(1)} custom-call(bf16[64,1024]{1,0:T(8,128)(2,1)S(1)} %collective-permute-done.10.refs_0_, bf16[1024,2048]{1,0:T(8,128)(2,1)S(1)} %get-tuple-element.17.refs_5_.refs_1_, f32[64,2048]{1,0:T(8,128)S(1)} %apply.10.refs_2_), custom_call_target="tpu_custom_call" | custom-call | flops 65536 | bytes 1024 | tf_op jit(solution)/shard_map/apply/pallas_call | solution.py:266
  49.0 0.1 collective-permute-start.13
  49.1 1.5 %collective-permute-done.13.other_ref = f32[64,1024]{1,0:T(8,128)S(1)} collective-permute-done((f32[64,1024]{1,0:T(8,128)S(1)}, f32[64,1024]{1,0:T(8,128)S(1)}, u32[]{:S(2)}, u32[]{:S(2)}) %collective-permute-start.13) | collective-permute-done | bytes 262176 | tf_op jit(solution)/shard_map/ppermute | solution.py:504
  50.6 0.4 second_gram.1
  51.1 0.1 collective-permute-start.14
  51.2 0.4 first_state.1.refs_5_
  51.6 0.6 collective-permute-done.14
  52.3 2.0 %collective-permute-start.17 = (f32[32,128]{1,0:T(8,128)S(1)}, f32[32,128]{1,0:T(8,128)S(1)}, u32[]{:S(2)}, u32[]{:S(2)}) collective-permute-start(f32[32,128]{1,0:T(8,128)S(1)} %add.75.refs_0_), channel_id=1, source_target_pairs={{0,6},{2,4},{4,2},{6,0},{8,14},{10,12},{12,10},{14,8},{1,7},{3,5},... | collective-permute-start | bytes 49160 | tf_op jit(solution)/shard_map/ppermute | solution.py:501
  54.3 0.4 collective-permute-start.16
  54.6 1.1 %collective-permute-start.15 = (f32[32,128]{1,0:T(8,128)S(1)}, f32[32,128]{1,0:T(8,128)S(1)}, u32[]{:S(2)}, u32[]{:S(2)}) collective-permute-start(f32[32,128]{1,0:T(8,128)S(1)} %add.75.refs_0_), channel_id=1, source_target_pairs={{0,2},{2,0},{4,6},{6,4},{8,10},{10,8},{12,14},{14,12},{1,3},{3,1},... | collective-permute-start | bytes 49160 | tf_op jit(solution)/shard_map/ppermute | solution.py:501
  55.8 1.1 %collective-permute-done.17.refs_3_ = f32[32,128]{1,0:T(8,128)S(1)} collective-permute-done((f32[32,128]{1,0:T(8,128)S(1)}, f32[32,128]{1,0:T(8,128)S(1)}, u32[]{:S(2)}, u32[]{:S(2)}) %collective-permute-start.17) | collective-permute-done | bytes 16416 | tf_op jit(solution)/shard_map/ppermute | solution.py:501
  56.9 1.1 %collective-permute-done.16.refs_2_ = f32[32,128]{1,0:T(8,128)S(1)} collective-permute-done((f32[32,128]{1,0:T(8,128)S(1)}, f32[32,128]{1,0:T(8,128)S(1)}, u32[]{:S(2)}, u32[]{:S(2)}) %collective-permute-start.16) | collective-permute-done | bytes 16416 | tf_op jit(solution)/shard_map/ppermute | solution.py:501
  58.0 0.4 collective-permute-done.15.refs_1_
  58.4 3.6 %last_update.1 = (f32[64,512]{1,0:T(8,128)}, f32[64,512]{1,0:T(8,128)}) custom-call(f32[32,128]{1,0:T(8,128)S(1)} %add.75.refs_0_, f32[32,128]{1,0:T(8,128)S(1)} %collective-permute-done.15.refs_1_, f32[32,128]{1,0:T(8,128)S(1)} %collective-permute-done.16.refs_2_, f32[32,128]{1,0:T(8,128)S(1)} %collective-permute-done.17.refs_3_, ...), custom_call_target="tpu_custom_call" | custom-call | flops 75497472 | bytes 786432 | tf_op jit(solution)/shard_map/last_update/pallas_call | solution.py:478
  (12 shorter events, 0.1 us)
Async XLA Ops:
  0.6 13.4 %collective-permute-start.1 = (f32[1,512]{1,0:T(1,128)}, f32[1,512]{1,0:T(1,128)S(1)}, u32[]{:S(2)}, u32[]{:S(2)}) collective-permute-start(f32[1,512]{1,0:T(1,128)} %bitcast.24), channel_id=1, source_target_pairs={{0,8},{2,10},{4,12},{6,14},{8,0},{10,2},{12,4},{14,6},{1,9},{3,11}... | collective-permute-start | bytes 6152 | tf_op jit(solution)/shard_map/ppermute | solution.py:501
  4.7 9.3 %collective-permute-start = (f32[64,512]{1,0:T(8,128)}, f32[64,512]{1,0:T(8,128)S(1)}, u32[]{:S(2)}, u32[]{:S(2)}) collective-permute-start(f32[64,512]{1,0:T(8,128)} %direction_ref.1), channel_id=1, source_target_pairs={{0,8},{2,10},{4,12},{6,14},{8,0},{10,2},{12,4},{14,6},{1,9},{3,11}... | collective-permute-start | bytes 393224 | tf_op jit(solution)/shard_map/ppermute | solution.py:501
  12.2 1.9 %copy-start = (f32[64,512]{1,0:T(8,128)S(1)}, f32[64,512]{1,0:T(8,128)}, u32[]{:S(2)}) copy-start(f32[64,512]{1,0:T(8,128)} %direction_ref.1) | copy-start | bytes 393220
  14.1 8.6 %collective-permute-start.4 = (bf16[64,1024]{1,0:T(8,128)(2,1)S(1)}, bf16[64,1024]{1,0:T(8,128)(2,1)S(1)}, u32[]{:S(2)}, u32[]{:S(2)}) collective-permute-start(bf16[64,1024]{1,0:T(8,128)(2,1)S(1)} %get-tuple-element.28.refs_0_), channel_id=1, source_target_pairs={{0,6},{2,4},{4,2},{6,0},{8,14},{10,12},{12,10},{14,8},{1,7},{3,5},... | collective-permute-start | bytes 393224 | tf_op jit(solution)/shard_map/ppermute | solution.py:501
  17.0 5.9 %collective-permute-start.3 = (bf16[64,1024]{1,0:T(8,128)(2,1)S(1)}, bf16[64,1024]{1,0:T(8,128)(2,1)S(1)}, u32[]{:S(2)}, u32[]{:S(2)}) collective-permute-start(bf16[64,1024]{1,0:T(8,128)(2,1)S(1)} %get-tuple-element.28.refs_0_), channel_id=1, source_target_pairs={{0,4},{2,6},{4,0},{6,2},{8,12},{10,14},{12,8},{14,10},{1,5},{3,7},... | collective-permute-start | bytes 393224 | tf_op jit(solution)/shard_map/ppermute | solution.py:501
  17.4 5.5 %collective-permute-start.2 = (bf16[64,1024]{1,0:T(8,128)(2,1)S(1)}, bf16[64,1024]{1,0:T(8,128)(2,1)S(1)}, u32[]{:S(2)}, u32[]{:S(2)}) collective-permute-start(bf16[64,1024]{1,0:T(8,128)(2,1)S(1)} %get-tuple-element.28.refs_0_), channel_id=1, source_target_pairs={{0,2},{2,0},{4,6},{6,4},{8,10},{10,8},{12,14},{14,12},{1,3},{3,1},... | collective-permute-start | bytes 393224 | tf_op jit(solution)/shard_map/ppermute | solution.py:501
  23.0 1.7 %copy-start.1 = (f32[512]{0:T(512)S(1)}, f32[512]{0:T(512)}, u32[]{:S(2)}) copy-start(f32[512]{0:T(512)} %param.9) | copy-start | bytes 6148
  24.5 1.7 %collective-permute-start.5 = (f32[64,1024]{1,0:T(8,128)S(1)}, f32[64,1024]{1,0:T(8,128)S(1)}, u32[]{:S(2)}, u32[]{:S(2)}) collective-permute-start(f32[64,1024]{1,0:T(8,128)S(1)} %apply.7), channel_id=1, source_target_pairs={{0,1},{1,0},{2,3},{3,2},{4,5},{5,4},{6,7},{7,6},{8,9},{9,8},{10,11... | collective-permute-start | bytes 786440 | tf_op jit(solution)/shard_map/ppermute | solution.py:504
  27.1 1.4 %collective-permute-start.6 = (f32[96,128]{1,0:T(8,128)S(1)}, f32[96,128]{1,0:T(8,128)S(1)}, u32[]{:S(2)}, u32[]{:S(2)}) collective-permute-start(f32[96,128]{1,0:T(8,128)S(1)} %get-tuple-element.21), channel_id=1, source_target_pairs={{0,1},{1,0},{2,3},{3,2},{4,5},{5,4},{6,7},{7,6},{8,9},{9,8},{10,11... | collective-permute-start | bytes 147464 | tf_op jit(solution)/shard_map/ppermute | solution.py:504
  28.5 5.0 %collective-permute-start.9 = (f32[96,128]{1,0:T(8,128)S(1)}, f32[96,128]{1,0:T(8,128)S(1)}, u32[]{:S(2)}, u32[]{:S(2)}) collective-permute-start(f32[96,128]{1,0:T(8,128)S(1)} %add.74.refs_0_), channel_id=1, source_target_pairs={{0,6},{2,4},{4,2},{6,0},{8,14},{10,12},{12,10},{14,8},{1,7},{3,5},... | collective-permute-start | bytes 147464 | tf_op jit(solution)/shard_map/ppermute | solution.py:501
  31.1 4.1 %collective-permute-start.8 = (f32[96,128]{1,0:T(8,128)S(1)}, f32[96,128]{1,0:T(8,128)S(1)}, u32[]{:S(2)}, u32[]{:S(2)}) collective-permute-start(f32[96,128]{1,0:T(8,128)S(1)} %add.74.refs_0_), channel_id=1, source_target_pairs={{0,4},{2,6},{4,0},{6,2},{8,12},{10,14},{12,8},{14,10},{1,5},{3,7},... | collective-permute-start | bytes 147464 | tf_op jit(solution)/shard_map/ppermute | solution.py:501
  31.5 4.1 %collective-permute-start.7 = (f32[96,128]{1,0:T(8,128)S(1)}, f32[96,128]{1,0:T(8,128)S(1)}, u32[]{:S(2)}, u32[]{:S(2)}) collective-permute-start(f32[96,128]{1,0:T(8,128)S(1)} %add.74.refs_0_), channel_id=1, source_target_pairs={{0,2},{2,0},{4,6},{6,4},{8,10},{10,8},{12,14},{14,12},{1,3},{3,1},... | collective-permute-start | bytes 147464 | tf_op jit(solution)/shard_map/ppermute | solution.py:501
  39.5 6.8 %collective-permute-start.12 = (bf16[64,1024]{1,0:T(8,128)(2,1)S(1)}, bf16[64,1024]{1,0:T(8,128)(2,1)S(1)}, u32[]{:S(2)}, u32[]{:S(2)}) collective-permute-start(bf16[64,1024]{1,0:T(8,128)(2,1)S(1)} %get-tuple-element.23.refs_0_), channel_id=1, source_target_pairs={{0,6},{2,4},{4,2},{6,0},{8,14},{10,12},{12,10},{14,8},{1,7},{3,5},... | collective-permute-start | bytes 393224 | tf_op jit(solution)/shard_map/ppermute | solution.py:501
  41.1 6.2 %collective-permute-start.11 = (bf16[64,1024]{1,0:T(8,128)(2,1)S(1)}, bf16[64,1024]{1,0:T(8,128)(2,1)S(1)}, u32[]{:S(2)}, u32[]{:S(2)}) collective-permute-start(bf16[64,1024]{1,0:T(8,128)(2,1)S(1)} %get-tuple-element.23.refs_0_), channel_id=1, source_target_pairs={{0,4},{2,6},{4,0},{6,2},{8,12},{10,14},{12,8},{14,10},{1,5},{3,7},... | collective-permute-start | bytes 393224 | tf_op jit(solution)/shard_map/ppermute | solution.py:501
  41.5 6.6 %collective-permute-start.10 = (bf16[64,1024]{1,0:T(8,128)(2,1)S(1)}, bf16[64,1024]{1,0:T(8,128)(2,1)S(1)}, u32[]{:S(2)}, u32[]{:S(2)}) collective-permute-start(bf16[64,1024]{1,0:T(8,128)(2,1)S(1)} %get-tuple-element.23.refs_0_), channel_id=1, source_target_pairs={{0,2},{2,0},{4,6},{6,4},{8,10},{10,8},{12,14},{14,12},{1,3},{3,1},... | collective-permute-start | bytes 393224 | tf_op jit(solution)/shard_map/ppermute | solution.py:501
  49.0 1.6 %collective-permute-start.13 = (f32[64,1024]{1,0:T(8,128)S(1)}, f32[64,1024]{1,0:T(8,128)S(1)}, u32[]{:S(2)}, u32[]{:S(2)}) collective-permute-start(f32[64,1024]{1,0:T(8,128)S(1)} %slice.30), channel_id=1, source_target_pairs={{0,1},{1,0},{2,3},{3,2},{4,5},{5,4},{6,7},{7,6},{8,9},{9,8},{10,11... | collective-permute-start | bytes 786440 | tf_op jit(solution)/shard_map/ppermute | solution.py:504
  51.1 1.2 %collective-permute-start.14 = (f32[32,128]{1,0:T(8,128)S(1)}, f32[32,128]{1,0:T(8,128)S(1)}, u32[]{:S(2)}, u32[]{:S(2)}) collective-permute-start(f32[32,128]{1,0:T(8,128)S(1)} %get-tuple-element.25), channel_id=1, source_target_pairs={{0,1},{1,0},{2,3},{3,2},{4,5},{5,4},{6,7},{7,6},{8,9},{9,8},{10,11... | collective-permute-start | bytes 49160 | tf_op jit(solution)/shard_map/ppermute | solution.py:504
  52.3 4.6 %collective-permute-start.17 = (f32[32,128]{1,0:T(8,128)S(1)}, f32[32,128]{1,0:T(8,128)S(1)}, u32[]{:S(2)}, u32[]{:S(2)}) collective-permute-start(f32[32,128]{1,0:T(8,128)S(1)} %add.75.refs_0_), channel_id=1, source_target_pairs={{0,6},{2,4},{4,2},{6,0},{8,14},{10,12},{12,10},{14,8},{1,7},{3,5},... | collective-permute-start | bytes 49160 | tf_op jit(solution)/shard_map/ppermute | solution.py:501
  54.3 3.7 %collective-permute-start.16 = (f32[32,128]{1,0:T(8,128)S(1)}, f32[32,128]{1,0:T(8,128)S(1)}, u32[]{:S(2)}, u32[]{:S(2)}) collective-permute-start(f32[32,128]{1,0:T(8,128)S(1)} %add.75.refs_0_), channel_id=1, source_target_pairs={{0,4},{2,6},{4,0},{6,2},{8,12},{10,14},{12,8},{14,10},{1,5},{3,7},... | collective-permute-start | bytes 49160 | tf_op jit(solution)/shard_map/ppermute | solution.py:501
  54.6 3.7 %collective-permute-start.15 = (f32[32,128]{1,0:T(8,128)S(1)}, f32[32,128]{1,0:T(8,128)S(1)}, u32[]{:S(2)}, u32[]{:S(2)}) collective-permute-start(f32[32,128]{1,0:T(8,128)S(1)} %add.75.refs_0_), channel_id=1, source_target_pairs={{0,2},{2,0},{4,6},{6,4},{8,10},{10,8},{12,14},{14,12},{1,3},{3,1},... | collective-permute-start | bytes 49160 | tf_op jit(solution)/shard_map/ppermute | solution.py:501

commit v6 on v5

--- a/solution.py
+++ b/solution.py
@@ -216,7 +216,7 @@
     source_rows[...] = features(source_ref[...], True).T
     target_cols[...] = features(target_ref[...], False)
     n_out, m = out_refs[0].shape
-    step, wide = 512, min(m, 1024)
+    step, wide = min(n_out, 1024), min(m, 1024)
     for piece, out_ref in enumerate(out_refs):
 
         def one(i, carry, piece=piece, out_ref=out_ref):

time: 62.1 us -> 61.8 us (level)
  Pallas kernels: 28.6 us -> 27 us
  waiting for transfers between devices: 12 us -> 13.3 us
    pallas_call x2, Pallas kernels: 6.82 us -> 4.99 us  [entries(): pl.pallas_call(entry_kernel, out_shape=[jax.ShapeDtypeStruct((n // pieces...]
    ppermute x14, waiting for transfers between devices: 9 us -> 10.3 us  [swap(): return lax.ppermute(value, 'tgt', [(i, i ^ bits) for i in range(n_tgt)])]
  transfers between devices with their start and end apart: 18 -> 18, of which waited for: 12 -> 13; matrix products, arithmetic and copies ran while one was open for 2% -> 2% of each run, Pallas kernels for 28% -> 25%
where the time goes in v6:
time: 61.8 us; the launch traced here: 61.6 us
  Pallas kernels  27 us (44%)
  starting transfers between devices  19.1 us (31%)
  waiting for transfers between devices  13.3 us (22%)
  local copies, waits for them, and re-layouts  1.09 us (2%)
  between operations  0.89 us (1%)
    ppermute x14, starting transfers between devices, swap(): return lax.ppermute(value, 'tgt', [(i, i ^ bits) for i in range(n_tgt)])  18.3 us
    ppermute x14, waiting for transfers between devices, swap(): return lax.ppermute(value, 'tgt', [(i, i ^ bits) for i in range(n_tgt)])  10.3 us
    pallas_call x6, Pallas kernels, apply_entries(): pl.pallas_call(functools.partial(apply_kernel, pieces=pieces, more=bool(m...  6.51 us
    pallas_call x1, Pallas kernels, chosen_positions(): pl.pallas_call(functools.partial(position_kernel, chunk=chunk, count=coun...  6.1 us
    pallas_call x2, Pallas kernels, entries(): pl.pallas_call(entry_kernel, out_shape=[jax.ShapeDtypeStruct((n // pieces...  4.99 us
    pallas_call x1, Pallas kernels, first_update(): pl.pallas_call(functools.partial(first_update_kernel, count=len(parts)),...  3.85 us
    pallas_call x1, Pallas kernels, last_update(): pl.pallas_call(functools.partial(last_update_kernel, count=len(parts)), o...  3.57 us
    ppermute x4, waiting for transfers between devices, swap_core(): return lax.ppermute(value, 'src', [(0, 1), (1, 0)])  2.98 us
  transfers between devices with their start and end apart: 18, of which 13 were waited for; matrix products, arithmetic and copies ran while one was open for 2% of the time, Pallas kernels for 25%

profile of v6, /device:TPU:0, one launch (start us, length us, event | category | flops | bytes accessed | tf_op | source)
XLA Modules:
  0.0 61.6 jit_solution(5735000342358269150)
XLA Ops:
  0.6 4.1 %collective-permute-start.1 = (f32[1,512]{1,0:T(1,128)}, f32[1,512]{1,0:T(1,128)S(1)}, u32[]{:S(2)}, u32[]{:S(2)}) collective-permute-start(f32[1,512]{1,0:T(1,128)} %bitcast.24), channel_id=1, source_target_pairs={{0,8},{2,10},{4,12},{6,14},{8,0},{10,2},{12,4},{14,6},{1,9},{3,11}... | collective-permute-start | bytes 6152 | tf_op jit(solution)/shard_map/ppermute | solution.py:501
  4.7 0.1 collective-permute-start
  4.8 0.8 %copy.12 = f32[1,2,64,128]{3,2,1,0:T(8,128)S(1)} copy(f32[1,2,64,128]{3,1,2,0:T(2,128)} %bitcast.23) | data formatting | bytes 131072
  5.7 0.2 cosine_multiply_fusion
  5.9 0.1 copy.11
  6.0 0.1 stack.49.starts
  6.1 6.1 %positions.1 = f32[3,5120]{1,0:T(4,128)S(1)} custom-call(s32[10]{0:T(128)S(1)} %stack.49.starts, f32[3,40000]{1,0:T(4,128)} %table_hbm.1, s32[1,8192]{1,0:T(1,128)} %bitcast.26, f32[3,8192]{1,0:T(4,128)S(1)} %bitcast.20), custom_call_target="tpu_custom_call" | custom-call | flops 3774873600 | bytes 480000 | tf_op jit(solution)/shard_map/positions/pallas_call | solution.py:170
  12.2 0.0 copy-start
  12.2 1.4 %entries.2.refs_4_.refs_1_ = bf16[1024,2048]{1,0:T(8,128)(2,1)S(1)} custom-call(f32[3,1024]{1,0:T(4,128)S(1)} %get-tuple-element.31.source_ref, f32[3,2048]{1,0:T(4,128)S(1)} %pad_maximum_fusion.1.target_ref), custom_call_target="tpu_custom_call" | custom-call | flops 25165824 | bytes 4194304 | tf_op jit(solution)/shard_map/entries/pallas_call | solution.py:236
  13.6 0.0 collective-permute-done.1
  13.7 0.0 collective-permute-done
  13.7 0.0 copy-done
  13.7 2.9 %collective-permute-start.4 = (bf16[64,1024]{1,0:T(8,128)(2,1)S(1)}, bf16[64,1024]{1,0:T(8,128)(2,1)S(1)}, u32[]{:S(2)}, u32[]{:S(2)}) collective-permute-start(bf16[64,1024]{1,0:T(8,128)(2,1)S(1)} %get-tuple-element.28.refs_0_), channel_id=1, source_target_pairs={{0,6},{2,4},{4,2},{6,0},{8,14},{10,12},{12,10},{14,8},{1,7},{3,5},... | collective-permute-start | bytes 393224 | tf_op jit(solution)/shard_map/ppermute | solution.py:501
  16.6 0.4 collective-permute-start.3
  17.0 0.3 collective-permute-start.2
  17.3 3.6 %entries.3 = (bf16[1024,2048]{1,0:T(8,128)(2,1)S(1)}, bf16[1024,2048]{1,0:T(8,128)(2,1)S(1)}, bf16[1024,2048]{1,0:T(8,128)(2,1)S(1)}) custom-call(f32[3,3072]{1,0:T(4,128)S(1)} %slice.29.source_ref, f32[3,2048]{1,0:T(4,128)S(1)} %pad_maximum_fusion.1.target_ref), custom_call_target="tpu_custom_call" | custom-call | flops 75497472 | bytes 12582912 | tf_op jit(solution)/shard_map/entries/pallas_call | solution.py:236
  20.9 0.3 collective-permute-done.4.refs_3_
  21.1 1.4 %collective-permute-done.3.refs_2_ = bf16[64,1024]{1,0:T(8,128)(2,1)S(1)} collective-permute-done((bf16[64,1024]{1,0:T(8,128)(2,1)S(1)}, bf16[64,1024]{1,0:T(8,128)(2,1)S(1)}, u32[]{:S(2)}, u32[]{:S(2)}) %collective-permute-start.3) | collective-permute-done | bytes 131104 | tf_op jit(solution)/shard_map/ppermute | solution.py:501
  22.5 0.0 collective-permute-done.2.refs_1_
  22.5 0.0 copy-start.1
  22.5 1.6 %apply.7 = f32[64,1024]{1,0:T(8,128)S(1)} custom-call(bf16[64,1024]{1,0:T(8,128)(2,1)S(1)} %get-tuple-element.28.refs_0_, bf16[64,1024]{1,0:T(8,128)(2,1)S(1)} %collective-permute-done.2.refs_1_, bf16[64,1024]{1,0:T(8,128)(2,1)S(1)} %collective-permute-done.3.refs_2_, bf16[64,1024]{1,0:T(8,128)(2,1)S(1)} %collective-permute-done.4.refs_3_, ...), custom_call_target="tpu_custom_call" | custom-call | flops 65536 | bytes 1024 | tf_op jit(solution)/shard_map/apply/pallas_call | solution.py:266
  24.1 0.1 collective-permute-start.5
  24.2 0.0 copy-done.1
  24.2 1.6 %apply.6.own_ref = f32[64,1024]{1,0:T(8,128)S(1)} custom-call(bf16[64,1024]{1,0:T(8,128)(2,1)S(1)} %get-tuple-element.28.refs_0_, bf16[64,1024]{1,0:T(8,128)(2,1)S(1)} %collective-permute-done.2.refs_1_, bf16[64,1024]{1,0:T(8,128)(2,1)S(1)} %collective-permute-done.3.refs_2_, bf16[64,1024]{1,0:T(8,128)(2,1)S(1)} %collective-permute-done.4.refs_3_, ...), custom_call_target="tpu_custom_call" | custom-call | flops 65536 | bytes 1024 | tf_op jit(solution)/shard_map/apply/pallas_call | solution.py:266
  25.8 0.0 collective-permute-done.5.other_ref
  25.8 1.1 %first_gram.1 = (f32[64,1024]{1,0:T(8,128)S(1)}, f32[96,128]{1,0:T(8,128)S(1)}) custom-call(f32[64,1024]{1,0:T(8,128)S(1)} %apply.6.own_ref, f32[64,1024]{1,0:T(8,128)S(1)} %collective-permute-done.5.other_ref, f32[1,1024]{1,0:T(1,128)S(1)} %broadcast_select_fusion.self_ref, f32[64,1024]{1,0:T(8,128)S(1)} %get-tuple-element.29.direction_ref.refs_5_), custom_call_target="tpu_custom_call" | custom-call | flops 150994944 | bytes 1048576 | tf_op jit(solution)/shard_map/first_gram/pallas_call | solution.py:358
  26.9 0.6 collective-permute-start.6
  27.4 0.9 %collective-permute-done.6 = f32[96,128]{1,0:T(8,128)S(1)} collective-permute-done((f32[96,128]{1,0:T(8,128)S(1)}, f32[96,128]{1,0:T(8,128)S(1)}, u32[]{:S(2)}, u32[]{:S(2)}) %collective-permute-start.6) | collective-permute-done | bytes 49184 | tf_op jit(solution)/shard_map/ppermute | solution.py:504
  28.3 2.4 %collective-permute-start.9 = (f32[96,128]{1,0:T(8,128)S(1)}, f32[96,128]{1,0:T(8,128)S(1)}, u32[]{:S(2)}, u32[]{:S(2)}) collective-permute-start(f32[96,128]{1,0:T(8,128)S(1)} %add.74.refs_0_), channel_id=1, source_target_pairs={{0,6},{2,4},{4,2},{6,0},{8,14},{10,12},{12,10},{14,8},{1,7},{3,5},... | collective-permute-start | bytes 147464 | tf_op jit(solution)/shard_map/ppermute | solution.py:501
  30.8 0.4 collective-permute-start.8
  31.2 0.6 %collective-permute-start.7 = (f32[96,128]{1,0:T(8,128)S(1)}, f32[96,128]{1,0:T(8,128)S(1)}, u32[]{:S(2)}, u32[]{:S(2)}) collective-permute-start(f32[96,128]{1,0:T(8,128)S(1)} %add.74.refs_0_), channel_id=1, source_target_pairs={{0,2},{2,0},{4,6},{6,4},{8,10},{10,8},{12,14},{14,12},{1,3},{3,1},... | collective-permute-start | bytes 147464 | tf_op jit(solution)/shard_map/ppermute | solution.py:501
  31.8 1.5 %collective-permute-done.9.refs_3_ = f32[96,128]{1,0:T(8,128)S(1)} collective-permute-done((f32[96,128]{1,0:T(8,128)S(1)}, f32[96,128]{1,0:T(8,128)S(1)}, u32[]{:S(2)}, u32[]{:S(2)}) %collective-permute-start.9) | collective-permute-done | bytes 49184 | tf_op jit(solution)/shard_map/ppermute | solution.py:501
  33.3 1.5 %collective-permute-done.8.refs_2_ = f32[96,128]{1,0:T(8,128)S(1)} collective-permute-done((f32[96,128]{1,0:T(8,128)S(1)}, f32[96,128]{1,0:T(8,128)S(1)}, u32[]{:S(2)}, u32[]{:S(2)}) %collective-permute-start.8) | collective-permute-done | bytes 49184 | tf_op jit(solution)/shard_map/ppermute | solution.py:501
  34.9 0.4 collective-permute-done.7.refs_1_
  35.3 3.8 %first_update.1 = (f32[64,128]{1,0:T(8,128)S(1)}, f32[64,1024]{1,0:T(8,128)S(1)}, bf16[64,1024]{1,0:T(8,128)(2,1)S(1)}) custom-call(f32[96,128]{1,0:T(8,128)S(1)} %add.74.refs_0_, f32[96,128]{1,0:T(8,128)S(1)} %collective-permute-done.7.refs_1_, f32[96,128]{1,0:T(8,128)S(1)} %collective-permute-done.8.refs_2_, f32[96,128]{1,0:T(8,128)S(1)} %collective-permute-done.9.refs_3_, ...), custom_call_target="tpu_custom_call" | custom-call | flops 100663296 | bytes 1310720 | tf_op jit(solution)/shard_map/first_update/pallas_call | solution.py:402
  39.1 1.7 %collective-permute-start.12 = (bf16[64,1024]{1,0:T(8,128)(2,1)S(1)}, bf16[64,1024]{1,0:T(8,128)(2,1)S(1)}, u32[]{:S(2)}, u32[]{:S(2)}) collective-permute-start(bf16[64,1024]{1,0:T(8,128)(2,1)S(1)} %get-tuple-element.23.refs_0_), channel_id=1, source_target_pairs={{0,6},{2,4},{4,2},{6,0},{8,14},{10,12},{12,10},{14,8},{1,7},{3,5},... | collective-permute-start | bytes 393224 | tf_op jit(solution)/shard_map/ppermute | solution.py:501
  40.9 0.4 collective-permute-start.11
  41.3 1.4 %collective-permute-start.10 = (bf16[64,1024]{1,0:T(8,128)(2,1)S(1)}, bf16[64,1024]{1,0:T(8,128)(2,1)S(1)}, u32[]{:S(2)}, u32[]{:S(2)}) collective-permute-start(bf16[64,1024]{1,0:T(8,128)(2,1)S(1)} %get-tuple-element.23.refs_0_), channel_id=1, source_target_pairs={{0,2},{2,0},{4,6},{6,4},{8,10},{10,8},{12,14},{14,12},{1,3},{3,1},... | collective-permute-start | bytes 393224 | tf_op jit(solution)/shard_map/ppermute | solution.py:501
  42.7 0.8 %apply.8.refs_2_ = f32[64,2048]{1,0:T(8,128)S(1)} custom-call(bf16[64,1024]{1,0:T(8,128)(2,1)S(1)} %get-tuple-element.23.refs_0_, bf16[1024,2048]{1,0:T(8,128)(2,1)S(1)} %entries.2.refs_4_.refs_1_), custom_call_target="tpu_custom_call" | custom-call | flops 65536 | bytes 1024 | tf_op jit(solution)/shard_map/apply/pallas_call | solution.py:266
  43.5 2.4 %collective-permute-done.12.refs_0_ = bf16[64,1024]{1,0:T(8,128)(2,1)S(1)} collective-permute-done((bf16[64,1024]{1,0:T(8,128)(2,1)S(1)}, bf16[64,1024]{1,0:T(8,128)(2,1)S(1)}, u32[]{:S(2)}, u32[]{:S(2)}) %collective-permute-start.12) | collective-permute-done | bytes 131104 | tf_op jit(solution)/shard_map/ppermute | solution.py:501
  46.0 0.8 %apply.9.refs_2_ = f32[64,2048]{1,0:T(8,128)S(1)} custom-call(bf16[64,1024]{1,0:T(8,128)(2,1)S(1)} %collective-permute-done.12.refs_0_, bf16[1024,2048]{1,0:T(8,128)(2,1)S(1)} %get-tuple-element.19.refs_7_.refs_1_, f32[64,2048]{1,0:T(8,128)S(1)} %apply.8.refs_2_), custom_call_target="tpu_custom_call" | custom-call | flops 65536 | bytes 1024 | tf_op jit(solution)/shard_map/apply/pallas_call | solution.py:266
  46.8 0.1 collective-permute-done.11.refs_0_
  46.9 0.8 %apply.10.refs_2_ = f32[64,2048]{1,0:T(8,128)S(1)} custom-call(bf16[64,1024]{1,0:T(8,128)(2,1)S(1)} %collective-permute-done.11.refs_0_, bf16[1024,2048]{1,0:T(8,128)(2,1)S(1)} %get-tuple-element.18.refs_6_.refs_1_, f32[64,2048]{1,0:T(8,128)S(1)} %apply.9.refs_2_), custom_call_target="tpu_custom_call" | custom-call | flops 65536 | bytes 1024 | tf_op jit(solution)/shard_map/apply/pallas_call | solution.py:266
  47.8 0.0 collective-permute-done.10.refs_0_
  47.8 0.8 %apply.11.own_ref = f32[64,2048]{1,0:T(8,128)S(1)} custom-call(bf16[64,1024]{1,0:T(8,128)(2,1)S(1)} %collective-permute-done.10.refs_0_, bf16[1024,2048]{1,0:T(8,128)(2,1)S(1)} %get-tuple-element.17.refs_5_.refs_1_, f32[64,2048]{1,0:T(8,128)S(1)} %apply.10.refs_2_), custom_call_target="tpu_custom_call" | custom-call | flops 65536 | bytes 1024 | tf_op jit(solution)/shard_map/apply/pallas_call | solution.py:266
  48.7 0.1 collective-permute-start.13
  48.8 1.5 %collective-permute-done.13.other_ref = f32[64,1024]{1,0:T(8,128)S(1)} collective-permute-done((f32[64,1024]{1,0:T(8,128)S(1)}, f32[64,1024]{1,0:T(8,128)S(1)}, u32[]{:S(2)}, u32[]{:S(2)}) %collective-permute-start.13) | collective-permute-done | bytes 262176 | tf_op jit(solution)/shard_map/ppermute | solution.py:504
  50.3 0.4 second_gram.1
  50.7 0.1 collective-permute-start.14
  50.9 0.4 first_state.1.refs_5_
  51.3 0.6 collective-permute-done.14
  51.9 2.1 %collective-permute-start.17 = (f32[32,128]{1,0:T(8,128)S(1)}, f32[32,128]{1,0:T(8,128)S(1)}, u32[]{:S(2)}, u32[]{:S(2)}) collective-permute-start(f32[32,128]{1,0:T(8,128)S(1)} %add.75.refs_0_), channel_id=1, source_target_pairs={{0,6},{2,4},{4,2},{6,0},{8,14},{10,12},{12,10},{14,8},{1,7},{3,5},... | collective-permute-start | bytes 49160 | tf_op jit(solution)/shard_map/ppermute | solution.py:501
  54.0 0.3 collective-permute-start.16
  54.3 1.1 %collective-permute-start.15 = (f32[32,128]{1,0:T(8,128)S(1)}, f32[32,128]{1,0:T(8,128)S(1)}, u32[]{:S(2)}, u32[]{:S(2)}) collective-permute-start(f32[32,128]{1,0:T(8,128)S(1)} %add.75.refs_0_), channel_id=1, source_target_pairs={{0,2},{2,0},{4,6},{6,4},{8,10},{10,8},{12,14},{14,12},{1,3},{3,1},... | collective-permute-start | bytes 49160 | tf_op jit(solution)/shard_map/ppermute | solution.py:501
  55.4 1.1 %collective-permute-done.17.refs_3_ = f32[32,128]{1,0:T(8,128)S(1)} collective-permute-done((f32[32,128]{1,0:T(8,128)S(1)}, f32[32,128]{1,0:T(8,128)S(1)}, u32[]{:S(2)}, u32[]{:S(2)}) %collective-permute-start.17) | collective-permute-done | bytes 16416 | tf_op jit(solution)/shard_map/ppermute | solution.py:501
  56.6 1.2 %collective-permute-done.16.refs_2_ = f32[32,128]{1,0:T(8,128)S(1)} collective-permute-done((f32[32,128]{1,0:T(8,128)S(1)}, f32[32,128]{1,0:T(8,128)S(1)}, u32[]{:S(2)}, u32[]{:S(2)}) %collective-permute-start.16) | collective-permute-done | bytes 16416 | tf_op jit(solution)/shard_map/ppermute | solution.py:501
  57.7 0.3 collective-permute-done.15.refs_1_
  58.1 3.6 %last_update.1 = (f32[64,512]{1,0:T(8,128)}, f32[64,512]{1,0:T(8,128)}) custom-call(f32[32,128]{1,0:T(8,128)S(1)} %add.75.refs_0_, f32[32,128]{1,0:T(8,128)S(1)} %collective-permute-done.15.refs_1_, f32[32,128]{1,0:T(8,128)S(1)} %collective-permute-done.16.refs_2_, f32[32,128]{1,0:T(8,128)S(1)} %collective-permute-done.17.refs_3_, ...), custom_call_target="tpu_custom_call" | custom-call | flops 75497472 | bytes 786432 | tf_op jit(solution)/shard_map/last_update/pallas_call | solution.py:478
  (12 shorter events, 0.1 us)
Async XLA Ops:
  0.6 13.0 %collective-permute-start.1 = (f32[1,512]{1,0:T(1,128)}, f32[1,512]{1,0:T(1,128)S(1)}, u32[]{:S(2)}, u32[]{:S(2)}) collective-permute-start(f32[1,512]{1,0:T(1,128)} %bitcast.24), channel_id=1, source_target_pairs={{0,8},{2,10},{4,12},{6,14},{8,0},{10,2},{12,4},{14,6},{1,9},{3,11}... | collective-permute-start | bytes 6152 | tf_op jit(solution)/shard_map/ppermute | solution.py:501
  4.7 8.9 %collective-permute-start = (f32[64,512]{1,0:T(8,128)}, f32[64,512]{1,0:T(8,128)S(1)}, u32[]{:S(2)}, u32[]{:S(2)}) collective-permute-start(f32[64,512]{1,0:T(8,128)} %direction_ref.1), channel_id=1, source_target_pairs={{0,8},{2,10},{4,12},{6,14},{8,0},{10,2},{12,4},{14,6},{1,9},{3,11}... | collective-permute-start | bytes 393224 | tf_op jit(solution)/shard_map/ppermute | solution.py:501
  12.2 1.5 %copy-start = (f32[64,512]{1,0:T(8,128)S(1)}, f32[64,512]{1,0:T(8,128)}, u32[]{:S(2)}) copy-start(f32[64,512]{1,0:T(8,128)} %direction_ref.1) | copy-start | bytes 393220
  13.7 7.4 %collective-permute-start.4 = (bf16[64,1024]{1,0:T(8,128)(2,1)S(1)}, bf16[64,1024]{1,0:T(8,128)(2,1)S(1)}, u32[]{:S(2)}, u32[]{:S(2)}) collective-permute-start(bf16[64,1024]{1,0:T(8,128)(2,1)S(1)} %get-tuple-element.28.refs_0_), channel_id=1, source_target_pairs={{0,6},{2,4},{4,2},{6,0},{8,14},{10,12},{12,10},{14,8},{1,7},{3,5},... | collective-permute-start | bytes 393224 | tf_op jit(solution)/shard_map/ppermute | solution.py:501
  16.6 5.9 %collective-permute-start.3 = (bf16[64,1024]{1,0:T(8,128)(2,1)S(1)}, bf16[64,1024]{1,0:T(8,128)(2,1)S(1)}, u32[]{:S(2)}, u32[]{:S(2)}) collective-permute-start(bf16[64,1024]{1,0:T(8,128)(2,1)S(1)} %get-tuple-element.28.refs_0_), channel_id=1, source_target_pairs={{0,4},{2,6},{4,0},{6,2},{8,12},{10,14},{12,8},{14,10},{1,5},{3,7},... | collective-permute-start | bytes 393224 | tf_op jit(solution)/shard_map/ppermute | solution.py:501
  17.0 5.5 %collective-permute-start.2 = (bf16[64,1024]{1,0:T(8,128)(2,1)S(1)}, bf16[64,1024]{1,0:T(8,128)(2,1)S(1)}, u32[]{:S(2)}, u32[]{:S(2)}) collective-permute-start(bf16[64,1024]{1,0:T(8,128)(2,1)S(1)} %get-tuple-element.28.refs_0_), channel_id=1, source_target_pairs={{0,2},{2,0},{4,6},{6,4},{8,10},{10,8},{12,14},{14,12},{1,3},{3,1},... | collective-permute-start | bytes 393224 | tf_op jit(solution)/shard_map/ppermute | solution.py:501
  22.5 1.7 %copy-start.1 = (f32[512]{0:T(512)S(1)}, f32[512]{0:T(512)}, u32[]{:S(2)}) copy-start(f32[512]{0:T(512)} %param.9) | copy-start | bytes 6148
  24.1 1.7 %collective-permute-start.5 = (f32[64,1024]{1,0:T(8,128)S(1)}, f32[64,1024]{1,0:T(8,128)S(1)}, u32[]{:S(2)}, u32[]{:S(2)}) collective-permute-start(f32[64,1024]{1,0:T(8,128)S(1)} %apply.7), channel_id=1, source_target_pairs={{0,1},{1,0},{2,3},{3,2},{4,5},{5,4},{6,7},{7,6},{8,9},{9,8},{10,11... | collective-permute-start | bytes 786440 | tf_op jit(solution)/shard_map/ppermute | solution.py:504
  26.9 1.4 %collective-permute-start.6 = (f32[96,128]{1,0:T(8,128)S(1)}, f32[96,128]{1,0:T(8,128)S(1)}, u32[]{:S(2)}, u32[]{:S(2)}) collective-permute-start(f32[96,128]{1,0:T(8,128)S(1)} %get-tuple-element.21), channel_id=1, source_target_pairs={{0,1},{1,0},{2,3},{3,2},{4,5},{5,4},{6,7},{7,6},{8,9},{9,8},{10,11... | collective-permute-start | bytes 147464 | tf_op jit(solution)/shard_map/ppermute | solution.py:504
  28.3 5.0 %collective-permute-start.9 = (f32[96,128]{1,0:T(8,128)S(1)}, f32[96,128]{1,0:T(8,128)S(1)}, u32[]{:S(2)}, u32[]{:S(2)}) collective-permute-start(f32[96,128]{1,0:T(8,128)S(1)} %add.74.refs_0_), channel_id=1, source_target_pairs={{0,6},{2,4},{4,2},{6,0},{8,14},{10,12},{12,10},{14,8},{1,7},{3,5},... | collective-permute-start | bytes 147464 | tf_op jit(solution)/shard_map/ppermute | solution.py:501
  30.8 4.1 %collective-permute-start.8 = (f32[96,128]{1,0:T(8,128)S(1)}, f32[96,128]{1,0:T(8,128)S(1)}, u32[]{:S(2)}, u32[]{:S(2)}) collective-permute-start(f32[96,128]{1,0:T(8,128)S(1)} %add.74.refs_0_), channel_id=1, source_target_pairs={{0,4},{2,6},{4,0},{6,2},{8,12},{10,14},{12,8},{14,10},{1,5},{3,7},... | collective-permute-start | bytes 147464 | tf_op jit(solution)/shard_map/ppermute | solution.py:501
  31.2 4.1 %collective-permute-start.7 = (f32[96,128]{1,0:T(8,128)S(1)}, f32[96,128]{1,0:T(8,128)S(1)}, u32[]{:S(2)}, u32[]{:S(2)}) collective-permute-start(f32[96,128]{1,0:T(8,128)S(1)} %add.74.refs_0_), channel_id=1, source_target_pairs={{0,2},{2,0},{4,6},{6,4},{8,10},{10,8},{12,14},{14,12},{1,3},{3,1},... | collective-permute-start | bytes 147464 | tf_op jit(solution)/shard_map/ppermute | solution.py:501
  39.1 6.8 %collective-permute-start.12 = (bf16[64,1024]{1,0:T(8,128)(2,1)S(1)}, bf16[64,1024]{1,0:T(8,128)(2,1)S(1)}, u32[]{:S(2)}, u32[]{:S(2)}) collective-permute-start(bf16[64,1024]{1,0:T(8,128)(2,1)S(1)} %get-tuple-element.23.refs_0_), channel_id=1, source_target_pairs={{0,6},{2,4},{4,2},{6,0},{8,14},{10,12},{12,10},{14,8},{1,7},{3,5},... | collective-permute-start | bytes 393224 | tf_op jit(solution)/shard_map/ppermute | solution.py:501
  40.9 6.1 %collective-permute-start.11 = (bf16[64,1024]{1,0:T(8,128)(2,1)S(1)}, bf16[64,1024]{1,0:T(8,128)(2,1)S(1)}, u32[]{:S(2)}, u32[]{:S(2)}) collective-permute-start(bf16[64,1024]{1,0:T(8,128)(2,1)S(1)} %get-tuple-element.23.refs_0_), channel_id=1, source_target_pairs={{0,4},{2,6},{4,0},{6,2},{8,12},{10,14},{12,8},{14,10},{1,5},{3,7},... | collective-permute-start | bytes 393224 | tf_op jit(solution)/shard_map/ppermute | solution.py:501
  41.3 6.5 %collective-permute-start.10 = (bf16[64,1024]{1,0:T(8,128)(2,1)S(1)}, bf16[64,1024]{1,0:T(8,128)(2,1)S(1)}, u32[]{:S(2)}, u32[]{:S(2)}) collective-permute-start(bf16[64,1024]{1,0:T(8,128)(2,1)S(1)} %get-tuple-element.23.refs_0_), channel_id=1, source_target_pairs={{0,2},{2,0},{4,6},{6,4},{8,10},{10,8},{12,14},{14,12},{1,3},{3,1},... | collective-permute-start | bytes 393224 | tf_op jit(solution)/shard_map/ppermute | solution.py:501
  48.7 1.6 %collective-permute-start.13 = (f32[64,1024]{1,0:T(8,128)S(1)}, f32[64,1024]{1,0:T(8,128)S(1)}, u32[]{:S(2)}, u32[]{:S(2)}) collective-permute-start(f32[64,1024]{1,0:T(8,128)S(1)} %slice.30), channel_id=1, source_target_pairs={{0,1},{1,0},{2,3},{3,2},{4,5},{5,4},{6,7},{7,6},{8,9},{9,8},{10,11... | collective-permute-start | bytes 786440 | tf_op jit(solution)/shard_map/ppermute | solution.py:504
  50.7 1.2 %collective-permute-start.14 = (f32[32,128]{1,0:T(8,128)S(1)}, f32[32,128]{1,0:T(8,128)S(1)}, u32[]{:S(2)}, u32[]{:S(2)}) collective-permute-start(f32[32,128]{1,0:T(8,128)S(1)} %get-tuple-element.25), channel_id=1, source_target_pairs={{0,1},{1,0},{2,3},{3,2},{4,5},{5,4},{6,7},{7,6},{8,9},{9,8},{10,11... | collective-permute-start | bytes 49160 | tf_op jit(solution)/shard_map/ppermute | solution.py:504
  51.9 4.6 %collective-permute-start.17 = (f32[32,128]{1,0:T(8,128)S(1)}, f32[32,128]{1,0:T(8,128)S(1)}, u32[]{:S(2)}, u32[]{:S(2)}) collective-permute-start(f32[32,128]{1,0:T(8,128)S(1)} %add.75.refs_0_), channel_id=1, source_target_pairs={{0,6},{2,4},{4,2},{6,0},{8,14},{10,12},{12,10},{14,8},{1,7},{3,5},... | collective-permute-start | bytes 49160 | tf_op jit(solution)/shard_map/ppermute | solution.py:501
  54.0 3.7 %collective-permute-start.16 = (f32[32,128]{1,0:T(8,128)S(1)}, f32[32,128]{1,0:T(8,128)S(1)}, u32[]{:S(2)}, u32[]{:S(2)}) collective-permute-start(f32[32,128]{1,0:T(8,128)S(1)} %add.75.refs_0_), channel_id=1, source_target_pairs={{0,4},{2,6},{4,0},{6,2},{8,12},{10,14},{12,8},{14,10},{1,5},{3,7},... | collective-permute-start | bytes 49160 | tf_op jit(solution)/shard_map/ppermute | solution.py:501
  54.3 3.7 %collective-permute-start.15 = (f32[32,128]{1,0:T(8,128)S(1)}, f32[32,128]{1,0:T(8,128)S(1)}, u32[]{:S(2)}, u32[]{:S(2)}) collective-permute-start(f32[32,128]{1,0:T(8,128)S(1)} %add.75.refs_0_), channel_id=1, source_target_pairs={{0,2},{2,0},{4,6},{6,4},{8,10},{10,8},{12,14},{14,12},{1,3},{3,1},... | collective-permute-start | bytes 49160 | tf_op jit(solution)/shard_map/ppermute | solution.py:501
